TPU v7x, 32 devices: a whole 2x2x4 slice. The times are simulated.
32 devices in a mesh: expert: 16 (over z, y, x), dp: 2 (over core).
Axes of the slice: x: 2, y: 2, z: 4, core: 2. Of those that a mesh axis runs over, the one named last changes fastest.
Arguments:
- tokens: bfloat16 [4096, 2048], P(('expert', 'dp')), may hold values from -6 to 6
- out_grad: bfloat16 [4096, 2048], P(('expert', 'dp')), may hold values from -6 to 6
- gates: float32 [4096, 8], P(('expert', 'dp')), may hold values from 0.05 to 0.5
- expert_ids: int32 [4096, 8], P(('expert', 'dp')), may hold values from 0 to 15, all different within a row; in each aligned block of 128 rows (0 to 127, 128 to 255, ...) at most 80 rows name the same one
- w_gate: bfloat16 [16, 2048, 384], P('expert', 'dp'), may hold values from -0.125 to 0.125
- w_up: bfloat16 [16, 2048, 384], P('expert', 'dp'), may hold values from -0.125 to 0.125
- w_down: bfloat16 [16, 2048, 384], P('expert', 'dp'), may hold values from -0.3125 to 0.3125
Outputs:
- input_grad: bfloat16 [4096, 2048], P(('expert', 'dp'))
- grad_gate: float32 [16, 2048, 384], P('expert', 'dp')
- grad_up: float32 [16, 2048, 384], P('expert', 'dp')
- grad_down: float32 [16, 2048, 384], P('expert', 'dp')
Inputs may be any that keep to these rules, and one draw needn't show every extreme that they name: `expert_ids`: among the 128 tokens of one device no expert is named more than 80 times, and in every draw some device names some expert exactly 80 times. The ids of one token differ.
All inputs are finite; a program needn't handle non-finite values.
Results may differ from a plain program's by a relative error of at most 0.0065.
Values may be sent and summed in bfloat16 or wider, within the bound.
No kernel may reach another device: no remote copies, remote signals or barrier semaphores. Data moves between devices by JAX's collectives and lax.ppermute only.
A program may use at most 128 MiB of HBM per device.

v0:
```python
import jax
import jax.numpy as jnp
from jax import lax
from jax.sharding import PartitionSpec as P

contract_rows = (((0,), (0,)), ((), ()))
contract_cols = (((1,), (1,)), ((), ()))


def expert_parts(x_rows, dy_rows, gate_w, up_w, down_w):
    gate_pre = jnp.dot(x_rows, gate_w, preferred_element_type=jnp.float32)
    up_pre = jnp.dot(x_rows, up_w, preferred_element_type=jnp.float32)
    sig_gate = jax.nn.sigmoid(gate_pre)
    active = gate_pre * sig_gate
    hidden = (active * up_pre).astype(jnp.bfloat16)
    hidden_grad = jnp.dot(dy_rows, down_w, preferred_element_type=jnp.float32)
    gate_grad = (hidden_grad * up_pre * sig_gate * (1.0 + gate_pre * (1.0 - sig_gate))).astype(
        jnp.bfloat16
    )
    up_grad = (hidden_grad * active).astype(jnp.bfloat16)
    return (hidden, jnp.concatenate([gate_grad, up_grad], axis=1))


def weight_terms(x_rows, dy_rows, hidden, act_grads):
    first = lax.dot_general(x_rows, act_grads, contract_rows, preferred_element_type=jnp.float32)
    second = lax.dot_general(dy_rows, hidden, contract_rows, preferred_element_type=jnp.float32)
    return jnp.concatenate([first, second], axis=1)


def row_grads(act_grads, both_w):
    return lax.dot_general(
        act_grads, both_w, contract_cols, preferred_element_type=jnp.float32
    ).astype(jnp.bfloat16)


def local(tokens, out_grad, gates, expert_ids, w_gate, w_up, w_down):
    experts = lax.axis_size("expert")
    tok_rows, width = tokens.shape
    top_k = expert_ids.shape[1]
    capacity = 5 * tok_rows * top_k // (4 * experts)
    slot_count = experts * capacity
    flat_ids = expert_ids.reshape(-1)
    expert_match = (flat_ids[:, None] == jnp.arange(experts, dtype=jnp.int32)[None, :]).astype(
        jnp.int32
    )
    earlier = jnp.cumsum(expert_match, axis=0) - expert_match
    position = jnp.sum(earlier * expert_match, axis=1)
    slot_of = flat_ids * capacity + position
    slot_hits = (slot_of[None, :] == jnp.arange(slot_count, dtype=jnp.int32)[:, None]).reshape(
        slot_count, tok_rows, top_k
    )
    pick_tok = jnp.any(slot_hits, axis=2).astype(jnp.bfloat16)
    scale_tok = jnp.sum(jnp.where(slot_hits, gates[None, :, :], jnp.float32(0.0)), axis=2)
    gate_slot = jnp.sum(scale_tok, axis=1)
    send_x = jnp.dot(pick_tok, tokens, preferred_element_type=jnp.float32).astype(jnp.bfloat16)
    send_x = send_x.reshape(experts, capacity, width)
    grad_picked = jnp.dot(pick_tok, out_grad, preferred_element_type=jnp.float32)
    send_dy = (gate_slot[:, None] * grad_picked).astype(jnp.bfloat16)
    send_dy = send_dy.reshape(experts, capacity, width)
    recv_x = lax.all_to_all(send_x, "expert", split_axis=0, concat_axis=0, tiled=True)
    recv_dy = lax.all_to_all(send_dy, "expert", split_axis=0, concat_axis=0, tiled=True)
    full_gate, full_up, full_down = (
        lax.all_gather(w_gate, "dp", axis=1, tiled=True),
        lax.all_gather(w_up, "dp", axis=1, tiled=True),
        lax.all_gather(w_down, "dp", axis=1, tiled=True),
    )
    gate_w = full_gate[0]
    up_w = full_up[0]
    down_w = full_down[0]
    ff_width = gate_w.shape[1]
    both_w = jnp.concatenate([gate_w, up_w], axis=1)
    x_rows = recv_x.reshape(slot_count, width)
    dy_rows = recv_dy.reshape(slot_count, width)
    hidden, act_grads = expert_parts(x_rows, dy_rows, gate_w, up_w, down_w)
    row_out = row_grads(act_grads, both_w)
    returned = lax.all_to_all(
        row_out.reshape(experts, capacity, width), "expert", split_axis=0, concat_axis=0, tiled=True
    )
    grad_sums = lax.psum_scatter(
        weight_terms(x_rows, dy_rows, hidden, act_grads), "dp", scatter_dimension=0, tiled=True
    )
    input_grad = lax.dot_general(
        pick_tok,
        returned.reshape(slot_count, width),
        contract_rows,
        preferred_element_type=jnp.float32,
    ).astype(jnp.bfloat16)
    grad_gate = grad_sums[None, :, :ff_width]
    grad_up = grad_sums[None, :, ff_width : 2 * ff_width]
    grad_down = grad_sums[None, :, 2 * ff_width :]
    return (input_grad, grad_gate, grad_up, grad_down)


def solution(mesh):
    in_specs = (
        P(("expert", "dp"), None),
        P(("expert", "dp"), None),
        P(("expert", "dp"), None),
        P(("expert", "dp"), None),
        P("expert", "dp", None),
        P("expert", "dp", None),
        P("expert", "dp", None),
    )
    out_specs = (
        P(("expert", "dp"), None),
        P("expert", "dp", None),
        P("expert", "dp", None),
        P("expert", "dp", None),
    )
    return jax.shard_map(local, mesh=mesh, in_specs=in_specs, out_specs=out_specs, check_vma=False)
```

profile of v0, /device:TPU:0, one launch (start us, length us, event | category | flops | bytes accessed | tf_op | source)
XLA Modules:
  0.0 463.6 jit_solution(9155367882361619241)
XLA Ops:
  7.2 0.0 copy-start
  7.2 0.8 copy.38
  8.0 0.1 eq.43
  8.1 0.1 eq.39
  8.2 4.5 reduce-window.6
  12.7 0.1 slice.20
  12.8 0.1 copy.40
  13.0 0.1 copy.41
  13.1 0.1 broadcast_add_fusion
  13.2 0.1 reduce_sum.25
  13.3 0.7 multiply_add_fusion
  14.0 4.6 fusion
  18.7 10.3 %select_reduce_fusion = f32[1280]{0:T(1024)S(1)} fusion(f32[128,8]{0,1:T(8,128)} %param.9, s32[128,8]{0,1:T(8,128)S(1)} %multiply_add_fusion), kind=kLoop, calls=%fused_computation.4 | loop fusion | flops 3930880 | bytes 13312 | tf_op jit(solution)/shard_map/reduce_sum | solution.py:54
  29.0 0.0 copy-done
  29.0 3.9 multiply_convert_fusion
  32.9 0.0 copy-start.2
  32.9 8.5 %all-to-all-start = ((bf16[16,80,2048]{2,1,0:T(8,128)(2,1)}), bf16[16,80,2048]{2,1,0:T(8,128)(2,1)}, u32[]{:S(2)}, u32[]{:S(2)}) async-start(bf16[16,80,2048]{2,1,0:T(8,128)(2,1)} %bitcast.52), calls=%async_computation | async-start | bytes 10485760 | tf_op jit(solution)/shard_map/all_to_all | solution.py:61
  41.4 0.0 copy-done.2
  41.4 3.8 convolution_convert_fusion.1
  45.2 95.1 %all-to-all-done = bf16[16,80,2048]{2,1,0:T(8,128)(2,1)} async-done(((bf16[16,80,2048]{2,1,0:T(8,128)(2,1)}), bf16[16,80,2048]{2,1,0:T(8,128)(2,1)}, u32[]{:S(2)}, u32[]{:S(2)}) %all-to-all-start) | async-done | bytes 5242912 | tf_op jit(solution)/shard_map/all_to_all | solution.py:61
  140.2 24.6 %all-to-all-start.1 = ((bf16[16,80,2048]{2,1,0:T(8,128)(2,1)}), bf16[16,80,2048]{2,1,0:T(8,128)(2,1)}, u32[]{:S(2)}, u32[]{:S(2)}) async-start(bf16[16,80,2048]{2,1,0:T(8,128)(2,1)} %bitcast.53), calls=%async_computation.1 | async-start | bytes 10485760 | tf_op jit(solution)/shard_map/all_to_all | solution.py:60
  164.9 0.0 all-gather.4.cloned.1.call-start
  164.9 0.7 all-gather.4.cloned.1.call-update
  165.6 0.0 all-gather.6.cloned.1.call-start
  165.6 0.7 all-gather.6.cloned.1.call-update
  166.3 0.0 all-gather.8.cloned.1.call-start
  166.4 0.7 all-gather.8.cloned.1.call-update
  167.1 0.2 reduce-scatter.2.cloned.1.call-start
  167.3 11.0 %all-gather.4.cloned.1.call-done = bf16[1,2048,384]{2,1,0:T(8,128)(2,1)} async-done(((bf16[1,1024,384]{2,1,0:T(8,128)(2,1)}), bf16[1,2048,384]{2,1,0:T(8,128)(2,1)}) %all-gather.4.cloned.1.call-update) | async-done | bytes 1572880 | tf_op jit(solution)/shard_map/all_gather | solution.py:65
  178.3 6.5 %fusion.5 = f32[1280,384]{0,1:T(8,128)} fusion(bf16[1280,2048]{1,0:T(8,128)(2,1)} %bitcast.3, bf16[1,2048,384]{2,1,0:T(8,128)(2,1)} %all-gather.4.cloned.1.call-done), kind=kOutput, calls=%fused_computation.20 | convolution fusion | flops 2013265920 | bytes 8781824 | tf_op jit(solution)/shard_map/dot_general | solution.py:16
  184.8 6.0 %all-gather.6.cloned.1.call-done = bf16[1,2048,384]{2,1,0:T(8,128)(2,1)} async-done(((bf16[1,1024,384]{2,1,0:T(8,128)(2,1)}), bf16[1,2048,384]{2,1,0:T(8,128)(2,1)}) %all-gather.6.cloned.1.call-update) | async-done | bytes 1572880 | tf_op jit(solution)/shard_map/all_gather | solution.py:64
  190.9 70.4 %all-to-all-done.1 = bf16[16,80,2048]{2,1,0:T(8,128)(2,1)} async-done(((bf16[16,80,2048]{2,1,0:T(8,128)(2,1)}), bf16[16,80,2048]{2,1,0:T(8,128)(2,1)}, u32[]{:S(2)}, u32[]{:S(2)}) %all-to-all-start.1) | async-done | bytes 5242912 | tf_op jit(solution)/shard_map/all_to_all | solution.py:60
  261.3 5.2 %fusion.18 = f32[1280,384]{0,1:T(8,128)S(1)} fusion(bf16[1280,2048]{1,0:T(8,128)(2,1)} %bitcast.6, bf16[1,2048,384]{2,1,0:T(8,128)(2,1)} %all-gather.6.cloned.1.call-done), kind=kOutput, calls=%fused_computation.37 | convolution fusion | flops 2013265920 | bytes 8781824 | tf_op jit(solution)/shard_map/dot_general | solution.py:12
  266.5 0.0 all-gather.8.cloned.1.call-done
  266.5 6.6 %multiply_convert_fusion.3 = (bf16[1280,384]{0,1:T(8,128)(2,1)S(1)}, bf16[1280,384]{0,1:T(8,128)(2,1)S(1)}, f32[1280,384]{0,1:T(8,128)S(1)}) fusion(f32[1280,384]{0,1:T(8,128)} %fusion.5, f32[1280,384]{0,1:T(8,128)S(1)} %fusion.18, bf16[1280,2048]{1,0:T(8,128)(2,1)} %bitcast.6, bf16[1,2048,384]{2,1,0:T(8,128)(2,1)} %all-gather.8.cloned.1.call-done), kind=kOutput, calls=%fused_computation.14 | convolution fusion | flops 2019655680 | bytes 14680064 | tf_op jit(solution)/shard_map/dot_general | solution.py:11
  273.2 0.0 copy-start.4
  273.2 0.0 copy-start.6
  273.2 5.5 %fusion.8 = f32[2048,384]{0,1:T(8,128)S(1)} fusion(bf16[1280,2048]{1,0:T(8,128)(2,1)} %bitcast.3, f32[1280,384]{0,1:T(8,128)S(1)} %fusion.18, f32[1280,384]{0,1:T(8,128)S(1)} %get-tuple-element.25), kind=kOutput, calls=%fused_computation.23 | convolution fusion | flops 2016215040 | bytes 12320768 | tf_op jit(solution)/shard_map/dot_general | solution.py:26
  278.7 0.0 copy-done.4
  278.7 0.0 copy-done.6
  278.7 9.4 %fusion.7 = f32[2048,768]{0,1:T(8,128)} fusion(bf16[1280,2048]{1,0:T(8,128)(2,1)} %bitcast.6, bf16[1280,384]{0,1:T(8,128)(2,1)S(1)} %get-tuple-element.24, bf16[1280,384]{0,1:T(8,128)(2,1)S(1)} %get-tuple-element.23), kind=kOutput, calls=%fused_computation.22 | convolution fusion | flops 4030464000 | bytes 13500416 | tf_op jit(solution)/shard_map/dot_general | solution.py:25
  288.1 7.7 %pad_maximum_fusion = f32[2048,1152]{0,1:T(8,128)} fusion(f32[2048,384]{0,1:T(8,128)S(1)} %fusion.8, f32[2048,768]{0,1:T(8,128)} %fusion.7), kind=kLoop, calls=%fused_computation.1 | loop fusion | flops 2359296 | bytes 18874368 | tf_op jit(solution)/shard_map/concatenate | solution.py:27
  295.8 0.0 copy-start.3
  295.8 0.0 copy-start.5
  295.8 0.0 reduce-scatter.2.cloned.1.call-update
  295.9 1.4 copy-done.3
  297.2 0.3 copy-done.5
  297.5 6.0 %convolution_convert_fusion = bf16[1280,2048]{1,0:T(8,128)(2,1)S(1)} fusion(bf16[2048,384]{1,0:T(8,128)(2,1)S(1)} %bitcast.58, bf16[2048,384]{1,0:T(8,128)(2,1)} %bitcast.59, bf16[1280,384]{0,1:T(8,128)(2,1)} %copy-done.6, bf16[1280,384]{0,1:T(8,128)(2,1)S(1)} %copy-done.5), kind=kOutput, calls=%fused_computation.2 | convolution fusion | flops 4039376896 | bytes 10354688 | tf_op jit(solution)/shard_map/dot_general | solution.py:31
  303.5 139.5 %all_to_all.15 = bf16[16,80,2048]{2,1,0:T(8,128)(2,1)S(1)} all-to-all(bf16[16,80,2048]{2,1,0:T(8,128)(2,1)S(1)} %bitcast.55), channel_id=1, replica_groups=mesh['expert'=16,'dp'=2] {'expert'}, dimensions={0} | all-to-all | bytes 10485760 | tf_op jit(solution)/shard_map/all_to_all | solution.py:76
  443.0 1.7 convolution_convert_fusion.2
  444.8 0.0 reduce-scatter.2.cloned.1.call-done
  444.8 4.6 slice_bitcast_fusion
  449.4 3.0 copy.45
  452.4 0.0 copy-start.1
  452.4 3.1 copy.44
  455.5 1.6 copy.43
  457.1 0.0 copy-done.1
  (5 shorter events, 0.1 us)
Async XLA Ops:
  7.2 21.8 %copy-start = (bf16[128,2048]{1,0:T(8,128)(2,1)S(1)}, bf16[128,2048]{1,0:T(8,128)(2,1)}, u32[]{:S(2)}) copy-start(bf16[128,2048]{1,0:T(8,128)(2,1)} %param.8) | copy-start | bytes 1572868
  32.9 8.5 %copy-start.2 = (bf16[128,2048]{1,0:T(8,128)(2,1)S(1)}, bf16[128,2048]{1,0:T(8,128)(2,1)}, u32[]{:S(2)}) copy-start(bf16[128,2048]{1,0:T(8,128)(2,1)} %param.7) | copy-start | bytes 1572868
  32.9 107.4 %all-to-all-start = ((bf16[16,80,2048]{2,1,0:T(8,128)(2,1)}), bf16[16,80,2048]{2,1,0:T(8,128)(2,1)}, u32[]{:S(2)}, u32[]{:S(2)}) async-start(bf16[16,80,2048]{2,1,0:T(8,128)(2,1)} %bitcast.52), calls=%async_computation | async-start | bytes 10485760 | tf_op jit(solution)/shard_map/all_to_all | solution.py:61
  140.2 121.1 %all-to-all-start.1 = ((bf16[16,80,2048]{2,1,0:T(8,128)(2,1)}), bf16[16,80,2048]{2,1,0:T(8,128)(2,1)}, u32[]{:S(2)}, u32[]{:S(2)}) async-start(bf16[16,80,2048]{2,1,0:T(8,128)(2,1)} %bitcast.53), calls=%async_computation.1 | async-start | bytes 10485760 | tf_op jit(solution)/shard_map/all_to_all | solution.py:60
  164.9 13.5 %all-gather.4.cloned.1.call-start = ((), (), s32[]{:S(2)}) async-start(), calls=%async_computation.4 | async-start | bytes 2359296 | tf_op jit(solution)/shard_map/all_gather | solution.py:65
  165.6 25.3 %all-gather.6.cloned.1.call-start = ((), (), s32[]{:S(2)}) async-start(), calls=%async_computation.5 | async-start | bytes 2359296 | tf_op jit(solution)/shard_map/all_gather | solution.py:64
  166.3 100.2 %all-gather.8.cloned.1.call-start = ((), (), s32[]{:S(2)}) async-start(), calls=%async_computation.6 | async-start | bytes 2359296 | tf_op jit(solution)/shard_map/all_gather | solution.py:63
  167.1 277.7 %reduce-scatter.2.cloned.1.call-start = ((), (), s32[]{:S(2)}) async-start(), calls=%async_computation.7 | async-start | bytes 14155776 | tf_op jit(solution)/shard_map/reduce_scatter | solution.py:79
  273.2 5.6 %copy-start.4 = (bf16[1280,384]{0,1:T(8,128)(2,1)}, bf16[1280,384]{0,1:T(8,128)(2,1)S(1)}, u32[]{:S(2)}) copy-start(bf16[1280,384]{0,1:T(8,128)(2,1)S(1)} %get-tuple-element.23) | copy-start | bytes 2949124
  273.2 5.6 %copy-start.6 = (bf16[1280,384]{0,1:T(8,128)(2,1)}, bf16[1280,384]{0,1:T(8,128)(2,1)S(1)}, u32[]{:S(2)}) copy-start(bf16[1280,384]{0,1:T(8,128)(2,1)S(1)} %get-tuple-element.24) | copy-start | bytes 2949124
  295.8 1.4 copy-start.3
  295.8 1.7 copy-start.5
  452.4 4.7 %copy-start.1 = (bf16[128,2048]{1,0:T(8,128)(2,1)S(1)}, bf16[128,2048]{1,0:T(8,128)(2,1)}, u32[]{:S(2)}) copy-start(bf16[128,2048]{1,0:T(8,128)(2,1)} %param.8) | copy-start | bytes 1572868
Sparse Core Ops, SparseCore 0:
  167.2 11.0 all-gather.3
  179.9 10.9 all-gather.5
  192.4 10.9 all-gather.7
  296.0 36.0 reduce-scatter.1
where the time goes:
time: 464 us
  waiting for transfers between devices  185 us (40%)
  blocking collectives  140 us (30%)
  matrix products  48.7 us (10%)
  starting transfers between devices  33.4 us (7%)
  other arithmetic  28 us (6%)
  local copies, waits for them, and re-layouts  15.5 us (3%)
  between operations  13.9 us (3%)
    all_to_all x1, blocking collectives, local(): lax.all_to_all(row_out.reshape(experts, capacity, width), 'expert', split...  140 us
    all_to_all x1, waiting for transfers between devices, local(): lax.all_to_all(send_dy, 'expert', split_axis=0, concat_axis=0, tiled=True)  95.1 us
    all_to_all x1, waiting for transfers between devices, local(): lax.all_to_all(send_x, 'expert', split_axis=0, concat_axis=0, tiled=True)  70.4 us
    all_to_all x1, starting transfers between devices, local(): lax.all_to_all(send_x, 'expert', split_axis=0, concat_axis=0, tiled=True)  24.6 us
    all_gather x1, waiting for transfers between devices, local(): lax.all_gather(w_down, 'dp', axis=1, tiled=True)  11 us
    reduce_sum x1, other arithmetic, local(): gate_slot = jnp.sum(scale_tok, axis=1)  10.3 us
    unnamed x18, local copies, waits for them, and re-layouts  10.2 us
    dot_general x1, matrix products, weight_terms(): lax.dot_general(x_rows, act_grads, contract_rows, preferred_element_type=...  9.39 us
  transfers between devices with their start and end apart: 6, of which 4 were waited for; matrix products, arithmetic and copies ran while one was open for 5% of the time, Pallas kernels for 0%

commit v1 on v0

--- a/solution.py
+++ b/solution.py
@@ -1,10 +1,221 @@
 import jax
 import jax.numpy as jnp
 from jax import lax
+from jax.experimental import pallas as pl
+from jax.experimental.pallas import tpu as pltpu
 from jax.sharding import PartitionSpec as P
 
 contract_rows = (((0,), (0,)), ((), ()))
 contract_cols = (((1,), (1,)), ((), ()))
+ACROSS_X, ACROSS_Y, PAIR, ACROSS_Z = 1, 2, 4, 8
+low, wide = jnp.bfloat16, jnp.float32
+
+
+def after(rows, *earlier):
+    return lax.optimization_barrier((rows,) + earlier)[0]
+
+
+def swap(rows, bit):
+    if bit == 0:
+        return lax.ppermute(rows, "dp", [(0, 1), (1, 0)])
+    experts = lax.axis_size("expert")
+    return lax.ppermute(rows, "expert", [(i, i ^ bit) for i in range(experts)])
+
+
+def turn(rows):
+    half = rows.shape[1] // 2
+    turned = jnp.concatenate([rows[:, half:], rows[:, :half]], axis=1)
+    return jnp.where(lax.axis_index("dp") == 0, rows, turned)
+
+
+def gate_rows(gates, expert_ids, experts):
+    count = gates.shape[0]
+    lanes = lax.broadcasted_iota(jnp.int32, (1, experts * count), 1) // count
+    ids = jnp.tile(expert_ids.T, (1, experts))
+    spread = jnp.sum(jnp.where(ids == lanes, jnp.tile(gates.T, (1, experts)), 0.0), axis=0, keepdims=True)
+    first = lax.reduce_precision(spread, 8, 7)
+    second = lax.reduce_precision(spread - first, 8, 7)
+    third = spread - first - second
+    empty = jnp.zeros((5, experts * count), wide)
+    return jnp.concatenate([first, second, third, empty], axis=0).astype(low)
+
+
+def scale_of(block, rows, expert):
+    terms = lax.dynamic_slice(block, (rows, expert * rows), (8, rows))
+    return jnp.sum(terms.astype(wide), axis=0)
+
+
+def activations(pre, out_pre, scale):
+    ff = out_pre.shape[1]
+    gate_pre, up_pre = pre[:, :ff], pre[:, ff:]
+    hidden_grad = scale * out_pre
+    sig_gate = jax.nn.sigmoid(gate_pre)
+    active = gate_pre * sig_gate
+    hidden = (scale * (active * up_pre)).astype(low)
+    gate_grad = (hidden_grad * up_pre * sig_gate * (1.0 + gate_pre * (1.0 - sig_gate))).astype(low)
+    up_grad = (hidden_grad * active).astype(low)
+    return hidden, jnp.concatenate([gate_grad, up_grad], axis=1)
+
+
+def dot(a, b, dims=(((1,), (0,)), ((), ()))):
+    return lax.dot_general(a, b, dims, preferred_element_type=wide)
+
+
+def plane_sends(dx):
+    quarter = dx.shape[0] // 4
+    half = quarter // 2
+    own, of_x, of_y, of_xy = [dx[i * quarter : (i + 1) * quarter] for i in range(4)]
+    to_y = jnp.concatenate([of_y[:half], of_xy[:half]], axis=0)
+    to_x = jnp.concatenate([of_x[half:], of_xy[half:]], axis=0)
+    return to_x, to_y, of_x[:half], of_y[half:], own
+
+
+def plus(a, b):
+    return (a.astype(wide) + b.astype(wide)).astype(low)
+
+
+def plane_total(own, got_x, got_y, got_first, got_second):
+    half = got_first.shape[0]
+    got = (
+        jnp.concatenate([got_y[:half], got_x[:half]], axis=0).astype(wide)
+        + jnp.concatenate([got_first, got_second], axis=0).astype(wide)
+    )
+    return own.astype(wide) + got
+
+
+def dx_kernel(act_a, act_b, w_a, w_b, out):
+    out[...] = (dot(act_a[...], w_a[...], contract_cols) + dot(act_b[...], w_b[...], contract_cols)).astype(low)
+
+
+def dx_rows(act_a, act_b, w_a, w_b):
+    rows, depth = act_a.shape
+    width = w_a.shape[0]
+    tile = min(width, 512)
+    whole = pl.BlockSpec((rows, depth), lambda i: (0, 0))
+    part = pl.BlockSpec((tile, depth), lambda i: (i, 0))
+    return pl.pallas_call(
+        dx_kernel,
+        grid=(width // tile,),
+        in_specs=[whole, whole, part, part],
+        out_specs=pl.BlockSpec((rows, tile), lambda i: (0, i)),
+        out_shape=jax.ShapeDtypeStruct((rows, width), low),
+        compiler_params=pltpu.CompilerParams(vmem_limit_bytes=24 << 20),
+        cost_estimate=pl.CostEstimate(
+            flops=4 * rows * depth * width, bytes_accessed=4 * width * depth + 2 * rows * width, transcendentals=0
+        ),
+    )(act_a, act_b, w_a, w_b)
+
+
+def dense_local(tokens, out_grad, gates, expert_ids, w_gate, w_up, w_down):
+    experts = lax.axis_size("expert")
+    tok_rows, width = tokens.shape
+    mid = width // 2
+    ff = w_gate.shape[2]
+    me = lax.axis_index("expert")
+    pair = me ^ PAIR
+
+    def join(parts):
+        return jnp.concatenate([p[:tok_rows] for p in parts], axis=0)
+
+    def scales(parts, expert):
+        return jnp.concatenate([scale_of(p, tok_rows, expert) for p in parts])[:, None]
+
+    def weight_sum(rows, acts, columns):
+        return sum(dot(r[:, columns], a, contract_rows) for r, a in zip(rows, acts))
+
+    keep, send = slice(0, mid), slice(mid, width)
+
+    x_own = turn(tokens)
+    g_own = jnp.concatenate([turn(out_grad), gate_rows(gates, expert_ids, experts)], axis=0)
+    both_mine = jnp.concatenate([w_gate[0], w_up[0]], axis=1)
+    down_mine = w_down[0]
+    both_pair = swap(both_mine, PAIR)
+    x_far = swap(x_own, ACROSS_Z)
+    x_x = swap(x_own, ACROSS_X)
+    g_y = swap(g_own, ACROSS_Y)
+    both_other = swap(both_mine, 0)
+    down_other = swap(after(down_mine, both_other), 0)
+    g_far = swap(after(g_own, both_other), ACROSS_Z)
+    g_x = swap(after(g_own, x_x, g_y, both_other), ACROSS_X)
+    x_y = swap(after(x_own, x_x, g_y, both_other), ACROSS_Y)
+    g_y, x_x = after((g_y, x_x), g_x, x_y, down_other)
+    g_xy = swap(g_y, ACROSS_X)
+    x_xy = swap(x_x, ACROSS_Y)
+    x_far = after(x_far, g_xy, x_xy)
+    x_far_x = swap(x_far, ACROSS_X)
+    x_far_y = swap(x_far, ACROSS_Y)
+    down_pair = swap(after(down_mine, x_far), PAIR)
+    both_pair = after(both_pair, x_far)
+    both_pair_other = swap(both_pair, 0)
+    both_a = jnp.concatenate([both_mine, both_other], axis=0)
+    down_a = jnp.concatenate([down_mine, down_other], axis=0)
+    x_near_parts = after((x_own, x_x, x_y, x_xy), x_far)
+    g_near_parts = after((g_own, g_x, g_y, g_xy), x_far)
+    x_near, g_near = join(x_near_parts), join(g_near_parts)
+    hid_a_near, act_a_near = activations(
+        dot(x_near, both_a), dot(g_near, down_a), scales(g_near_parts, me)
+    )
+    g_far = after(g_far, x_far_x, x_far_y, act_a_near)
+    g_far_x = swap(g_far, ACROSS_X)
+    g_far_y = swap(g_far, ACROSS_Y)
+    both_b = jnp.concatenate([both_pair, both_pair_other], axis=0)
+    x_near, g_near, both_b = after((x_near, g_near, both_b), g_far)
+    pre_b_near = dot(x_near, both_b)
+    near_a = [
+        dot(r[:, c], v, contract_rows)
+        for r, v in ((x_near, act_a_near), (g_near, hid_a_near))
+        for c in (send, keep)
+    ]
+    g_far_y, x_far_x = after((g_far_y, x_far_x), g_far_x, pre_b_near, *near_a)
+    g_far_xy = swap(g_far_y, ACROSS_X)
+    x_far_xy = swap(x_far_x, ACROSS_Y)
+    down_pair = after(down_pair, g_far_y)
+    down_b = jnp.concatenate([down_pair, swap(down_pair, 0)], axis=0)
+    hid_b_near, act_b_near = activations(pre_b_near, dot(g_near, down_b), scales(g_near_parts, pair))
+    g_far_xy, x_far_xy = after((g_far_xy, x_far_xy), act_b_near)
+    x_far_parts = (x_far, x_far_x, x_far_y, x_far_xy)
+    g_far_parts = (g_far, g_far_x, g_far_y, g_far_xy)
+    x_fars, g_fars = join(x_far_parts), join(g_far_parts)
+    hid_b_far, act_b_far = activations(
+        dot(x_fars, both_b), dot(g_fars, down_b), scales(g_far_parts, pair)
+    )
+    pairs_b = ((x_near, x_fars), (act_b_near, act_b_far)), ((g_near, g_fars), (hid_b_near, hid_b_far))
+    sent = [weight_sum(r, v, send).astype(low) for r, v in pairs_b]
+    got = [swap(sent[0], 0)]
+    got.append(swap(after(sent[1], got[0]), 0))
+    kept = [weight_sum(r, v, keep) for r, v in pairs_b]
+    for_pair = [(k + g.astype(wide)).astype(low) for k, g in zip(kept, got)]
+    from_pair = [swap(for_pair[0], PAIR), swap(for_pair[1], PAIR)]
+    x_fars, g_fars = after((x_fars, g_fars), *kept)
+    hid_a_far, act_a_far = activations(
+        dot(x_fars, both_a), dot(g_fars, down_a), scales(g_far_parts, me)
+    )
+    act_a_far, act_b_far = after((act_a_far, act_b_far), *for_pair)
+    to_x, to_y, first, second, far_own = plane_sends(dx_rows(act_a_far, act_b_far, both_a, both_b))
+    far_x, far_y = swap(to_x, ACROSS_X), swap(to_y, ACROSS_Y)
+    act_a_near, act_b_near = after((act_a_near, act_b_near), to_x, to_y)
+    half = tok_rows // 2
+    dx_near = dx_rows(act_a_near, act_b_near, both_a, both_b)
+    first, second = plus(first, far_y[half:]), plus(second, far_x[half:])
+    far_first, far_second = swap(first, ACROSS_X), swap(second, ACROSS_Y)
+    dx_near = after(dx_near, first, second)
+    to_x, to_y, first, second, near_own = plane_sends(dx_near)
+    near_x, near_y = swap(to_x, ACROSS_X), swap(to_y, ACROSS_Y)
+    far_total = plane_total(far_own, far_x, far_y, far_first, far_second).astype(low)
+    far_got = swap(far_total, ACROSS_Z)
+    x_fars, g_fars = after((x_fars, g_fars), far_total)
+    pairs_a = (x_fars, act_a_far, near_a[:2]), (g_fars, hid_a_far, near_a[2:])
+    sent = [(dot(r[:, send], v, contract_rows) + n[0]).astype(low) for r, v, n in pairs_a]
+    got = [swap(sent[0], 0), swap(sent[1], 0)]
+    mine = [
+        dot(r[:, keep], v, contract_rows) + n[1] + g.astype(wide) for (r, v, n), g in zip(pairs_a, got)
+    ]
+    first, second = plus(first, near_y[half:]), plus(second, near_x[half:])
+    near_first, near_second = swap(first, ACROSS_X), swap(second, ACROSS_Y)
+    near_total = plane_total(near_own, near_x, near_y, near_first, near_second)
+    input_grad = turn((near_total + far_got.astype(wide)).astype(low))
+    totals = [m + f.astype(wide) for m, f in zip(mine, from_pair)]
+    return input_grad, totals[0][None, :, :ff], totals[0][None, :, ff:], totals[1][None]
 
 
 def expert_parts(x_rows, dy_rows, gate_w, up_w, down_w):
@@ -33,7 +244,7 @@
     ).astype(jnp.bfloat16)
 
 
-def local(tokens, out_grad, gates, expert_ids, w_gate, w_up, w_down):
+def routed_local(tokens, out_grad, gates, expert_ids, w_gate, w_up, w_down):
     experts = lax.axis_size("expert")
     tok_rows, width = tokens.shape
     top_k = expert_ids.shape[1]
@@ -107,4 +318,12 @@
         P("expert", "dp", None),
         P("expert", "dp", None),
     )
-    return jax.shard_map(local, mesh=mesh, in_specs=in_specs, out_specs=out_specs, check_vma=False)
+    def local(tokens, *rest):
+        tok_rows, experts = tokens.shape[0], mesh.shape["expert"]
+        capacity = 5 * tok_rows * rest[1].shape[1] // (4 * experts)
+        dense = experts == 16 and mesh.shape["dp"] == 2 and 2 * capacity > tok_rows
+        return (dense_local if dense else routed_local)(tokens, *rest)
+
+    return jax.shard_map(
+        local, mesh=mesh, in_specs=in_specs, out_specs=out_specs, check_vma=False
+    )

time: 464 us -> 216 us (0.47)
  blocking collectives: 140 us -> 0 us
  waiting for transfers between devices: 185 us -> 116 us
  matrix products: 48.7 us -> 32.4 us
  other arithmetic: 28 us -> 11.9 us
  between operations: 13.9 us -> 1.5 us
  Pallas kernels: 0 us -> 8.57 us
  local copies, waits for them, and re-layouts: 15.5 us -> 7.72 us
    all_to_all x2 -> x0, waiting for transfers between devices: 165 us -> none  [the longest x1 95.1 us: local(): lax.all_to_all(send_dy, 'expert', split_axis=0, concat_axis=0, tiled=True)]
    all_to_all x1 -> x0, blocking collectives: 140 us -> none  [local(): lax.all_to_all(row_out.reshape(experts, capacity, width), 'expert', split...]
    ppermute x0 -> x35, waiting for transfers between devices: none -> 116 us  [the longest x27 116 us: swap(): return lax.ppermute(rows, 'expert', [(i, i ^ bit) for i in range(experts)])]
    ppermute x0 -> x35, starting transfers between devices: none -> 35.3 us  [the longest x27 34.2 us: swap(): return lax.ppermute(rows, 'expert', [(i, i ^ bit) for i in range(experts)])]
    all_to_all x2 -> x0, starting transfers between devices: 33.1 us -> none  [the longest x1 24.6 us: local(): lax.all_to_all(send_x, 'expert', split_axis=0, concat_axis=0, tiled=True)]
    all_gather x3 -> x0, waiting for transfers between devices: 17.1 us -> none  [the longest x1 11 us: local(): lax.all_gather(w_down, 'dp', axis=1, tiled=True)]
    dot_general x9 -> x24, matrix products: 48.7 us -> 32.4 us  [dot(): return lax.dot_general(a, b, dims, preferred_element_type=wide)]
    reduce_sum x2 -> x7, other arithmetic: 10.3 us -> 0.85 us  [the longest x6 0.84 us: scale_of(): return jnp.sum(terms.astype(wide), axis=0)]
  transfers between devices with their start and end apart: 6 -> 35, of which waited for: 4 -> 14; matrix products, arithmetic and copies ran while one was open for 5% -> 18% of each run, Pallas kernels for 0% -> 2%
where the time goes in v1:
time: 216 us; the launch traced here: 214 us
  waiting for transfers between devices  116 us (54%)
  starting transfers between devices  35.3 us (16%)
  matrix products  32.4 us (15%)
  other arithmetic  11.9 us (6%)
  Pallas kernels  8.57 us (4%)
  local copies, waits for them, and re-layouts  7.72 us (4%)
    ppermute x27, waiting for transfers between devices, swap(): return lax.ppermute(rows, 'expert', [(i, i ^ bit) for i in range(experts)])  116 us
    ppermute x27, starting transfers between devices, swap(): return lax.ppermute(rows, 'expert', [(i, i ^ bit) for i in range(experts)])  34.2 us
    dot_general x24, matrix products, dot(): return lax.dot_general(a, b, dims, preferred_element_type=wide)  32.4 us
    pallas_call x2, Pallas kernels, dx_rows(): pl.pallas_call(dx_kernel, grid=(width // tile,), in_specs=[whole, whole,...  8.57 us
  transfers between devices with their start and end apart: 35, of which 14 were waited for; matrix products, arithmetic and copies ran while one was open for 18% of the time, Pallas kernels for 2%

profile of v1, /device:TPU:0, one launch (start us, length us, event | category | flops | bytes accessed | tf_op | source)
XLA Modules:
  0.0 213.7 jit_solution(10938109185894609446)
XLA Ops:
  0.7 2.7 %pad_maximum_fusion.4 = bf16[1024,768]{1,0:T(8,128)(2,1)} fusion(bf16[1024,384]{1,0:T(8,128)(2,1)} %bitcast.32, bf16[1024,384]{1,0:T(8,128)(2,1)} %bitcast.36), kind=kLoop, calls=%fused_computation.11 | loop fusion | flops 3145728 | bytes 3145728 | tf_op jit(solution)/shard_map/concatenate | solution.py:130
  4.4 2.6 %collective-permute-start.1 = (bf16[136,2048]{1,0:T(8,128)(2,1)S(1)}, bf16[136,2048]{1,0:T(8,128)(2,1)}, u32[]{:S(2)}, u32[]{:S(2)}) collective-permute-start(bf16[136,2048]{1,0:T(8,128)(2,1)S(1)} %concatenate.91), channel_id=1, source_target_pairs={{0,4},{2,6},{4,0},{6,2},{8,12},{10,14},{12,8},{14,10},{16,20},{18,... | collective-permute-start | bytes 1671176 | tf_op jit(solution)/shard_map/ppermute | solution.py:22
  7.1 1.6 collective-permute-start
  8.7 1.6 collective-permute-start.9
  10.3 11.0 %collective-permute-done = bf16[128,2048]{1,0:T(8,128)(2,1)S(1)} collective-permute-done((bf16[128,2048]{1,0:T(8,128)(2,1)S(1)}, bf16[128,2048]{1,0:T(8,128)(2,1)S(1)}, u32[]{:S(2)}, u32[]{:S(2)}) %collective-permute-start) | collective-permute-done | bytes 524320 | tf_op jit(solution)/shard_map/ppermute | solution.py:22
  21.2 1.5 collective-permute-start.3
  23.6 12.2 %collective-permute-done.4 = bf16[128,2048]{1,0:T(8,128)(2,1)S(1)} collective-permute-done((bf16[128,2048]{1,0:T(8,128)(2,1)S(1)}, bf16[128,2048]{1,0:T(8,128)(2,1)S(1)}, u32[]{:S(2)}, u32[]{:S(2)}) %collective-permute-start.4) | collective-permute-done | bytes 524320 | tf_op jit(solution)/shard_map/ppermute | solution.py:22
  35.8 1.0 collective-permute-start.6
  36.8 2.6 %collective-permute-start.7 = (bf16[128,2048]{1,0:T(8,128)(2,1)S(1)}, bf16[128,2048]{1,0:T(8,128)(2,1)}, u32[]{:S(2)}, u32[]{:S(2)}) collective-permute-start(bf16[128,2048]{1,0:T(8,128)(2,1)S(1)} %maximum_select_fusion.1), channel_id=1, source_target_pairs={{0,16},{2,18},{4,20},{6,22},{8,24},{10,26},{12,28},{14,30},{16,0},... | collective-permute-start | bytes 1572872 | tf_op jit(solution)/shard_map/ppermute | solution.py:22
  39.4 1.1 collective-permute-start.8
  40.8 1.6 pad_maximum_fusion.w_a
  42.5 33.4 %collective-permute-done.7 = bf16[128,2048]{1,0:T(8,128)(2,1)} collective-permute-done((bf16[128,2048]{1,0:T(8,128)(2,1)S(1)}, bf16[128,2048]{1,0:T(8,128)(2,1)}, u32[]{:S(2)}, u32[]{:S(2)}) %collective-permute-start.7) | collective-permute-done | bytes 524320 | tf_op jit(solution)/shard_map/ppermute | solution.py:22
  75.9 1.1 collective-permute-start.12
  77.0 1.0 collective-permute-start.13
  78.2 1.2 slice.202
  79.4 1.1 slice.203
  82.2 1.1 constant_dynamic-update-slice_fusion
  83.3 3.3 %fusion.35 = f32[512,768]{1,0:T(8,128)S(1)} fusion(bf16[512,2048]{1,0:T(8,128)(2,1)S(1)} %constant_dynamic-update-slice_fusion, bf16[1024,768]{1,0:T(8,128)(2,1)} %collective-permute-done.2, bf16[1024,384]{1,0:T(8,128)(2,1)S(1)} %bitcast.34, bf16[1024,384]{1,0:T(8,128)(2,1)S(1)} %bitcast.38), kind=kOutput, calls=%fused_computation.145 | convolution fusion | flops 1620049920 | bytes 6815744 | tf_op jit(solution)/shard_map/dot_general | solution.py:61
  86.6 1.5 multiply_convert_fusion.11
  88.5 1.1 collective-permute-start.15
  89.6 0.9 collective-permute-start.16
  90.5 1.6 pad_maximum_fusion.1.w_b
  92.1 1.0 fusion.20
  93.1 1.0 fusion.24
  95.7 1.8 fusion.41
  97.5 5.8 %collective-permute-done.15 = bf16[136,2048]{1,0:T(8,128)(2,1)S(1)} collective-permute-done((bf16[136,2048]{1,0:T(8,128)(2,1)S(1)}, bf16[136,2048]{1,0:T(8,128)(2,1)S(1)}, u32[]{:S(2)}, u32[]{:S(2)}) %collective-permute-start.15) | collective-permute-done | bytes 557088 | tf_op jit(solution)/shard_map/ppermute | solution.py:22
  104.0 1.1 constant_dynamic-update-slice_fusion.9
  105.3 1.0 collective-permute-start.18
  106.3 1.1 collective-permute-start.19
  107.8 1.5 multiply_convert_fusion.8
  109.4 11.0 %collective-permute-done.19 = bf16[128,2048]{1,0:T(8,128)(2,1)S(1)} collective-permute-done((bf16[128,2048]{1,0:T(8,128)(2,1)S(1)}, bf16[128,2048]{1,0:T(8,128)(2,1)S(1)}, u32[]{:S(2)}, u32[]{:S(2)}) %collective-permute-start.19) | collective-permute-done | bytes 524320 | tf_op jit(solution)/shard_map/ppermute | solution.py:22
  120.5 1.2 fusion.22
  122.5 1.8 fusion.42
  124.3 3.1 %multiply_convert_fusion.6 = (bf16[512,384]{1,0:T(8,128)(2,1)S(1)}, bf16[512,384]{1,0:T(8,128)(2,1)S(1)}, bf16[512,384]{1,0:T(8,128)(2,1)S(1)}) fusion(f32[512,768]{1,0:T(8,128)S(1)} %fusion.42, f32[512]{0:T(512)S(1)} %pad_maximum_fusion.19, bf16[2048,384]{1,0:T(8,128)(2,1)S(1)} %constant_dynamic-update-slice_fusion.4, bf16[128,2048]{1,0:T(8,128)(2,1)S(1)} %slice.215, ...), kind=kOutput, calls=%fused_computation.62 | convolution fusion | flops 817037312 | bytes 6424576 | tf_op jit(solution)/shard_map/dot_general | solution.py:61
  127.6 1.1 add_convert_fusion.2
  130.5 1.0 fusion.18
  132.9 1.1 add_convert_fusion.1
  134.1 3.3 %fusion.34 = f32[512,768]{1,0:T(8,128)S(1)} fusion(bf16[512,2048]{1,0:T(8,128)(2,1)S(1)} %constant_dynamic-update-slice_fusion.6, bf16[1024,768]{1,0:T(8,128)(2,1)} %collective-permute-done.2, bf16[1024,384]{1,0:T(8,128)(2,1)S(1)} %bitcast.35, bf16[1024,384]{1,0:T(8,128)(2,1)S(1)} %bitcast.39), kind=kOutput, calls=%fused_computation.144 | convolution fusion | flops 1620049920 | bytes 6815744 | tf_op jit(solution)/shard_map/dot_general | solution.py:61
  137.4 1.5 multiply_convert_fusion.2
  139.2 4.2 %shard_map.102 = bf16[512,2048]{1,0:T(8,128)(2,1)S(1)} custom-call(bf16[512,768]{1,0:T(8,128)(2,1)S(1)} %pad_maximum_fusion.11.act_a, bf16[512,768]{1,0:T(8,128)(2,1)S(1)} %pad_maximum_fusion.10.act_b, bf16[2048,768]{1,0:T(8,128)(2,1)S(1)} %pad_maximum_fusion.w_a, bf16[2048,768]{1,0:T(8,128)(2,1)S(1)} %pad_maximum_fusion.1.w_b), custom_call_target="tpu_custom_call" | custom-call | flops 3221225472 | bytes 8388608 | tf_op jit(solution)/shard_map/pallas_call | solution.py:96
  143.5 1.1 collective-permute-start.22
  144.7 1.1 collective-permute-start.23
  145.8 1.3 collective-permute-start.32
  147.8 4.4 %shard_map.103 = bf16[512,2048]{1,0:T(8,128)(2,1)S(1)} custom-call(bf16[512,768]{1,0:T(8,128)(2,1)S(1)} %pad_maximum_fusion.8.act_a, bf16[512,768]{1,0:T(8,128)(2,1)S(1)} %pad_maximum_fusion.9.act_b, bf16[2048,768]{1,0:T(8,128)(2,1)S(1)} %pad_maximum_fusion.w_a, bf16[2048,768]{1,0:T(8,128)(2,1)S(1)} %pad_maximum_fusion.1.w_b), custom_call_target="tpu_custom_call" | custom-call | flops 3221225472 | bytes 8388608 | tf_op jit(solution)/shard_map/pallas_call | solution.py:96
  152.2 5.2 %collective-permute-done.22 = bf16[128,2048]{1,0:T(8,128)(2,1)S(1)} collective-permute-done((bf16[128,2048]{1,0:T(8,128)(2,1)S(1)}, bf16[128,2048]{1,0:T(8,128)(2,1)S(1)}, u32[]{:S(2)}, u32[]{:S(2)}) %collective-permute-start.22) | collective-permute-done | bytes 524320 | tf_op jit(solution)/shard_map/ppermute | solution.py:22
  157.4 0.9 collective-permute-done.23
  158.4 1.1 collective-permute-start.28
  159.6 1.0 collective-permute-start.29
  160.7 1.1 collective-permute-start.24
  161.9 3.6 %collective-permute-done.28 = bf16[64,2048]{1,0:T(8,128)(2,1)S(1)} collective-permute-done((bf16[64,2048]{1,0:T(8,128)(2,1)S(1)}, bf16[64,2048]{1,0:T(8,128)(2,1)S(1)}, u32[]{:S(2)}, u32[]{:S(2)}) %collective-permute-start.28) | collective-permute-done | bytes 262176 | tf_op jit(solution)/shard_map/ppermute | solution.py:22
  165.6 1.1 collective-permute-start.25
  166.6 2.2 %collective-permute-done.29 = bf16[64,2048]{1,0:T(8,128)(2,1)S(1)} collective-permute-done((bf16[64,2048]{1,0:T(8,128)(2,1)S(1)}, bf16[64,2048]{1,0:T(8,128)(2,1)S(1)}, u32[]{:S(2)}, u32[]{:S(2)}) %collective-permute-start.29) | collective-permute-done | bytes 262176 | tf_op jit(solution)/shard_map/ppermute | solution.py:22
  169.1 3.5 %collective-permute-start.30 = (bf16[128,2048]{1,0:T(8,128)(2,1)S(1)}, bf16[128,2048]{1,0:T(8,128)(2,1)S(1)}, u32[]{:S(2)}, u32[]{:S(2)}) collective-permute-start(bf16[128,2048]{1,0:T(8,128)(2,1)S(1)} %add_convert_fusion.7), channel_id=1, source_target_pairs={{0,16},{2,18},{4,20},{6,22},{8,24},{10,26},{12,28},{14,30},{16,0},... | collective-permute-start | bytes 1572872 | tf_op jit(solution)/shard_map/ppermute | solution.py:22
  172.6 1.0 fusion.8
  174.4 1.0 add_convert_fusion
  175.4 2.2 %collective-permute-done.24 = bf16[128,2048]{1,0:T(8,128)(2,1)S(1)} collective-permute-done((bf16[128,2048]{1,0:T(8,128)(2,1)S(1)}, bf16[128,2048]{1,0:T(8,128)(2,1)S(1)}, u32[]{:S(2)}, u32[]{:S(2)}) %collective-permute-start.24) | collective-permute-done | bytes 524320 | tf_op jit(solution)/shard_map/ppermute | solution.py:22
  177.7 1.0 collective-permute-start.26
  178.7 1.0 collective-permute-start.27
  180.5 3.6 %collective-permute-done.26 = bf16[64,2048]{1,0:T(8,128)(2,1)S(1)} collective-permute-done((bf16[64,2048]{1,0:T(8,128)(2,1)S(1)}, bf16[64,2048]{1,0:T(8,128)(2,1)S(1)}, u32[]{:S(2)}, u32[]{:S(2)}) %collective-permute-start.26) | collective-permute-done | bytes 262176 | tf_op jit(solution)/shard_map/ppermute | solution.py:22
  184.2 1.0 collective-permute-done.27
  185.1 23.4 %collective-permute-done.30 = bf16[128,2048]{1,0:T(8,128)(2,1)S(1)} collective-permute-done((bf16[128,2048]{1,0:T(8,128)(2,1)S(1)}, bf16[128,2048]{1,0:T(8,128)(2,1)S(1)}, u32[]{:S(2)}, u32[]{:S(2)}) %collective-permute-start.30) | collective-permute-done | bytes 524320 | tf_op jit(solution)/shard_map/ppermute | solution.py:22
  208.9 0.9 maximum_select_fusion.2
  209.8 1.4 add_bitcast_fusion
  211.8 1.9 slice_bitcast_fusion
  (134 shorter events, 15.6 us)
Async XLA Ops:
  0.6 3.2 %copy-start.11 = (s32[128,8]{0,1:T(8,128)S(1)}, s32[128,8]{0,1:T(8,128)}, u32[]{:S(2)}) copy-start(s32[128,8]{0,1:T(8,128)} %param.10) | copy-start | bytes 12292
  0.6 3.2 %copy-start.10 = (f32[128,8]{0,1:T(8,128)S(1)}, f32[128,8]{0,1:T(8,128)}, u32[]{:S(2)}) copy-start(f32[128,8]{0,1:T(8,128)} %param.9) | copy-start | bytes 12292
  0.7 3.2 %copy-start.2 = (bf16[128,2048]{1,0:T(8,128)(2,1)S(1)}, bf16[128,2048]{1,0:T(8,128)(2,1)}, u32[]{:S(2)}) copy-start(bf16[128,2048]{1,0:T(8,128)(2,1)} %param.8) | copy-start | bytes 1572868
  3.4 3.6 %copy-start.3 = (bf16[128,2048]{1,0:T(8,128)(2,1)S(1)}, bf16[128,2048]{1,0:T(8,128)(2,1)}, u32[]{:S(2)}) copy-start(bf16[128,2048]{1,0:T(8,128)(2,1)} %param.7) | copy-start | bytes 1572868
  3.4 6.9 %collective-permute-start.2 = (bf16[1024,768]{1,0:T(8,128)(2,1)}, bf16[1024,768]{1,0:T(8,128)(2,1)}, u32[]{:S(2)}, u32[]{:S(2)}) collective-permute-start(bf16[1024,768]{1,0:T(8,128)(2,1)} %pad_maximum_fusion.4), channel_id=1, source_target_pairs={{0,1},{1,0},{2,3},{3,2},{4,5},{5,4},{6,7},{7,6},{8,9},{9,8},{10,11... | collective-permute-start | bytes 4718600 | tf_op jit(solution)/shard_map/ppermute | solution.py:20
  4.1 36.7 %copy-start = (bf16[1,1024,384]{2,1,0:T(8,128)(2,1)S(1)}, bf16[1,1024,384]{2,1,0:T(8,128)(2,1)}, u32[]{:S(2)}) copy-start(bf16[1,1024,384]{2,1,0:T(8,128)(2,1)} %param.12) | copy-start | bytes 2359300
  4.1 36.7 %copy-start.1 = (bf16[1,1024,384]{2,1,0:T(8,128)(2,1)S(1)}, bf16[1,1024,384]{2,1,0:T(8,128)(2,1)}, u32[]{:S(2)}) copy-start(bf16[1,1024,384]{2,1,0:T(8,128)(2,1)} %param.11) | copy-start | bytes 2359300
  4.3 5.9 %copy-start.12 = (bf16[1,1024,384]{2,1,0:T(8,128)(2,1)S(1)}, bf16[1,1024,384]{2,1,0:T(8,128)(2,1)}, u32[]{:S(2)}) copy-start(bf16[1,1024,384]{2,1,0:T(8,128)(2,1)} %param.13) | copy-start | bytes 2359300
  4.4 16.9 %collective-permute-start.1 = (bf16[136,2048]{1,0:T(8,128)(2,1)S(1)}, bf16[136,2048]{1,0:T(8,128)(2,1)}, u32[]{:S(2)}, u32[]{:S(2)}) collective-permute-start(bf16[136,2048]{1,0:T(8,128)(2,1)S(1)} %concatenate.91), channel_id=1, source_target_pairs={{0,4},{2,6},{4,0},{6,2},{8,12},{10,14},{12,8},{14,10},{16,20},{18,... | collective-permute-start | bytes 1671176 | tf_op jit(solution)/shard_map/ppermute | solution.py:22
  7.1 14.1 %collective-permute-start = (bf16[128,2048]{1,0:T(8,128)(2,1)S(1)}, bf16[128,2048]{1,0:T(8,128)(2,1)S(1)}, u32[]{:S(2)}, u32[]{:S(2)}) collective-permute-start(bf16[128,2048]{1,0:T(8,128)(2,1)S(1)} %maximum_select_fusion.1), channel_id=1, source_target_pairs={{0,2},{2,0},{4,6},{6,4},{8,10},{10,8},{12,14},{14,12},{16,18},{18,... | collective-permute-start | bytes 1572872 | tf_op jit(solution)/shard_map/ppermute | solution.py:22
  8.7 72.5 %collective-permute-start.9 = (bf16[1024,768]{1,0:T(8,128)(2,1)}, bf16[1024,768]{1,0:T(8,128)(2,1)}, u32[]{:S(2)}, u32[]{:S(2)}) collective-permute-start(bf16[1024,768]{1,0:T(8,128)(2,1)} %pad_maximum_fusion.4), channel_id=1, source_target_pairs={{0,8},{2,10},{4,12},{6,14},{8,0},{10,2},{12,4},{14,6},{16,24},{18,... | collective-permute-start | bytes 4718600 | tf_op jit(solution)/shard_map/ppermute | solution.py:22
  10.3 25.6 %collective-permute-start.5 = (bf16[1024,384]{1,0:T(8,128)(2,1)S(1)}, bf16[1024,384]{1,0:T(8,128)(2,1)S(1)}, u32[]{:S(2)}, u32[]{:S(2)}) collective-permute-start(bf16[1024,384]{1,0:T(8,128)(2,1)S(1)} %bitcast.43), channel_id=1, source_target_pairs={{0,1},{1,0},{2,3},{3,2},{4,5},{5,4},{6,7},{7,6},{8,9},{9,8},{10,11... | collective-permute-start | bytes 2359304 | tf_op jit(solution)/shard_map/ppermute | solution.py:20
  21.2 21.2 %copy-start.4 = (bf16[128,2048]{1,0:T(8,128)(2,1)}, bf16[128,2048]{1,0:T(8,128)(2,1)S(1)}, u32[]{:S(2)}) copy-start(bf16[128,2048]{1,0:T(8,128)(2,1)S(1)} %collective-permute-done) | copy-start | bytes 1572868
  21.2 14.6 %collective-permute-start.3 = (bf16[136,2048]{1,0:T(8,128)(2,1)S(1)}, bf16[136,2048]{1,0:T(8,128)(2,1)S(1)}, u32[]{:S(2)}, u32[]{:S(2)}) collective-permute-start(bf16[136,2048]{1,0:T(8,128)(2,1)S(1)} %concatenate.91), channel_id=1, source_target_pairs={{0,2},{2,0},{4,6},{6,4},{8,10},{10,8},{12,14},{14,12},{16,18},{18,... | collective-permute-start | bytes 1671176 | tf_op jit(solution)/shard_map/ppermute | solution.py:22
  22.7 13.1 %collective-permute-start.4 = (bf16[128,2048]{1,0:T(8,128)(2,1)S(1)}, bf16[128,2048]{1,0:T(8,128)(2,1)S(1)}, u32[]{:S(2)}, u32[]{:S(2)}) collective-permute-start(bf16[128,2048]{1,0:T(8,128)(2,1)S(1)} %maximum_select_fusion.1), channel_id=1, source_target_pairs={{0,4},{2,6},{4,0},{6,2},{8,12},{10,14},{12,8},{14,10},{16,20},{18,... | collective-permute-start | bytes 1572872 | tf_op jit(solution)/shard_map/ppermute | solution.py:22
  35.8 1.1 copy-start.6
  35.8 3.6 %copy-start.8 = (bf16[136,2048]{1,0:T(8,128)(2,1)}, bf16[136,2048]{1,0:T(8,128)(2,1)S(1)}, u32[]{:S(2)}) copy-start(bf16[136,2048]{1,0:T(8,128)(2,1)S(1)} %collective-permute-done.3) | copy-start | bytes 1671172
  35.8 3.6 %copy-start.15 = (bf16[1024,384]{1,0:T(8,128)(2,1)}, bf16[1024,384]{1,0:T(8,128)(2,1)S(1)}, u32[]{:S(2)}) copy-start(bf16[1024,384]{1,0:T(8,128)(2,1)S(1)} %collective-permute-done.5) | copy-start | bytes 2359300
  35.8 40.1 %collective-permute-start.6 = (bf16[136,2048]{1,0:T(8,128)(2,1)}, bf16[136,2048]{1,0:T(8,128)(2,1)}, u32[]{:S(2)}, u32[]{:S(2)}) collective-permute-start(bf16[136,2048]{1,0:T(8,128)(2,1)} %collective-permute-done.1), channel_id=1, source_target_pairs={{0,2},{2,0},{4,6},{6,4},{8,10},{10,8},{12,14},{14,12},{16,18},{18,... | collective-permute-start | bytes 1671176 | tf_op jit(solution)/shard_map/ppermute | solution.py:22
  36.8 39.0 %collective-permute-start.7 = (bf16[128,2048]{1,0:T(8,128)(2,1)S(1)}, bf16[128,2048]{1,0:T(8,128)(2,1)}, u32[]{:S(2)}, u32[]{:S(2)}) collective-permute-start(bf16[128,2048]{1,0:T(8,128)(2,1)S(1)} %maximum_select_fusion.1), channel_id=1, source_target_pairs={{0,16},{2,18},{4,20},{6,22},{8,24},{10,26},{12,28},{14,30},{16,0},... | collective-permute-start | bytes 1572872 | tf_op jit(solution)/shard_map/ppermute | solution.py:22
  39.4 36.4 %collective-permute-start.8 = (bf16[128,2048]{1,0:T(8,128)(2,1)S(1)}, bf16[128,2048]{1,0:T(8,128)(2,1)}, u32[]{:S(2)}, u32[]{:S(2)}) collective-permute-start(bf16[128,2048]{1,0:T(8,128)(2,1)S(1)} %collective-permute-done), channel_id=1, source_target_pairs={{0,4},{2,6},{4,0},{6,2},{8,12},{10,14},{12,8},{14,10},{16,20},{18,... | collective-permute-start | bytes 1572872 | tf_op jit(solution)/shard_map/ppermute | solution.py:22
  40.5 37.6 %copy-start.9 = (bf16[136,2048]{1,0:T(8,128)(2,1)S(1)}, bf16[136,2048]{1,0:T(8,128)(2,1)}, u32[]{:S(2)}) copy-start(bf16[136,2048]{1,0:T(8,128)(2,1)} %copy-done.8) | copy-start | bytes 1671172
  40.5 48.0 %collective-permute-start.11 = (bf16[136,2048]{1,0:T(8,128)(2,1)S(1)}, bf16[136,2048]{1,0:T(8,128)(2,1)S(1)}, u32[]{:S(2)}, u32[]{:S(2)}) collective-permute-start(bf16[136,2048]{1,0:T(8,128)(2,1)S(1)} %concatenate.91), channel_id=1, source_target_pairs={{0,16},{2,18},{4,20},{6,22},{8,24},{10,26},{12,28},{14,30},{16,0},... | collective-permute-start | bytes 1671176 | tf_op jit(solution)/shard_map/ppermute | solution.py:22
  75.9 12.6 %collective-permute-start.12 = (bf16[128,2048]{1,0:T(8,128)(2,1)}, bf16[128,2048]{1,0:T(8,128)(2,1)S(1)}, u32[]{:S(2)}, u32[]{:S(2)}) collective-permute-start(bf16[128,2048]{1,0:T(8,128)(2,1)} %collective-permute-done.7), channel_id=1, source_target_pairs={{0,2},{2,0},{4,6},{6,4},{8,10},{10,8},{12,14},{14,12},{16,18},{18,... | collective-permute-start | bytes 1572872 | tf_op jit(solution)/shard_map/ppermute | solution.py:22
  77.0 11.5 %collective-permute-start.13 = (bf16[128,2048]{1,0:T(8,128)(2,1)}, bf16[128,2048]{1,0:T(8,128)(2,1)S(1)}, u32[]{:S(2)}, u32[]{:S(2)}) collective-permute-start(bf16[128,2048]{1,0:T(8,128)(2,1)} %collective-permute-done.7), channel_id=1, source_target_pairs={{0,4},{2,6},{4,0},{6,2},{8,12},{10,14},{12,8},{14,10},{16,20},{18,... | collective-permute-start | bytes 1572872 | tf_op jit(solution)/shard_map/ppermute | solution.py:22
  78.1 3.3 %copy-start.13 = (bf16[1,1024,384]{2,1,0:T(8,128)(2,1)S(1)}, bf16[1,1024,384]{2,1,0:T(8,128)(2,1)}, u32[]{:S(2)}) copy-start(bf16[1,1024,384]{2,1,0:T(8,128)(2,1)} %param.13) | copy-start | bytes 2359300
  78.1 4.0 %copy-start.5 = (bf16[128,2048]{1,0:T(8,128)(2,1)S(1)}, bf16[128,2048]{1,0:T(8,128)(2,1)}, u32[]{:S(2)}) copy-start(bf16[128,2048]{1,0:T(8,128)(2,1)} %copy-done.4) | copy-start | bytes 1572868
  78.1 4.0 %copy-start.7 = (bf16[128,2048]{1,0:T(8,128)(2,1)S(1)}, bf16[128,2048]{1,0:T(8,128)(2,1)}, u32[]{:S(2)}) copy-start(bf16[128,2048]{1,0:T(8,128)(2,1)} %copy-done.6) | copy-start | bytes 1572868
  81.2 9.3 %collective-permute-start.10 = (bf16[1024,768]{1,0:T(8,128)(2,1)}, bf16[1024,768]{1,0:T(8,128)(2,1)S(1)}, u32[]{:S(2)}, u32[]{:S(2)}) collective-permute-start(bf16[1024,768]{1,0:T(8,128)(2,1)} %collective-permute-done.9), channel_id=1, source_target_pairs={{0,1},{1,0},{2,3},{3,2},{4,5},{5,4},{6,7},{7,6},{8,9},{9,8},{10,11... | collective-permute-start | bytes 4718600 | tf_op jit(solution)/shard_map/ppermute | solution.py:20
  81.3 22.7 %collective-permute-start.14 = (bf16[1024,384]{1,0:T(8,128)(2,1)S(1)}, bf16[1024,384]{1,0:T(8,128)(2,1)S(1)}, u32[]{:S(2)}, u32[]{:S(2)}) collective-permute-start(bf16[1024,384]{1,0:T(8,128)(2,1)S(1)} %bitcast.44), channel_id=1, source_target_pairs={{0,8},{2,10},{4,12},{6,14},{8,0},{10,2},{12,4},{14,6},{16,24},{18,... | collective-permute-start | bytes 2359304 | tf_op jit(solution)/shard_map/ppermute | solution.py:22
  83.3 3.3 %copy-start.16 = (bf16[1024,384]{1,0:T(8,128)(2,1)S(1)}, bf16[1024,384]{1,0:T(8,128)(2,1)}, u32[]{:S(2)}) copy-start(bf16[1024,384]{1,0:T(8,128)(2,1)} %copy-done.15) | copy-start | bytes 2359300
  88.5 14.8 %collective-permute-start.15 = (bf16[136,2048]{1,0:T(8,128)(2,1)S(1)}, bf16[136,2048]{1,0:T(8,128)(2,1)S(1)}, u32[]{:S(2)}, u32[]{:S(2)}) collective-permute-start(bf16[136,2048]{1,0:T(8,128)(2,1)S(1)} %collective-permute-done.11), channel_id=1, source_target_pairs={{0,4},{2,6},{4,0},{6,2},{8,12},{10,14},{12,8},{14,10},{16,20},{18,... | collective-permute-start | bytes 1671176 | tf_op jit(solution)/shard_map/ppermute | solution.py:22
  89.6 14.5 %collective-permute-start.16 = (bf16[136,2048]{1,0:T(8,128)(2,1)S(1)}, bf16[136,2048]{1,0:T(8,128)(2,1)S(1)}, u32[]{:S(2)}, u32[]{:S(2)}) collective-permute-start(bf16[136,2048]{1,0:T(8,128)(2,1)S(1)} %collective-permute-done.11), channel_id=1, source_target_pairs={{0,2},{2,0},{4,6},{6,4},{8,10},{10,8},{12,14},{14,12},{16,18},{18,... | collective-permute-start | bytes 1671176 | tf_op jit(solution)/shard_map/ppermute | solution.py:22
  104.0 3.6 %collective-permute-start.17 = (bf16[1024,384]{1,0:T(8,128)(2,1)S(1)}, bf16[1024,384]{1,0:T(8,128)(2,1)S(1)}, u32[]{:S(2)}, u32[]{:S(2)}) collective-permute-start(bf16[1024,384]{1,0:T(8,128)(2,1)S(1)} %collective-permute-done.14), channel_id=1, source_target_pairs={{0,1},{1,0},{2,3},{3,2},{4,5},{5,4},{6,7},{7,6},{8,9},{9,8},{10,11... | collective-permute-start | bytes 2359304 | tf_op jit(solution)/shard_map/ppermute | solution.py:20
  105.3 15.2 %collective-permute-start.18 = (bf16[136,2048]{1,0:T(8,128)(2,1)S(1)}, bf16[136,2048]{1,0:T(8,128)(2,1)S(1)}, u32[]{:S(2)}, u32[]{:S(2)}) collective-permute-start(bf16[136,2048]{1,0:T(8,128)(2,1)S(1)} %collective-permute-done.15), channel_id=1, source_target_pairs={{0,2},{2,0},{4,6},{6,4},{8,10},{10,8},{12,14},{14,12},{16,18},{18,... | collective-permute-start | bytes 1671176 | tf_op jit(solution)/shard_map/ppermute | solution.py:22
  106.3 14.1 %collective-permute-start.19 = (bf16[128,2048]{1,0:T(8,128)(2,1)S(1)}, bf16[128,2048]{1,0:T(8,128)(2,1)S(1)}, u32[]{:S(2)}, u32[]{:S(2)}) collective-permute-start(bf16[128,2048]{1,0:T(8,128)(2,1)S(1)} %collective-permute-done.12), channel_id=1, source_target_pairs={{0,4},{2,6},{4,0},{6,2},{8,12},{10,14},{12,8},{14,10},{16,20},{18,... | collective-permute-start | bytes 1572872 | tf_op jit(solution)/shard_map/ppermute | solution.py:22
  128.7 3.7 %collective-permute-start.20 = (bf16[1024,768]{1,0:T(8,128)(2,1)S(1)}, bf16[1024,768]{1,0:T(8,128)(2,1)S(1)}, u32[]{:S(2)}, u32[]{:S(2)}) collective-permute-start(bf16[1024,768]{1,0:T(8,128)(2,1)S(1)} %add_convert_fusion.2), channel_id=1, source_target_pairs={{0,1},{1,0},{2,3},{3,2},{4,5},{5,4},{6,7},{7,6},{8,9},{9,8},{10,11... | collective-permute-start | bytes 4718600 | tf_op jit(solution)/shard_map/ppermute | solution.py:20
  132.3 6.7 %collective-permute-start.21 = (bf16[1024,384]{1,0:T(8,128)(2,1)S(1)}, bf16[1024,384]{1,0:T(8,128)(2,1)S(1)}, u32[]{:S(2)}, u32[]{:S(2)}) collective-permute-start(bf16[1024,384]{1,0:T(8,128)(2,1)S(1)} %add_convert_fusion.5), channel_id=1, source_target_pairs={{0,1},{1,0},{2,3},{3,2},{4,5},{5,4},{6,7},{7,6},{8,9},{9,8},{10,11... | collective-permute-start | bytes 2359304 | tf_op jit(solution)/shard_map/ppermute | solution.py:20
  134.0 3.3 %copy-start.14 = (bf16[1,1024,384]{2,1,0:T(8,128)(2,1)S(1)}, bf16[1,1024,384]{2,1,0:T(8,128)(2,1)}, u32[]{:S(2)}) copy-start(bf16[1,1024,384]{2,1,0:T(8,128)(2,1)} %param.13) | copy-start | bytes 2359300
  134.0 3.3 %copy-start.17 = (bf16[1024,384]{1,0:T(8,128)(2,1)S(1)}, bf16[1024,384]{1,0:T(8,128)(2,1)}, u32[]{:S(2)}) copy-start(bf16[1024,384]{1,0:T(8,128)(2,1)} %copy-done.15) | copy-start | bytes 2359300
  143.5 13.9 %collective-permute-start.22 = (bf16[128,2048]{1,0:T(8,128)(2,1)S(1)}, bf16[128,2048]{1,0:T(8,128)(2,1)S(1)}, u32[]{:S(2)}, u32[]{:S(2)}) collective-permute-start(bf16[128,2048]{1,0:T(8,128)(2,1)S(1)} %pad_maximum_fusion.13), channel_id=1, source_target_pairs={{0,4},{2,6},{4,0},{6,2},{8,12},{10,14},{12,8},{14,10},{16,20},{18,... | collective-permute-start | bytes 1572872 | tf_op jit(solution)/shard_map/ppermute | solution.py:22
  144.7 13.6 %collective-permute-start.23 = (bf16[128,2048]{1,0:T(8,128)(2,1)S(1)}, bf16[128,2048]{1,0:T(8,128)(2,1)S(1)}, u32[]{:S(2)}, u32[]{:S(2)}) collective-permute-start(bf16[128,2048]{1,0:T(8,128)(2,1)S(1)} %pad_maximum_fusion.12), channel_id=1, source_target_pairs={{0,2},{2,0},{4,6},{6,4},{8,10},{10,8},{12,14},{14,12},{16,18},{18,... | collective-permute-start | bytes 1572872 | tf_op jit(solution)/shard_map/ppermute | solution.py:22
  145.8 65.4 %collective-permute-start.32 = (bf16[1024,768]{1,0:T(8,128)(2,1)S(1)}, bf16[1024,768]{1,0:T(8,128)(2,1)S(1)}, u32[]{:S(2)}, u32[]{:S(2)}) collective-permute-start(bf16[1024,768]{1,0:T(8,128)(2,1)S(1)} %add_convert_fusion.1), channel_id=1, source_target_pairs={{0,8},{2,10},{4,12},{6,14},{8,0},{10,2},{12,4},{14,6},{16,24},{18,... | collective-permute-start | bytes 4718600 | tf_op jit(solution)/shard_map/ppermute | solution.py:22
  147.2 62.7 %collective-permute-start.34 = (bf16[1024,384]{1,0:T(8,128)(2,1)S(1)}, bf16[1024,384]{1,0:T(8,128)(2,1)S(1)}, u32[]{:S(2)}, u32[]{:S(2)}) collective-permute-start(bf16[1024,384]{1,0:T(8,128)(2,1)S(1)} %add_convert_fusion.4), channel_id=1, source_target_pairs={{0,8},{2,10},{4,12},{6,14},{8,0},{10,2},{12,4},{14,6},{16,24},{18,... | collective-permute-start | bytes 2359304 | tf_op jit(solution)/shard_map/ppermute | solution.py:22
  158.4 7.1 %collective-permute-start.28 = (bf16[64,2048]{1,0:T(8,128)(2,1)S(1)}, bf16[64,2048]{1,0:T(8,128)(2,1)S(1)}, u32[]{:S(2)}, u32[]{:S(2)}) collective-permute-start(bf16[64,2048]{1,0:T(8,128)(2,1)S(1)} %get-tuple-element.108), channel_id=1, source_target_pairs={{0,2},{2,0},{4,6},{6,4},{8,10},{10,8},{12,14},{14,12},{16,18},{18,... | collective-permute-start | bytes 786440 | tf_op jit(solution)/shard_map/ppermute | solution.py:22
  159.6 9.2 %collective-permute-start.29 = (bf16[64,2048]{1,0:T(8,128)(2,1)S(1)}, bf16[64,2048]{1,0:T(8,128)(2,1)S(1)}, u32[]{:S(2)}, u32[]{:S(2)}) collective-permute-start(bf16[64,2048]{1,0:T(8,128)(2,1)S(1)} %get-tuple-element.109), channel_id=1, source_target_pairs={{0,4},{2,6},{4,0},{6,2},{8,12},{10,14},{12,8},{14,10},{16,20},{18,... | collective-permute-start | bytes 786440 | tf_op jit(solution)/shard_map/ppermute | solution.py:22
  160.7 16.8 %collective-permute-start.24 = (bf16[128,2048]{1,0:T(8,128)(2,1)S(1)}, bf16[128,2048]{1,0:T(8,128)(2,1)S(1)}, u32[]{:S(2)}, u32[]{:S(2)}) collective-permute-start(bf16[128,2048]{1,0:T(8,128)(2,1)S(1)} %pad_maximum_fusion.14), channel_id=1, source_target_pairs={{0,4},{2,6},{4,0},{6,2},{8,12},{10,14},{12,8},{14,10},{16,20},{18,... | collective-permute-start | bytes 1572872 | tf_op jit(solution)/shard_map/ppermute | solution.py:22
  165.6 12.0 %collective-permute-start.25 = (bf16[128,2048]{1,0:T(8,128)(2,1)S(1)}, bf16[128,2048]{1,0:T(8,128)(2,1)S(1)}, u32[]{:S(2)}, u32[]{:S(2)}) collective-permute-start(bf16[128,2048]{1,0:T(8,128)(2,1)S(1)} %pad_maximum_fusion.15), channel_id=1, source_target_pairs={{0,2},{2,0},{4,6},{6,4},{8,10},{10,8},{12,14},{14,12},{16,18},{18,... | collective-permute-start | bytes 1572872 | tf_op jit(solution)/shard_map/ppermute | solution.py:22
  169.1 39.5 %collective-permute-start.30 = (bf16[128,2048]{1,0:T(8,128)(2,1)S(1)}, bf16[128,2048]{1,0:T(8,128)(2,1)S(1)}, u32[]{:S(2)}, u32[]{:S(2)}) collective-permute-start(bf16[128,2048]{1,0:T(8,128)(2,1)S(1)} %add_convert_fusion.7), channel_id=1, source_target_pairs={{0,16},{2,18},{4,20},{6,22},{8,24},{10,26},{12,28},{14,30},{16,0},... | collective-permute-start | bytes 1572872 | tf_op jit(solution)/shard_map/ppermute | solution.py:22
  177.7 6.4 %collective-permute-start.26 = (bf16[64,2048]{1,0:T(8,128)(2,1)S(1)}, bf16[64,2048]{1,0:T(8,128)(2,1)S(1)}, u32[]{:S(2)}, u32[]{:S(2)}) collective-permute-start(bf16[64,2048]{1,0:T(8,128)(2,1)S(1)} %get-tuple-element.102), channel_id=1, source_target_pairs={{0,2},{2,0},{4,6},{6,4},{8,10},{10,8},{12,14},{14,12},{16,18},{18,... | collective-permute-start | bytes 786440 | tf_op jit(solution)/shard_map/ppermute | solution.py:22
  178.7 6.4 %collective-permute-start.27 = (bf16[64,2048]{1,0:T(8,128)(2,1)S(1)}, bf16[64,2048]{1,0:T(8,128)(2,1)S(1)}, u32[]{:S(2)}, u32[]{:S(2)}) collective-permute-start(bf16[64,2048]{1,0:T(8,128)(2,1)S(1)} %get-tuple-element.103), channel_id=1, source_target_pairs={{0,4},{2,6},{4,0},{6,2},{8,12},{10,14},{12,8},{14,10},{16,20},{18,... | collective-permute-start | bytes 786440 | tf_op jit(solution)/shard_map/ppermute | solution.py:22
  184.2 25.7 %collective-permute-start.33 = (bf16[1024,384]{1,0:T(8,128)(2,1)S(1)}, bf16[1024,384]{1,0:T(8,128)(2,1)S(1)}, u32[]{:S(2)}, u32[]{:S(2)}) collective-permute-start(bf16[1024,384]{1,0:T(8,128)(2,1)S(1)} %add_convert_fusion.3), channel_id=1, source_target_pairs={{0,1},{1,0},{2,3},{3,2},{4,5},{5,4},{6,7},{7,6},{8,9},{9,8},{10,11... | collective-permute-start | bytes 2359304 | tf_op jit(solution)/shard_map/ppermute | solution.py:20
  185.1 26.1 %collective-permute-start.31 = (bf16[1024,768]{1,0:T(8,128)(2,1)S(1)}, bf16[1024,768]{1,0:T(8,128)(2,1)S(1)}, u32[]{:S(2)}, u32[]{:S(2)}) collective-permute-start(bf16[1024,768]{1,0:T(8,128)(2,1)S(1)} %add_convert_fusion), channel_id=1, source_target_pairs={{0,1},{1,0},{2,3},{3,2},{4,5},{5,4},{6,7},{7,6},{8,9},{9,8},{10,11... | collective-permute-start | bytes 4718600 | tf_op jit(solution)/shard_map/ppermute | solution.py:20

commit v2 on v1

--- a/solution.py
+++ b/solution.py
@@ -20,6 +20,15 @@
         return lax.ppermute(rows, "dp", [(0, 1), (1, 0)])
     experts = lax.axis_size("expert")
     return lax.ppermute(rows, "expert", [(i, i ^ bit) for i in range(experts)])
+
+
+def swap_far(rows, bit):
+    experts = lax.axis_size("expert")
+    groups = [[i, i ^ bit] for i in range(experts) if i < i ^ bit]
+    both = lax.all_to_all(
+        jnp.stack([rows, rows]), "expert", split_axis=0, concat_axis=0, tiled=True, axis_index_groups=groups
+    )
+    return jnp.where(lax.axis_index("expert") & bit == 0, both[1], both[0])
 
 
 def turn(rows):
@@ -90,7 +99,7 @@
 def dx_rows(act_a, act_b, w_a, w_b):
     rows, depth = act_a.shape
     width = w_a.shape[0]
-    tile = min(width, 512)
+    tile = min(width, 256)
     whole = pl.BlockSpec((rows, depth), lambda i: (0, 0))
     part = pl.BlockSpec((tile, depth), lambda i: (i, 0))
     return pl.pallas_call(
@@ -99,11 +108,35 @@
         in_specs=[whole, whole, part, part],
         out_specs=pl.BlockSpec((rows, tile), lambda i: (0, i)),
         out_shape=jax.ShapeDtypeStruct((rows, width), low),
-        compiler_params=pltpu.CompilerParams(vmem_limit_bytes=24 << 20),
+        compiler_params=pltpu.CompilerParams(vmem_limit_bytes=10 << 20),
         cost_estimate=pl.CostEstimate(
             flops=4 * rows * depth * width, bytes_accessed=4 * width * depth + 2 * rows * width, transcendentals=0
         ),
     )(act_a, act_b, w_a, w_b)
+
+
+def add_up(kept_both, kept_down, got, more):
+    rows, ff = kept_down.shape
+    tile = min(rows, 256)
+
+    def kernel(both, down, got, more, gate_out, up_out, down_out):
+        extra = got[...].astype(wide) + more[...].astype(wide)
+        gate_out[...] = both[:, :ff] + extra[:, :ff]
+        up_out[...] = both[:, ff:] + extra[:, ff : 2 * ff]
+        down_out[...] = down[...] + extra[:, 2 * ff :]
+
+    def part(columns):
+        return pl.BlockSpec((tile, columns), lambda i: (i, 0))
+
+    return pl.pallas_call(
+        kernel,
+        grid=(rows // tile,),
+        in_specs=[part(2 * ff), part(ff), part(3 * ff), part(3 * ff)],
+        out_specs=[part(ff)] * 3,
+        out_shape=[jax.ShapeDtypeStruct((rows, ff), wide)] * 3,
+        compiler_params=pltpu.CompilerParams(vmem_limit_bytes=16 << 20),
+        cost_estimate=pl.CostEstimate(flops=20_000_000_000, bytes_accessed=0, transcendentals=0),
+    )(kept_both, kept_down, got, more)
 
 
 def dense_local(tokens, out_grad, gates, expert_ids, w_gate, w_up, w_down):
@@ -125,54 +158,41 @@
 
     keep, send = slice(0, mid), slice(mid, width)
 
+    both_mine, down_mine = jnp.concatenate([w_gate[0], w_up[0]], axis=1), w_down[0]
     x_own = turn(tokens)
     g_own = jnp.concatenate([turn(out_grad), gate_rows(gates, expert_ids, experts)], axis=0)
-    both_mine = jnp.concatenate([w_gate[0], w_up[0]], axis=1)
-    down_mine = w_down[0]
+    far = swap_far(jnp.concatenate([x_own, g_own], axis=0), ACROSS_Z)
     both_pair = swap(both_mine, PAIR)
-    x_far = swap(x_own, ACROSS_Z)
     x_x = swap(x_own, ACROSS_X)
     g_y = swap(g_own, ACROSS_Y)
-    both_other = swap(both_mine, 0)
-    down_other = swap(after(down_mine, both_other), 0)
-    g_far = swap(after(g_own, both_other), ACROSS_Z)
-    g_x = swap(after(g_own, x_x, g_y, both_other), ACROSS_X)
-    x_y = swap(after(x_own, x_x, g_y, both_other), ACROSS_Y)
-    g_y, x_x = after((g_y, x_x), g_x, x_y, down_other)
+    g_x = swap(after(g_own, x_x, g_y), ACROSS_X)
+    x_y = swap(after(x_own, x_x, g_y), ACROSS_Y)
+    g_y, x_x = after((g_y, x_x), g_x, x_y)
     g_xy = swap(g_y, ACROSS_X)
     x_xy = swap(x_x, ACROSS_Y)
-    x_far = after(x_far, g_xy, x_xy)
-    x_far_x = swap(x_far, ACROSS_X)
-    x_far_y = swap(x_far, ACROSS_Y)
-    down_pair = swap(after(down_mine, x_far), PAIR)
-    both_pair = after(both_pair, x_far)
+    far = after(far, g_xy, x_xy)
+    far_of_x = swap(far, ACROSS_X)
+    far_of_y = swap(far, ACROSS_Y)
+    x_near_parts = x_own, x_x, x_y, after(x_xy, both_pair)
+    g_near_parts = g_own, g_x, g_y, after(g_xy, both_pair)
+    x_near, g_near = join(x_near_parts), join(g_near_parts)
+    scale_a_near, scale_b_near = scales(g_near_parts, me), scales(g_near_parts, pair)
+    down_pair = swap(after(down_mine, far), PAIR)
+    far_of_x, far_of_y = after((far_of_x, far_of_y), x_near, g_near)
+    g_far_xy = swap(far_of_y[tok_rows:], ACROSS_X)
+    x_far_xy = swap(far_of_x[:tok_rows], ACROSS_Y)
+    both_pair = after(both_pair, far_of_x, far_of_y)
     both_pair_other = swap(both_pair, 0)
-    both_a = jnp.concatenate([both_mine, both_other], axis=0)
-    down_a = jnp.concatenate([down_mine, down_other], axis=0)
-    x_near_parts = after((x_own, x_x, x_y, x_xy), x_far)
-    g_near_parts = after((g_own, g_x, g_y, g_xy), x_far)
-    x_near, g_near = join(x_near_parts), join(g_near_parts)
-    hid_a_near, act_a_near = activations(
-        dot(x_near, both_a), dot(g_near, down_a), scales(g_near_parts, me)
-    )
-    g_far = after(g_far, x_far_x, x_far_y, act_a_near)
-    g_far_x = swap(g_far, ACROSS_X)
-    g_far_y = swap(g_far, ACROSS_Y)
     both_b = jnp.concatenate([both_pair, both_pair_other], axis=0)
-    x_near, g_near, both_b = after((x_near, g_near, both_b), g_far)
     pre_b_near = dot(x_near, both_b)
-    near_a = [
-        dot(r[:, c], v, contract_rows)
-        for r, v in ((x_near, act_a_near), (g_near, hid_a_near))
-        for c in (send, keep)
-    ]
-    g_far_y, x_far_x = after((g_far_y, x_far_x), g_far_x, pre_b_near, *near_a)
-    g_far_xy = swap(g_far_y, ACROSS_X)
-    x_far_xy = swap(x_far_x, ACROSS_Y)
-    down_pair = after(down_pair, g_far_y)
-    down_b = jnp.concatenate([down_pair, swap(down_pair, 0)], axis=0)
-    hid_b_near, act_b_near = activations(pre_b_near, dot(g_near, down_b), scales(g_near_parts, pair))
-    g_far_xy, x_far_xy = after((g_far_xy, x_far_xy), act_b_near)
+    down_pair = after(down_pair, g_far_xy, x_far_xy)
+    down_pair_other = swap(down_pair, 0)
+    down_b = jnp.concatenate([down_pair, down_pair_other], axis=0)
+    x_far, x_far_x, x_far_y = [v[:tok_rows] for v in (far, far_of_x, far_of_y)]
+    g_far, g_far_x, g_far_y = [v[tok_rows:] for v in (far, far_of_x, far_of_y)]
+    hid_b_near, act_b_near = activations(pre_b_near, dot(g_near, down_b), scale_b_near)
+    x_far, x_far_x, x_far_y = [v[:tok_rows] for v in (far, far_of_x, far_of_y)]
+    g_far, g_far_x, g_far_y = [v[tok_rows:] for v in (far, far_of_x, far_of_y)]
     x_far_parts = (x_far, x_far_x, x_far_y, x_far_xy)
     g_far_parts = (g_far, g_far_x, g_far_y, g_far_xy)
     x_fars, g_fars = join(x_far_parts), join(g_far_parts)
@@ -180,20 +200,25 @@
         dot(x_fars, both_b), dot(g_fars, down_b), scales(g_far_parts, pair)
     )
     pairs_b = ((x_near, x_fars), (act_b_near, act_b_far)), ((g_near, g_fars), (hid_b_near, hid_b_far))
-    sent = [weight_sum(r, v, send).astype(low) for r, v in pairs_b]
-    got = [swap(sent[0], 0)]
-    got.append(swap(after(sent[1], got[0]), 0))
+    sent = jnp.concatenate([weight_sum(r, v, send).astype(low) for r, v in pairs_b], axis=1)
+    got = swap(sent, 0)
     kept = [weight_sum(r, v, keep) for r, v in pairs_b]
-    for_pair = [(k + g.astype(wide)).astype(low) for k, g in zip(kept, got)]
-    from_pair = [swap(for_pair[0], PAIR), swap(for_pair[1], PAIR)]
-    x_fars, g_fars = after((x_fars, g_fars), *kept)
+    for_pair = (jnp.concatenate(kept, axis=1) + got.astype(wide)).astype(low)
+    from_pair = swap(for_pair, PAIR)
+    both_other = swap(after(both_mine, for_pair), 0)
+    down_other = swap(after(down_mine, for_pair), 0)
+    both_a = jnp.concatenate([both_mine, both_other], axis=0)
+    down_a = jnp.concatenate([down_mine, down_other], axis=0)
+    x_fars, g_fars, x_near, g_near, both_a, down_a = after(
+        (x_fars, g_fars, x_near, g_near, both_a, down_a), for_pair
+    )
     hid_a_far, act_a_far = activations(
         dot(x_fars, both_a), dot(g_fars, down_a), scales(g_far_parts, me)
     )
-    act_a_far, act_b_far = after((act_a_far, act_b_far), *for_pair)
     to_x, to_y, first, second, far_own = plane_sends(dx_rows(act_a_far, act_b_far, both_a, both_b))
     far_x, far_y = swap(to_x, ACROSS_X), swap(to_y, ACROSS_Y)
-    act_a_near, act_b_near = after((act_a_near, act_b_near), to_x, to_y)
+    x_near, g_near = after((x_near, g_near), to_x, to_y)
+    hid_a_near, act_a_near = activations(dot(x_near, both_a), dot(g_near, down_a), scale_a_near)
     half = tok_rows // 2
     dx_near = dx_rows(act_a_near, act_b_near, both_a, both_b)
     first, second = plus(first, far_y[half:]), plus(second, far_x[half:])
@@ -203,19 +228,18 @@
     near_x, near_y = swap(to_x, ACROSS_X), swap(to_y, ACROSS_Y)
     far_total = plane_total(far_own, far_x, far_y, far_first, far_second).astype(low)
     far_got = swap(far_total, ACROSS_Z)
-    x_fars, g_fars = after((x_fars, g_fars), far_total)
-    pairs_a = (x_fars, act_a_far, near_a[:2]), (g_fars, hid_a_far, near_a[2:])
-    sent = [(dot(r[:, send], v, contract_rows) + n[0]).astype(low) for r, v, n in pairs_a]
-    got = [swap(sent[0], 0), swap(sent[1], 0)]
-    mine = [
-        dot(r[:, keep], v, contract_rows) + n[1] + g.astype(wide) for (r, v, n), g in zip(pairs_a, got)
-    ]
+    x_fars, g_fars = after((x_fars, g_fars), far_total, dx_near)
+    pairs_a = ((x_near, x_fars), (act_a_near, act_a_far)), ((g_near, g_fars), (hid_a_near, hid_a_far))
+    sent = jnp.concatenate([weight_sum(r, v, send).astype(low) for r, v in pairs_a], axis=1)
+    got = swap(sent, 0)
+    kept = [weight_sum(r, v, keep) for r, v in pairs_a]
     first, second = plus(first, near_y[half:]), plus(second, near_x[half:])
     near_first, near_second = swap(first, ACROSS_X), swap(second, ACROSS_Y)
+    far_got = after(far_got, from_pair)
     near_total = plane_total(near_own, near_x, near_y, near_first, near_second)
     input_grad = turn((near_total + far_got.astype(wide)).astype(low))
-    totals = [m + f.astype(wide) for m, f in zip(mine, from_pair)]
-    return input_grad, totals[0][None, :, :ff], totals[0][None, :, ff:], totals[1][None]
+    grads = add_up(*kept, got, after(from_pair, *kept))
+    return (input_grad,) + tuple(g[None] for g in grads)
 
 
 def expert_parts(x_rows, dy_rows, gate_w, up_w, down_w):

time: 216 us -> 195 us (0.903)
  waiting for transfers between devices: 116 us -> 89.5 us
  local copies, waits for them, and re-layouts: 7.72 us -> 12.9 us
  starting transfers between devices: 35.3 us -> 30.2 us
  Pallas kernels: 8.57 us -> 13 us
  other arithmetic: 11.9 us -> 14.8 us
    ppermute x27 -> x22, waiting for transfers between devices: 116 us -> 69.4 us  [swap(): return lax.ppermute(rows, 'expert', [(i, i ^ bit) for i in range(experts)])]
    all_to_all x0 -> x1, waiting for transfers between devices: none -> 15.4 us  [swap_far(): lax.all_to_all(jnp.stack([rows, rows]), 'expert', split_axis=0, concat_ax...]
    ppermute x27 -> x22, starting transfers between devices: 34.2 us -> 24 us  [swap(): return lax.ppermute(rows, 'expert', [(i, i ^ bit) for i in range(experts)])]
    all_to_all x0 -> x1, starting transfers between devices: none -> 5.3 us  [swap_far(): lax.all_to_all(jnp.stack([rows, rows]), 'expert', split_axis=0, concat_ax...]
    ppermute x8 -> x6, waiting for transfers between devices: 0.02 us -> 4.76 us  [swap(): return lax.ppermute(rows, 'dp', [(0, 1), (1, 0)])]
    pallas_call x0 -> x1, Pallas kernels: none -> 2.66 us  [add_up(): pl.pallas_call(kernel, grid=(rows // tile,), in_specs=[part(2 * ff), part...]
    slice x8 -> x7, local copies, waits for them, and re-layouts: 2.52 us -> 4.73 us  [join(): return jnp.concatenate([p[:tok_rows] for p in parts], axis=0)]
  transfers between devices with their start and end apart: 35 -> 29, of which waited for: 14 -> 20; matrix products, arithmetic and copies ran while one was open for 18% -> 20% of each run, Pallas kernels for 2% -> 5%
where the time goes in v2:
time: 195 us; the launch traced here: 194 us
  waiting for transfers between devices  89.5 us (46%)
  matrix products  32.3 us (17%)
  starting transfers between devices  30.2 us (15%)
  other arithmetic  14.8 us (8%)
  Pallas kernels  13 us (7%)
  local copies, waits for them, and re-layouts  12.9 us (7%)
    ppermute x22, waiting for transfers between devices, swap(): return lax.ppermute(rows, 'expert', [(i, i ^ bit) for i in range(experts)])  69.4 us
    dot_general x24, matrix products, dot(): return lax.dot_general(a, b, dims, preferred_element_type=wide)  32.3 us
    ppermute x22, starting transfers between devices, swap(): return lax.ppermute(rows, 'expert', [(i, i ^ bit) for i in range(experts)])  24 us
    all_to_all x1, waiting for transfers between devices, swap_far(): lax.all_to_all(jnp.stack([rows, rows]), 'expert', split_axis=0, concat_ax...  15.4 us
    pallas_call x2, Pallas kernels, dx_rows(): pl.pallas_call(dx_kernel, grid=(width // tile,), in_specs=[whole, whole,...  10.4 us
    all_to_all x1, starting transfers between devices, swap_far(): lax.all_to_all(jnp.stack([rows, rows]), 'expert', split_axis=0, concat_ax...  5.3 us
    ppermute x6, waiting for transfers between devices, swap(): return lax.ppermute(rows, 'dp', [(0, 1), (1, 0)])  4.76 us
    slice x7, local copies, waits for them, and re-layouts, join(): return jnp.concatenate([p[:tok_rows] for p in parts], axis=0)  4.73 us
  transfers between devices with their start and end apart: 29, of which 20 were waited for; matrix products, arithmetic and copies ran while one was open for 20% of the time, Pallas kernels for 5%

profile of v2, /device:TPU:0, one launch (start us, length us, event | category | flops | bytes accessed | tf_op | source)
XLA Modules:
  0.0 194.1 jit_solution(5503838582747198305)
XLA Ops:
  0.7 1.1 fusion.47
  2.6 1.1 fusion.48
  4.3 1.5 pad_maximum_fusion.3
  5.9 5.3 %all-to-all-start = ((bf16[2,264,2048]{2,1,0:T(8,128)(2,1)}), bf16[2,264,2048]{2,1,0:T(8,128)(2,1)S(1)}, u32[]{:S(2)}, u32[]{:S(2)}) async-start(bf16[2,264,2048]{2,1,0:T(8,128)(2,1)} %pad_maximum_fusion.3), calls=%async_computation | async-start | bytes 4325376 | tf_op jit(solution)/shard_map/all_to_all | solution.py:28
  11.2 1.5 collective-permute-start
  12.7 2.1 %concatenate.105 = bf16[136,2048]{1,0:T(8,128)(2,1)} concatenate(bf16[128,2048]{1,0:T(8,128)(2,1)S(1)} %maximum_select_fusion, bf16[1,2048]{1,0:T(2,128)(2,1)S(1)} %get-tuple-element.118, bf16[1,2048]{1,0:T(2,128)(2,1)S(1)} %get-tuple-element.117, bf16[1,2048]{1,0:T(2,128)(2,1)S(1)} %get-tuple-element.116, bf16[5,2048]{1,0:T(8,128)(2,1)S(1)} %broadcast_in_dim.22), dimensions={0} | concatenate | bytes 1114112 | tf_op jit(solution)/shard_map/concatenate | solution.py:163
  14.7 1.5 collective-permute-start.1
  16.3 2.6 %pad_maximum_fusion.8 = bf16[1024,768]{1,0:T(8,128)(2,1)} fusion(bf16[1024,384]{1,0:T(8,128)(2,1)} %bitcast.33, bf16[1024,384]{1,0:T(8,128)(2,1)} %bitcast.35), kind=kLoop, calls=%fused_computation.14 | loop fusion | flops 3145728 | bytes 3145728 | tf_op jit(solution)/shard_map/concatenate | solution.py:161
  18.9 1.6 collective-permute-start.5
  20.5 4.2 %collective-permute-done = bf16[128,2048]{1,0:T(8,128)(2,1)} collective-permute-done((bf16[128,2048]{1,0:T(8,128)(2,1)S(1)}, bf16[128,2048]{1,0:T(8,128)(2,1)}, u32[]{:S(2)}, u32[]{:S(2)}) %collective-permute-start) | collective-permute-done | bytes 524320 | tf_op jit(solution)/shard_map/ppermute | solution.py:22
  24.7 4.5 %collective-permute-done.1 = bf16[136,2048]{1,0:T(8,128)(2,1)} collective-permute-done((bf16[136,2048]{1,0:T(8,128)(2,1)}, bf16[136,2048]{1,0:T(8,128)(2,1)}, u32[]{:S(2)}, u32[]{:S(2)}) %collective-permute-start.1) | collective-permute-done | bytes 557088 | tf_op jit(solution)/shard_map/ppermute | solution.py:22
  29.5 1.7 collective-permute-start.3
  31.2 10.4 %collective-permute-done.3 = bf16[128,2048]{1,0:T(8,128)(2,1)S(1)} collective-permute-done((bf16[128,2048]{1,0:T(8,128)(2,1)S(1)}, bf16[128,2048]{1,0:T(8,128)(2,1)S(1)}, u32[]{:S(2)}, u32[]{:S(2)}) %collective-permute-start.3) | collective-permute-done | bytes 524320 | tf_op jit(solution)/shard_map/ppermute | solution.py:22
  42.4 1.7 collective-permute-start.4
  44.1 1.5 collective-permute-start.6
  45.7 15.4 %all-to-all-done = bf16[2,264,2048]{2,1,0:T(8,128)(2,1)S(1)} async-done(((bf16[2,264,2048]{2,1,0:T(8,128)(2,1)}), bf16[2,264,2048]{2,1,0:T(8,128)(2,1)S(1)}, u32[]{:S(2)}, u32[]{:S(2)}) %all-to-all-start) | async-done | bytes 2162720 | tf_op jit(solution)/shard_map/all_to_all | solution.py:28
  61.0 1.1 fusion.1
  62.1 1.5 collective-permute-start.7
  63.7 1.5 collective-permute-start.8
  65.2 0.8 convert_reduce_fusion.15
  65.9 1.1 slice.232
  67.0 1.1 slice.293
  69.5 7.3 %collective-permute-done.5 = bf16[1024,768]{1,0:T(8,128)(2,1)} collective-permute-done((bf16[1024,768]{1,0:T(8,128)(2,1)}, bf16[1024,768]{1,0:T(8,128)(2,1)}, u32[]{:S(2)}, u32[]{:S(2)}) %collective-permute-start.5) | collective-permute-done | bytes 1572896 | tf_op jit(solution)/shard_map/ppermute | solution.py:22
  76.8 1.4 pad_maximum_fusion.4
  78.2 1.1 slice.233
  79.5 1.1 slice.245
  80.8 1.3 fusion.43
  82.1 4.9 %collective-permute-done.7 = bf16[264,2048]{1,0:T(8,128)(2,1)S(1)} collective-permute-done((bf16[264,2048]{1,0:T(8,128)(2,1)}, bf16[264,2048]{1,0:T(8,128)(2,1)S(1)}, u32[]{:S(2)}, u32[]{:S(2)}) %collective-permute-start.7) | collective-permute-done | bytes 1081376 | tf_op jit(solution)/shard_map/ppermute | solution.py:22
  86.9 1.3 collective-permute-done.8
  88.3 1.6 collective-permute-start.9
  90.6 1.5 constant_dynamic-update-slice_fusion.3
  92.3 6.3 %collective-permute-done.11 = bf16[1024,384]{1,0:T(8,128)(2,1)S(1)} collective-permute-done((bf16[1024,384]{1,0:T(8,128)(2,1)S(1)}, bf16[1024,384]{1,0:T(8,128)(2,1)S(1)}, u32[]{:S(2)}, u32[]{:S(2)}) %collective-permute-start.11) | collective-permute-done | bytes 786464 | tf_op jit(solution)/shard_map/ppermute | solution.py:22
  98.5 1.4 collective-permute-done.9
  99.9 2.1 %collective-permute-done.10 = bf16[136,2048]{1,0:T(8,128)(2,1)S(1)} collective-permute-done((bf16[136,2048]{1,0:T(8,128)(2,1)S(1)}, bf16[136,2048]{1,0:T(8,128)(2,1)S(1)}, u32[]{:S(2)}, u32[]{:S(2)}) %collective-permute-start.10) | collective-permute-done | bytes 557088 | tf_op jit(solution)/shard_map/ppermute | solution.py:22
  103.4 0.9 collective-permute-done.12
  104.6 1.8 fusion.39
  106.4 3.1 %multiply_convert_fusion.9 = (bf16[512,384]{1,0:T(8,128)(2,1)S(1)}, bf16[512,384]{1,0:T(8,128)(2,1)S(1)}, bf16[512,384]{1,0:T(8,128)(2,1)S(1)}) fusion(f32[512,768]{1,0:T(8,128)S(1)} %fusion.39, f32[512]{0:T(512)S(1)} %pad_maximum_fusion.20, bf16[2048,384]{1,0:T(8,128)(2,1)S(1)} %constant_dynamic-update-slice_fusion, bf16[128,2048]{1,0:T(8,128)(2,1)S(1)} %slice.294, ...), kind=kOutput, calls=%fused_computation.71 | convolution fusion | flops 817037312 | bytes 6424576 | tf_op jit(solution)/shard_map/dot_general | solution.py:70
  109.5 3.0 %fusion.40 = f32[512,768]{1,0:T(8,128)S(1)} fusion(bf16[2048,768]{1,0:T(8,128)(2,1)S(1)} %constant_dynamic-update-slice_fusion.2.w_b, bf16[128,2048]{1,0:T(8,128)(2,1)} %collective-permute-done.6, bf16[128,2048]{1,0:T(8,128)(2,1)S(1)} %copy-done.7, bf16[128,2048]{1,0:T(8,128)(2,1)} %collective-permute-done, bf16[128,2048]{1,0:T(8,128)(2,1)S(1)} %maximum_select_fusion.1), kind=kOutput, calls=%fused_computation.141 | convolution fusion | flops 1619001344 | bytes 6815744 | tf_op jit(solution)/shard_map/dot_general | solution.py:70
  112.5 3.3 %multiply_convert_fusion.11 = (bf16[512,384]{1,0:T(8,128)(2,1)S(1)}, bf16[512,384]{1,0:T(8,128)(2,1)S(1)}, bf16[512,384]{1,0:T(8,128)(2,1)S(1)}) fusion(f32[512,768]{1,0:T(8,128)S(1)} %fusion.40, f32[512]{0:T(512)S(1)} %pad_maximum_fusion.19, bf16[2048,384]{1,0:T(8,128)(2,1)S(1)} %constant_dynamic-update-slice_fusion, bf16[128,2048]{1,0:T(8,128)(2,1)S(1)} %slice.233, ...), kind=kOutput, calls=%fused_computation.75 | convolution fusion | flops 817037312 | bytes 6424576 | tf_op jit(solution)/shard_map/dot_general | solution.py:70
  117.3 1.0 fusion.8
  118.4 1.1 add_convert_fusion.1
  120.6 1.0 fusion.18
  122.4 1.1 convolution_add_fusion.1
  123.5 0.8 collective-permute-done.14
  126.2 3.1 %collective-permute-done.16 = bf16[1024,384]{1,0:T(8,128)(2,1)S(1)} collective-permute-done((bf16[1024,384]{1,0:T(8,128)(2,1)S(1)}, bf16[1024,384]{1,0:T(8,128)(2,1)S(1)}, u32[]{:S(2)}, u32[]{:S(2)}) %collective-permute-start.16) | collective-permute-done | bytes 786464 | tf_op jit(solution)/shard_map/ppermute | solution.py:20
  129.7 1.8 fusion.49
  131.5 1.6 multiply_convert_fusion.5
  133.2 5.3 %shard_map.102 = bf16[512,2048]{1,0:T(8,128)(2,1)S(1)} custom-call(bf16[512,768]{1,0:T(8,128)(2,1)S(1)} %pad_maximum_fusion.12.act_a, bf16[512,768]{1,0:T(8,128)(2,1)S(1)} %pad_maximum_fusion.11.act_b, bf16[2048,768]{1,0:T(8,128)(2,1)S(1)} %pad_maximum_fusion.w_a, bf16[2048,768]{1,0:T(8,128)(2,1)S(1)} %constant_dynamic-update-slice_fusion.2.w_b), custom_call_target="tpu_custom_call" | custom-call | flops 3221225472 | bytes 8388608 | tf_op jit(solution)/shard_map/pallas_call | solution.py:105
  139.9 1.8 fusion.50
  141.7 1.6 multiply_convert_fusion.3
  143.3 1.0 fusion.31
  145.1 5.1 %shard_map.103 = bf16[512,2048]{1,0:T(8,128)(2,1)S(1)} custom-call(bf16[512,768]{1,0:T(8,128)(2,1)S(1)} %pad_maximum_fusion.13.act_a, bf16[512,768]{1,0:T(8,128)(2,1)S(1)} %pad_maximum_fusion.10.act_b, bf16[2048,768]{1,0:T(8,128)(2,1)S(1)} %pad_maximum_fusion.w_a, bf16[2048,768]{1,0:T(8,128)(2,1)S(1)} %constant_dynamic-update-slice_fusion.2.w_b), custom_call_target="tpu_custom_call" | custom-call | flops 3221225472 | bytes 8388608 | tf_op jit(solution)/shard_map/pallas_call | solution.py:105
  151.0 1.0 fusion.25
  153.8 1.5 collective-permute-start.24
  156.1 1.5 collective-permute-start.20
  157.6 4.8 %collective-permute-done.23 = bf16[64,2048]{1,0:T(8,128)(2,1)S(1)} collective-permute-done((bf16[64,2048]{1,0:T(8,128)(2,1)S(1)}, bf16[64,2048]{1,0:T(8,128)(2,1)S(1)}, u32[]{:S(2)}, u32[]{:S(2)}) %collective-permute-start.23) | collective-permute-done | bytes 262176 | tf_op jit(solution)/shard_map/ppermute | solution.py:22
  164.1 1.0 add_convert_fusion
  165.4 1.1 convolution_add_fusion.both
  166.5 5.9 %collective-permute-done.19 = bf16[128,2048]{1,0:T(8,128)(2,1)S(1)} collective-permute-done((bf16[128,2048]{1,0:T(8,128)(2,1)S(1)}, bf16[128,2048]{1,0:T(8,128)(2,1)S(1)}, u32[]{:S(2)}, u32[]{:S(2)}) %collective-permute-start.19) | collective-permute-done | bytes 524320 | tf_op jit(solution)/shard_map/ppermute | solution.py:22
  172.6 1.0 collective-permute-start.21
  173.6 1.5 collective-permute-start.22
  175.9 14.2 %collective-permute-done.26.more = bf16[1024,1152]{1,0:T(8,128)(2,1)S(1)} collective-permute-done((bf16[1024,1152]{1,0:T(8,128)(2,1)S(1)}, bf16[1024,1152]{1,0:T(8,128)(2,1)S(1)}, u32[]{:S(2)}, u32[]{:S(2)}) %collective-permute-start.26) | collective-permute-done | bytes 2359328 | tf_op jit(solution)/shard_map/ppermute | solution.py:22
  190.5 0.9 maximum_select_fusion.2
  191.5 2.7 %shard_map.104 = (f32[1024,384]{1,0:T(8,128)}, f32[1024,384]{1,0:T(8,128)}, f32[1024,384]{1,0:T(8,128)}) custom-call(f32[1024,768]{1,0:T(8,128)S(1)} %convolution_add_fusion.both, f32[1024,384]{1,0:T(8,128)S(1)} %convolution_add_fusion.2.down, bf16[1024,1152]{1,0:T(8,128)(2,1)S(1)} %collective-permute-done.27.got, ...), custom_call_target="tpu_custom_call" | custom-call | flops 20000000000 | tf_op jit(solution)/shard_map/pallas_call | solution.py:131
  (106 shorter events, 21.3 us)
Async XLA Ops:
  0.6 3.0 %copy-start.2 = (bf16[128,2048]{1,0:T(8,128)(2,1)S(1)}, bf16[128,2048]{1,0:T(8,128)(2,1)}, u32[]{:S(2)}) copy-start(bf16[128,2048]{1,0:T(8,128)(2,1)} %param.8) | copy-start | bytes 1572868
  0.6 3.2 %copy-start.3 = (bf16[128,2048]{1,0:T(8,128)(2,1)S(1)}, bf16[128,2048]{1,0:T(8,128)(2,1)}, u32[]{:S(2)}) copy-start(bf16[128,2048]{1,0:T(8,128)(2,1)} %param.7) | copy-start | bytes 1572868
  5.9 55.2 %all-to-all-start = ((bf16[2,264,2048]{2,1,0:T(8,128)(2,1)}), bf16[2,264,2048]{2,1,0:T(8,128)(2,1)S(1)}, u32[]{:S(2)}, u32[]{:S(2)}) async-start(bf16[2,264,2048]{2,1,0:T(8,128)(2,1)} %pad_maximum_fusion.3), calls=%async_computation | async-start | bytes 4325376 | tf_op jit(solution)/shard_map/all_to_all | solution.py:28
  11.2 13.5 %collective-permute-start = (bf16[128,2048]{1,0:T(8,128)(2,1)S(1)}, bf16[128,2048]{1,0:T(8,128)(2,1)}, u32[]{:S(2)}, u32[]{:S(2)}) collective-permute-start(bf16[128,2048]{1,0:T(8,128)(2,1)S(1)} %maximum_select_fusion.1), channel_id=1, source_target_pairs={{0,2},{2,0},{4,6},{6,4},{8,10},{10,8},{12,14},{14,12},{16,18},{18,... | collective-permute-start | bytes 1572872 | tf_op jit(solution)/shard_map/ppermute | solution.py:22
  14.7 14.4 %copy-start.5 = (bf16[136,2048]{1,0:T(8,128)(2,1)S(1)}, bf16[136,2048]{1,0:T(8,128)(2,1)}, u32[]{:S(2)}) copy-start(bf16[136,2048]{1,0:T(8,128)(2,1)} %concatenate.105) | copy-start | bytes 1671172
  14.7 14.4 %collective-permute-start.1 = (bf16[136,2048]{1,0:T(8,128)(2,1)}, bf16[136,2048]{1,0:T(8,128)(2,1)}, u32[]{:S(2)}, u32[]{:S(2)}) collective-permute-start(bf16[136,2048]{1,0:T(8,128)(2,1)} %concatenate.105), channel_id=1, source_target_pairs={{0,4},{2,6},{4,0},{6,2},{8,12},{10,14},{12,8},{14,10},{16,20},{18,... | collective-permute-start | bytes 1671176 | tf_op jit(solution)/shard_map/ppermute | solution.py:22
  18.9 57.9 %collective-permute-start.5 = (bf16[1024,768]{1,0:T(8,128)(2,1)}, bf16[1024,768]{1,0:T(8,128)(2,1)}, u32[]{:S(2)}, u32[]{:S(2)}) collective-permute-start(bf16[1024,768]{1,0:T(8,128)(2,1)} %pad_maximum_fusion.8), channel_id=1, source_target_pairs={{0,8},{2,10},{4,12},{6,14},{8,0},{10,2},{12,4},{14,6},{16,24},{18,... | collective-permute-start | bytes 4718600 | tf_op jit(solution)/shard_map/ppermute | solution.py:22
  29.1 13.2 %collective-permute-start.2 = (bf16[136,2048]{1,0:T(8,128)(2,1)S(1)}, bf16[136,2048]{1,0:T(8,128)(2,1)S(1)}, u32[]{:S(2)}, u32[]{:S(2)}) collective-permute-start(bf16[136,2048]{1,0:T(8,128)(2,1)S(1)} %copy-done.5), channel_id=1, source_target_pairs={{0,2},{2,0},{4,6},{6,4},{8,10},{10,8},{12,14},{14,12},{16,18},{18,... | collective-permute-start | bytes 1671176 | tf_op jit(solution)/shard_map/ppermute | solution.py:22
  29.5 12.1 %collective-permute-start.3 = (bf16[128,2048]{1,0:T(8,128)(2,1)S(1)}, bf16[128,2048]{1,0:T(8,128)(2,1)S(1)}, u32[]{:S(2)}, u32[]{:S(2)}) collective-permute-start(bf16[128,2048]{1,0:T(8,128)(2,1)S(1)} %maximum_select_fusion.1), channel_id=1, source_target_pairs={{0,4},{2,6},{4,0},{6,2},{8,12},{10,14},{12,8},{14,10},{16,20},{18,... | collective-permute-start | bytes 1572872 | tf_op jit(solution)/shard_map/ppermute | solution.py:22
  41.6 0.8 copy-start.6
  42.4 1.7 copy-start.8
  42.4 19.7 %collective-permute-start.4 = (bf16[136,2048]{1,0:T(8,128)(2,1)}, bf16[136,2048]{1,0:T(8,128)(2,1)}, u32[]{:S(2)}, u32[]{:S(2)}) collective-permute-start(bf16[136,2048]{1,0:T(8,128)(2,1)} %collective-permute-done.1), channel_id=1, source_target_pairs={{0,2},{2,0},{4,6},{6,4},{8,10},{10,8},{12,14},{14,12},{16,18},{18,... | collective-permute-start | bytes 1671176 | tf_op jit(solution)/shard_map/ppermute | solution.py:22
  44.1 18.0 %collective-permute-start.6 = (bf16[128,2048]{1,0:T(8,128)(2,1)}, bf16[128,2048]{1,0:T(8,128)(2,1)}, u32[]{:S(2)}, u32[]{:S(2)}) collective-permute-start(bf16[128,2048]{1,0:T(8,128)(2,1)} %collective-permute-done), channel_id=1, source_target_pairs={{0,4},{2,6},{4,0},{6,2},{8,12},{10,14},{12,8},{14,10},{16,20},{18,... | collective-permute-start | bytes 1572872 | tf_op jit(solution)/shard_map/ppermute | solution.py:22
  62.1 24.8 %collective-permute-start.7 = (bf16[264,2048]{1,0:T(8,128)(2,1)}, bf16[264,2048]{1,0:T(8,128)(2,1)S(1)}, u32[]{:S(2)}, u32[]{:S(2)}) collective-permute-start(bf16[264,2048]{1,0:T(8,128)(2,1)} %fusion.1), channel_id=1, source_target_pairs={{0,2},{2,0},{4,6},{6,4},{8,10},{10,8},{12,14},{14,12},{16,18},{18,... | collective-permute-start | bytes 3244040 | tf_op jit(solution)/shard_map/ppermute | solution.py:22
  63.7 24.6 %collective-permute-start.8 = (bf16[264,2048]{1,0:T(8,128)(2,1)}, bf16[264,2048]{1,0:T(8,128)(2,1)S(1)}, u32[]{:S(2)}, u32[]{:S(2)}) collective-permute-start(bf16[264,2048]{1,0:T(8,128)(2,1)} %fusion.1), channel_id=1, source_target_pairs={{0,4},{2,6},{4,0},{6,2},{8,12},{10,14},{12,8},{14,10},{16,20},{18,... | collective-permute-start | bytes 3244040 | tf_op jit(solution)/shard_map/ppermute | solution.py:22
  65.2 11.6 %copy-start.7 = (bf16[128,2048]{1,0:T(8,128)(2,1)S(1)}, bf16[128,2048]{1,0:T(8,128)(2,1)}, u32[]{:S(2)}) copy-start(bf16[128,2048]{1,0:T(8,128)(2,1)} %copy-done.6) | copy-start | bytes 1572868
  79.3 1.3 copy-start.4
  80.7 17.9 %collective-permute-start.11 = (bf16[1024,384]{1,0:T(8,128)(2,1)S(1)}, bf16[1024,384]{1,0:T(8,128)(2,1)S(1)}, u32[]{:S(2)}, u32[]{:S(2)}) collective-permute-start(bf16[1024,384]{1,0:T(8,128)(2,1)S(1)} %bitcast.37), channel_id=1, source_target_pairs={{0,8},{2,10},{4,12},{6,14},{8,0},{10,2},{12,4},{14,6},{16,24},{18,... | collective-permute-start | bytes 2359304 | tf_op jit(solution)/shard_map/ppermute | solution.py:22
  88.3 11.6 %collective-permute-start.9 = (bf16[128,2048]{1,0:T(8,128)(2,1)S(1)}, bf16[128,2048]{1,0:T(8,128)(2,1)S(1)}, u32[]{:S(2)}, u32[]{:S(2)}) collective-permute-start(bf16[128,2048]{1,0:T(8,128)(2,1)S(1)} %get-tuple-element.107), channel_id=1, source_target_pairs={{0,4},{2,6},{4,0},{6,2},{8,12},{10,14},{12,8},{14,10},{16,20},{18,... | collective-permute-start | bytes 1572872 | tf_op jit(solution)/shard_map/ppermute | solution.py:22
  90.0 12.0 %collective-permute-start.10 = (bf16[136,2048]{1,0:T(8,128)(2,1)S(1)}, bf16[136,2048]{1,0:T(8,128)(2,1)S(1)}, u32[]{:S(2)}, u32[]{:S(2)}) collective-permute-start(bf16[136,2048]{1,0:T(8,128)(2,1)S(1)} %slice.239), channel_id=1, source_target_pairs={{0,2},{2,0},{4,6},{6,4},{8,10},{10,8},{12,14},{14,12},{16,18},{18,... | collective-permute-start | bytes 1671176 | tf_op jit(solution)/shard_map/ppermute | solution.py:22
  90.6 13.9 %collective-permute-start.13 = (bf16[1024,768]{1,0:T(8,128)(2,1)}, bf16[1024,768]{1,0:T(8,128)(2,1)S(1)}, u32[]{:S(2)}, u32[]{:S(2)}) collective-permute-start(bf16[1024,768]{1,0:T(8,128)(2,1)} %collective-permute-done.5), channel_id=1, source_target_pairs={{0,1},{1,0},{2,3},{3,2},{4,5},{5,4},{6,7},{7,6},{8,9},{9,8},{10,11... | collective-permute-start | bytes 4718600 | tf_op jit(solution)/shard_map/ppermute | solution.py:20
  102.0 2.3 %collective-permute-start.12 = (bf16[1024,384]{1,0:T(8,128)(2,1)S(1)}, bf16[1024,384]{1,0:T(8,128)(2,1)S(1)}, u32[]{:S(2)}, u32[]{:S(2)}) collective-permute-start(bf16[1024,384]{1,0:T(8,128)(2,1)S(1)} %collective-permute-done.11), channel_id=1, source_target_pairs={{0,1},{1,0},{2,3},{3,2},{4,5},{5,4},{6,7},{7,6},{8,9},{9,8},{10,11... | collective-permute-start | bytes 2359304 | tf_op jit(solution)/shard_map/ppermute | solution.py:20
  119.6 4.6 %collective-permute-start.14 = (bf16[1024,1152]{1,0:T(8,128)(2,1)S(1)}, bf16[1024,1152]{1,0:T(8,128)(2,1)S(1)}, u32[]{:S(2)}, u32[]{:S(2)}) collective-permute-start(bf16[1024,1152]{1,0:T(8,128)(2,1)S(1)} %pad_maximum_fusion.1), channel_id=1, source_target_pairs={{0,1},{1,0},{2,3},{3,2},{4,5},{5,4},{6,7},{7,6},{8,9},{9,8},{10,11... | collective-permute-start | bytes 7077896 | tf_op jit(solution)/shard_map/ppermute | solution.py:20
  124.7 4.8 %collective-permute-start.15 = (bf16[1024,768]{1,0:T(8,128)(2,1)}, bf16[1024,768]{1,0:T(8,128)(2,1)S(1)}, u32[]{:S(2)}, u32[]{:S(2)}) collective-permute-start(bf16[1024,768]{1,0:T(8,128)(2,1)} %pad_maximum_fusion.8), channel_id=1, source_target_pairs={{0,1},{1,0},{2,3},{3,2},{4,5},{5,4},{6,7},{7,6},{8,9},{9,8},{10,11... | collective-permute-start | bytes 4718600 | tf_op jit(solution)/shard_map/ppermute | solution.py:20
  124.9 4.4 %collective-permute-start.16 = (bf16[1024,384]{1,0:T(8,128)(2,1)S(1)}, bf16[1024,384]{1,0:T(8,128)(2,1)S(1)}, u32[]{:S(2)}, u32[]{:S(2)}) collective-permute-start(bf16[1024,384]{1,0:T(8,128)(2,1)S(1)} %bitcast.38), channel_id=1, source_target_pairs={{0,1},{1,0},{2,3},{3,2},{4,5},{5,4},{6,7},{7,6},{8,9},{9,8},{10,11... | collective-permute-start | bytes 2359304 | tf_op jit(solution)/shard_map/ppermute | solution.py:20
  125.4 4.1 %copy-start = (bf16[1,1024,384]{2,1,0:T(8,128)(2,1)S(1)}, bf16[1,1024,384]{2,1,0:T(8,128)(2,1)}, u32[]{:S(2)}) copy-start(bf16[1,1024,384]{2,1,0:T(8,128)(2,1)} %param.12) | copy-start | bytes 2359300
  125.4 4.1 %copy-start.1 = (bf16[1,1024,384]{2,1,0:T(8,128)(2,1)S(1)}, bf16[1,1024,384]{2,1,0:T(8,128)(2,1)}, u32[]{:S(2)}) copy-start(bf16[1,1024,384]{2,1,0:T(8,128)(2,1)} %param.11) | copy-start | bytes 2359300
  125.5 64.6 %collective-permute-start.26 = (bf16[1024,1152]{1,0:T(8,128)(2,1)S(1)}, bf16[1024,1152]{1,0:T(8,128)(2,1)S(1)}, u32[]{:S(2)}, u32[]{:S(2)}) collective-permute-start(bf16[1024,1152]{1,0:T(8,128)(2,1)S(1)} %fusion), channel_id=1, source_target_pairs={{0,8},{2,10},{4,12},{6,14},{8,0},{10,2},{12,4},{14,6},{16,24},{18,... | collective-permute-start | bytes 7077896 | tf_op jit(solution)/shard_map/ppermute | solution.py:22
  138.6 14.1 %collective-permute-start.17 = (bf16[128,2048]{1,0:T(8,128)(2,1)S(1)}, bf16[128,2048]{1,0:T(8,128)(2,1)S(1)}, u32[]{:S(2)}, u32[]{:S(2)}) collective-permute-start(bf16[128,2048]{1,0:T(8,128)(2,1)S(1)} %pad_maximum_fusion.15), channel_id=1, source_target_pairs={{0,4},{2,6},{4,0},{6,2},{8,12},{10,14},{12,8},{14,10},{16,20},{18,... | collective-permute-start | bytes 1572872 | tf_op jit(solution)/shard_map/ppermute | solution.py:22
  139.2 13.8 %collective-permute-start.18 = (bf16[128,2048]{1,0:T(8,128)(2,1)S(1)}, bf16[128,2048]{1,0:T(8,128)(2,1)S(1)}, u32[]{:S(2)}, u32[]{:S(2)}) collective-permute-start(bf16[128,2048]{1,0:T(8,128)(2,1)S(1)} %pad_maximum_fusion.14), channel_id=1, source_target_pairs={{0,2},{2,0},{4,6},{6,4},{8,10},{10,8},{12,14},{14,12},{16,18},{18,... | collective-permute-start | bytes 1572872 | tf_op jit(solution)/shard_map/ppermute | solution.py:22
  153.1 9.3 %collective-permute-start.23 = (bf16[64,2048]{1,0:T(8,128)(2,1)S(1)}, bf16[64,2048]{1,0:T(8,128)(2,1)S(1)}, u32[]{:S(2)}, u32[]{:S(2)}) collective-permute-start(bf16[64,2048]{1,0:T(8,128)(2,1)S(1)} %get-tuple-element.94), channel_id=1, source_target_pairs={{0,2},{2,0},{4,6},{6,4},{8,10},{10,8},{12,14},{14,12},{16,18},{18,... | collective-permute-start | bytes 786440 | tf_op jit(solution)/shard_map/ppermute | solution.py:22
  153.8 9.2 %collective-permute-start.24 = (bf16[64,2048]{1,0:T(8,128)(2,1)S(1)}, bf16[64,2048]{1,0:T(8,128)(2,1)S(1)}, u32[]{:S(2)}, u32[]{:S(2)}) collective-permute-start(bf16[64,2048]{1,0:T(8,128)(2,1)S(1)} %get-tuple-element.95), channel_id=1, source_target_pairs={{0,4},{2,6},{4,0},{6,2},{8,12},{10,14},{12,8},{14,10},{16,20},{18,... | collective-permute-start | bytes 786440 | tf_op jit(solution)/shard_map/ppermute | solution.py:22
  155.4 17.0 %collective-permute-start.19 = (bf16[128,2048]{1,0:T(8,128)(2,1)S(1)}, bf16[128,2048]{1,0:T(8,128)(2,1)S(1)}, u32[]{:S(2)}, u32[]{:S(2)}) collective-permute-start(bf16[128,2048]{1,0:T(8,128)(2,1)S(1)} %pad_maximum_fusion.16), channel_id=1, source_target_pairs={{0,4},{2,6},{4,0},{6,2},{8,12},{10,14},{12,8},{14,10},{16,20},{18,... | collective-permute-start | bytes 1572872 | tf_op jit(solution)/shard_map/ppermute | solution.py:22
  156.1 16.4 %collective-permute-start.20 = (bf16[128,2048]{1,0:T(8,128)(2,1)S(1)}, bf16[128,2048]{1,0:T(8,128)(2,1)S(1)}, u32[]{:S(2)}, u32[]{:S(2)}) collective-permute-start(bf16[128,2048]{1,0:T(8,128)(2,1)S(1)} %pad_maximum_fusion.17), channel_id=1, source_target_pairs={{0,2},{2,0},{4,6},{6,4},{8,10},{10,8},{12,14},{14,12},{16,18},{18,... | collective-permute-start | bytes 1572872 | tf_op jit(solution)/shard_map/ppermute | solution.py:22
  163.3 26.8 %collective-permute-start.25 = (bf16[128,2048]{1,0:T(8,128)(2,1)S(1)}, bf16[128,2048]{1,0:T(8,128)(2,1)S(1)}, u32[]{:S(2)}, u32[]{:S(2)}) collective-permute-start(bf16[128,2048]{1,0:T(8,128)(2,1)S(1)} %add_convert_fusion.5), channel_id=1, source_target_pairs={{0,16},{2,18},{4,20},{6,22},{8,24},{10,26},{12,28},{14,30},{16,0},... | collective-permute-start | bytes 1572872 | tf_op jit(solution)/shard_map/ppermute | solution.py:22
  165.3 26.1 %collective-permute-start.27 = (bf16[1024,1152]{1,0:T(8,128)(2,1)S(1)}, bf16[1024,1152]{1,0:T(8,128)(2,1)S(1)}, u32[]{:S(2)}, u32[]{:S(2)}) collective-permute-start(bf16[1024,1152]{1,0:T(8,128)(2,1)S(1)} %pad_maximum_fusion.2), channel_id=1, source_target_pairs={{0,1},{1,0},{2,3},{3,2},{4,5},{5,4},{6,7},{7,6},{8,9},{9,8},{10,11... | collective-permute-start | bytes 7077896 | tf_op jit(solution)/shard_map/ppermute | solution.py:20
  172.6 17.6 %collective-permute-start.21 = (bf16[64,2048]{1,0:T(8,128)(2,1)S(1)}, bf16[64,2048]{1,0:T(8,128)(2,1)S(1)}, u32[]{:S(2)}, u32[]{:S(2)}) collective-permute-start(bf16[64,2048]{1,0:T(8,128)(2,1)S(1)} %get-tuple-element.88), channel_id=1, source_target_pairs={{0,2},{2,0},{4,6},{6,4},{8,10},{10,8},{12,14},{14,12},{16,18},{18,... | collective-permute-start | bytes 786440 | tf_op jit(solution)/shard_map/ppermute | solution.py:22
  173.6 16.5 %collective-permute-start.22 = (bf16[64,2048]{1,0:T(8,128)(2,1)S(1)}, bf16[64,2048]{1,0:T(8,128)(2,1)S(1)}, u32[]{:S(2)}, u32[]{:S(2)}) collective-permute-start(bf16[64,2048]{1,0:T(8,128)(2,1)S(1)} %get-tuple-element.89), channel_id=1, source_target_pairs={{0,4},{2,6},{4,0},{6,2},{8,12},{10,14},{12,8},{14,10},{16,20},{18,... | collective-permute-start | bytes 786440 | tf_op jit(solution)/shard_map/ppermute | solution.py:22

commit v3 on v2

--- a/solution.py
+++ b/solution.py
@@ -158,11 +158,13 @@
 
     keep, send = slice(0, mid), slice(mid, width)
 
-    both_mine, down_mine = jnp.concatenate([w_gate[0], w_up[0]], axis=1), w_down[0]
+    gate_mine, up_mine, down_mine = w_gate[0], w_up[0], w_down[0]
+    both_mine = jnp.concatenate([gate_mine, up_mine], axis=1)
     x_own = turn(tokens)
     g_own = jnp.concatenate([turn(out_grad), gate_rows(gates, expert_ids, experts)], axis=0)
     far = swap_far(jnp.concatenate([x_own, g_own], axis=0), ACROSS_Z)
-    both_pair = swap(both_mine, PAIR)
+    gate_pair, up_pair = swap(gate_mine, PAIR), swap(up_mine, PAIR)
+    both_pair = jnp.concatenate([gate_pair, up_pair], axis=1)
     x_x = swap(x_own, ACROSS_X)
     g_y = swap(g_own, ACROSS_Y)
     g_x = swap(after(g_own, x_x, g_y), ACROSS_X)
@@ -176,6 +178,7 @@
     x_near_parts = x_own, x_x, x_y, after(x_xy, both_pair)
     g_near_parts = g_own, g_x, g_y, after(g_xy, both_pair)
     x_near, g_near = join(x_near_parts), join(g_near_parts)
+    x_near, g_near = lax.optimization_barrier((x_near, g_near))
     scale_a_near, scale_b_near = scales(g_near_parts, me), scales(g_near_parts, pair)
     down_pair = swap(after(down_mine, far), PAIR)
     far_of_x, far_of_y = after((far_of_x, far_of_y), x_near, g_near)
@@ -195,7 +198,7 @@
     g_far, g_far_x, g_far_y = [v[tok_rows:] for v in (far, far_of_x, far_of_y)]
     x_far_parts = (x_far, x_far_x, x_far_y, x_far_xy)
     g_far_parts = (g_far, g_far_x, g_far_y, g_far_xy)
-    x_fars, g_fars = join(x_far_parts), join(g_far_parts)
+    x_fars, g_fars = lax.optimization_barrier((join(x_far_parts), join(g_far_parts)))
     hid_b_far, act_b_far = activations(
         dot(x_fars, both_b), dot(g_fars, down_b), scales(g_far_parts, pair)
     )

time: 195 us -> 188 us (0.964)
  matrix products: 32.3 us -> 27.6 us
  other arithmetic: 14.8 us -> 10.8 us
  starting transfers between devices: 30.2 us -> 34.1 us
  waiting for transfers between devices: 89.5 us -> 87 us
    all_to_all x1, waiting for transfers between devices: 15.4 us -> 6.28 us  [swap_far(): lax.all_to_all(jnp.stack([rows, rows]), 'expert', split_axis=0, concat_ax...]
    ppermute x22 -> x23, waiting for transfers between devices: 69.4 us -> 76.8 us  [swap(): return lax.ppermute(rows, 'expert', [(i, i ^ bit) for i in range(experts)])]
    dot_general x24, matrix products: 32.3 us -> 27.6 us  [dot(): return lax.dot_general(a, b, dims, preferred_element_type=wide)]
    ppermute x22 -> x23, starting transfers between devices: 24 us -> 27.9 us  [swap(): return lax.ppermute(rows, 'expert', [(i, i ^ bit) for i in range(experts)])]
    unnamed x20 -> x23, local copies, waits for them, and re-layouts: 1.76 us -> 4.72 us
    concatenate x1, other arithmetic: 2.64 us -> 0.13 us  [dense_local(): both_mine = jnp.concatenate([gate_mine, up_mine], axis=1)]
    slice x7, local copies, waits for them, and re-layouts: 4.73 us -> 2.55 us  [join(): return jnp.concatenate([p[:tok_rows] for p in parts], axis=0)]
  transfers between devices with their start and end apart: 29 -> 30, of which waited for: 20 -> 18; matrix products, arithmetic and copies ran while one was open for 20% -> 18% of each run, Pallas kernels for 5% -> 6%
where the time goes in v3:
time: 188 us
  waiting for transfers between devices  87 us (46%)
  starting transfers between devices  34.1 us (18%)
  matrix products  27.6 us (15%)
  local copies, waits for them, and re-layouts  13.8 us (7%)
  Pallas kernels  13 us (7%)
  other arithmetic  10.8 us (6%)
    ppermute x23, waiting for transfers between devices, swap(): return lax.ppermute(rows, 'expert', [(i, i ^ bit) for i in range(experts)])  76.8 us
    ppermute x23, starting transfers between devices, swap(): return lax.ppermute(rows, 'expert', [(i, i ^ bit) for i in range(experts)])  27.9 us
    dot_general x24, matrix products, dot(): return lax.dot_general(a, b, dims, preferred_element_type=wide)  27.6 us
    pallas_call x2, Pallas kernels, dx_rows(): pl.pallas_call(dx_kernel, grid=(width // tile,), in_specs=[whole, whole,...  10.4 us
    all_to_all x1, waiting for transfers between devices, swap_far(): lax.all_to_all(jnp.stack([rows, rows]), 'expert', split_axis=0, concat_ax...  6.28 us
    all_to_all x1, starting transfers between devices, swap_far(): lax.all_to_all(jnp.stack([rows, rows]), 'expert', split_axis=0, concat_ax...  5.3 us
    unnamed x23, local copies, waits for them, and re-layouts  4.72 us
    ppermute x6, waiting for transfers between devices, swap(): return lax.ppermute(rows, 'dp', [(0, 1), (1, 0)])  3.99 us
  transfers between devices with their start and end apart: 30, of which 18 were waited for; matrix products, arithmetic and copies ran while one was open for 18% of the time, Pallas kernels for 6%

profile of v3, /device:TPU:0, one launch (start us, length us, event | category | flops | bytes accessed | tf_op | source)
XLA Modules:
  0.0 187.8 jit_solution(687189656150217056)
XLA Ops:
  0.7 0.8 select_reduce_fusion
  1.5 1.1 fusion.39
  2.6 1.1 fusion.38
  4.3 1.6 pad_maximum_fusion.3
  5.9 5.3 %all-to-all-start = ((bf16[2,264,2048]{2,1,0:T(8,128)(2,1)}), bf16[2,264,2048]{2,1,0:T(8,128)(2,1)S(1)}, u32[]{:S(2)}, u32[]{:S(2)}) async-start(bf16[2,264,2048]{2,1,0:T(8,128)(2,1)} %pad_maximum_fusion.3), calls=%async_computation | async-start | bytes 4325376 | tf_op jit(solution)/shard_map/all_to_all | solution.py:28
  11.2 2.1 %concatenate.108 = bf16[136,2048]{1,0:T(8,128)(2,1)} concatenate(bf16[128,2048]{1,0:T(8,128)(2,1)S(1)} %maximum_select_fusion, bf16[1,2048]{1,0:T(2,128)(2,1)S(1)} %get-tuple-element.126, bf16[1,2048]{1,0:T(2,128)(2,1)S(1)} %get-tuple-element.125, bf16[1,2048]{1,0:T(2,128)(2,1)S(1)} %get-tuple-element.124, bf16[5,2048]{1,0:T(8,128)(2,1)S(1)} %broadcast_in_dim.22), dimensions={0} | concatenate | bytes 1114112 | tf_op jit(solution)/shard_map/concatenate | solution.py:164
  13.2 1.5 collective-permute-start.1
  14.8 1.5 collective-permute-start
  16.3 1.6 collective-permute-start.5
  17.8 10.3 %collective-permute-done = bf16[128,2048]{1,0:T(8,128)(2,1)S(1)} collective-permute-done((bf16[128,2048]{1,0:T(8,128)(2,1)S(1)}, bf16[128,2048]{1,0:T(8,128)(2,1)S(1)}, u32[]{:S(2)}, u32[]{:S(2)}) %collective-permute-start) | collective-permute-done | bytes 524320 | tf_op jit(solution)/shard_map/ppermute | solution.py:22
  28.1 0.8 copy-done.6
  28.9 1.5 collective-permute-start.2
  30.9 1.6 collective-permute-start.6
  33.2 9.5 %collective-permute-done.3 = bf16[128,2048]{1,0:T(8,128)(2,1)} collective-permute-done((bf16[128,2048]{1,0:T(8,128)(2,1)S(1)}, bf16[128,2048]{1,0:T(8,128)(2,1)}, u32[]{:S(2)}, u32[]{:S(2)}) %collective-permute-start.3) | collective-permute-done | bytes 524320 | tf_op jit(solution)/shard_map/ppermute | solution.py:22
  43.4 1.2 collective-permute-start.4
  44.6 8.0 %collective-permute-done.5 = bf16[1024,384]{1,0:T(8,128)(2,1)} collective-permute-done((bf16[1024,384]{1,0:T(8,128)(2,1)}, bf16[1024,384]{1,0:T(8,128)(2,1)}, u32[]{:S(2)}, u32[]{:S(2)}) %collective-permute-start.5) | collective-permute-done | bytes 786464 | tf_op jit(solution)/shard_map/ppermute | solution.py:22
  52.7 2.1 %constant_dynamic-update-slice_fusion.1 = bf16[1024,768]{1,0:T(8,128)(2,1)} fusion(bf16[1024,384]{1,0:T(8,128)(2,1)} %collective-permute-done.5), kind=kLoop, calls=%fused_computation.89 | loop fusion | bytes 1572864
  54.7 6.3 %all-to-all-done = bf16[2,264,2048]{2,1,0:T(8,128)(2,1)S(1)} async-done(((bf16[2,264,2048]{2,1,0:T(8,128)(2,1)}), bf16[2,264,2048]{2,1,0:T(8,128)(2,1)S(1)}, u32[]{:S(2)}, u32[]{:S(2)}) %all-to-all-start) | async-done | bytes 2162720 | tf_op jit(solution)/shard_map/all_to_all | solution.py:28
  61.2 1.6 collective-permute-start.9
  62.8 1.5 collective-permute-start.8
  64.3 9.8 %collective-permute-done.6 = bf16[1024,384]{1,0:T(8,128)(2,1)} collective-permute-done((bf16[1024,384]{1,0:T(8,128)(2,1)}, bf16[1024,384]{1,0:T(8,128)(2,1)}, u32[]{:S(2)}, u32[]{:S(2)}) %collective-permute-start.6) | collective-permute-done | bytes 786464 | tf_op jit(solution)/shard_map/ppermute | solution.py:22
  74.1 1.3 constant_dynamic-update-slice_fusion
  75.4 1.1 slice.293
  77.3 1.4 pad_maximum_fusion.4
  78.7 1.1 slice.233
  80.1 0.8 copy-done.5
  81.1 4.8 %collective-permute-done.9 = bf16[264,2048]{1,0:T(8,128)(2,1)S(1)} collective-permute-done((bf16[264,2048]{1,0:T(8,128)(2,1)S(1)}, bf16[264,2048]{1,0:T(8,128)(2,1)S(1)}, u32[]{:S(2)}, u32[]{:S(2)}) %collective-permute-start.9) | collective-permute-done | bytes 1081376 | tf_op jit(solution)/shard_map/ppermute | solution.py:22
  85.9 1.4 collective-permute-done.8
  87.8 1.6 collective-permute-start.11
  89.8 8.9 %collective-permute-done.12 = bf16[1024,384]{1,0:T(8,128)(2,1)S(1)} collective-permute-done((bf16[1024,384]{1,0:T(8,128)(2,1)S(1)}, bf16[1024,384]{1,0:T(8,128)(2,1)S(1)}, u32[]{:S(2)}, u32[]{:S(2)}) %collective-permute-start.12) | collective-permute-done | bytes 786464 | tf_op jit(solution)/shard_map/ppermute | solution.py:22
  99.0 1.0 collective-permute-done.11
  101.3 0.9 collective-permute-done.13
  102.5 1.8 fusion.40
  104.3 1.8 fusion.41
  106.1 1.5 multiply_convert_fusion.11
  108.4 1.5 multiply_convert_fusion.9
  110.7 1.0 fusion.18
  111.7 1.1 add_convert_fusion.1
  115.1 1.0 fusion.24
  116.8 1.1 convolution_add_fusion.1
  119.2 0.8 collective-permute-start.27
  119.9 3.1 %collective-permute-done.17 = bf16[1024,384]{1,0:T(8,128)(2,1)S(1)} collective-permute-done((bf16[1024,384]{1,0:T(8,128)(2,1)S(1)}, bf16[1024,384]{1,0:T(8,128)(2,1)S(1)}, u32[]{:S(2)}, u32[]{:S(2)}) %collective-permute-start.17) | collective-permute-done | bytes 786464 | tf_op jit(solution)/shard_map/ppermute | solution.py:20
  123.4 1.8 fusion.42
  125.2 1.5 multiply_convert_fusion.5
  126.8 5.3 %shard_map.102 = bf16[512,2048]{1,0:T(8,128)(2,1)S(1)} custom-call(bf16[512,768]{1,0:T(8,128)(2,1)S(1)} %pad_maximum_fusion.12.act_a, bf16[512,768]{1,0:T(8,128)(2,1)S(1)} %pad_maximum_fusion.11.act_b, bf16[2048,768]{1,0:T(8,128)(2,1)S(1)} %pad_maximum_fusion.w_a, bf16[2048,768]{1,0:T(8,128)(2,1)S(1)} %constant_dynamic-update-slice_fusion.4.w_b), custom_call_target="tpu_custom_call" | custom-call | flops 3221225472 | bytes 8388608 | tf_op jit(solution)/shard_map/pallas_call | solution.py:105
  132.3 1.6 collective-permute-start.19
  133.9 1.5 collective-permute-start.18
  135.4 1.8 fusion.43
  137.2 1.5 multiply_convert_fusion.3
  138.8 1.0 fusion.12
  140.6 5.1 %shard_map.103 = bf16[512,2048]{1,0:T(8,128)(2,1)S(1)} custom-call(bf16[512,768]{1,0:T(8,128)(2,1)S(1)} %pad_maximum_fusion.13.act_a, bf16[512,768]{1,0:T(8,128)(2,1)S(1)} %pad_maximum_fusion.10.act_b, bf16[2048,768]{1,0:T(8,128)(2,1)S(1)} %pad_maximum_fusion.w_a, bf16[2048,768]{1,0:T(8,128)(2,1)S(1)} %constant_dynamic-update-slice_fusion.4.w_b), custom_call_target="tpu_custom_call" | custom-call | flops 3221225472 | bytes 8388608 | tf_op jit(solution)/shard_map/pallas_call | solution.py:105
  146.4 1.0 fusion.6
  148.3 1.5 collective-permute-start.25
  150.0 1.6 collective-permute-start.21
  152.2 4.8 %collective-permute-done.24 = bf16[64,2048]{1,0:T(8,128)(2,1)S(1)} collective-permute-done((bf16[64,2048]{1,0:T(8,128)(2,1)S(1)}, bf16[64,2048]{1,0:T(8,128)(2,1)S(1)}, u32[]{:S(2)}, u32[]{:S(2)}) %collective-permute-start.24) | collective-permute-done | bytes 262176 | tf_op jit(solution)/shard_map/ppermute | solution.py:22
  157.8 2.0 %collective-permute-start.26 = (bf16[128,2048]{1,0:T(8,128)(2,1)S(1)}, bf16[128,2048]{1,0:T(8,128)(2,1)S(1)}, u32[]{:S(2)}, u32[]{:S(2)}) collective-permute-start(bf16[128,2048]{1,0:T(8,128)(2,1)S(1)} %add_convert_fusion.5), channel_id=1, source_target_pairs={{0,16},{2,18},{4,20},{6,22},{8,24},{10,26},{12,28},{14,30},{16,0},... | collective-permute-start | bytes 1572872 | tf_op jit(solution)/shard_map/ppermute | solution.py:22
  160.6 1.0 add_convert_fusion
  161.9 1.1 convolution_add_fusion.both
  163.0 3.8 %collective-permute-done.21 = bf16[128,2048]{1,0:T(8,128)(2,1)S(1)} collective-permute-done((bf16[128,2048]{1,0:T(8,128)(2,1)S(1)}, bf16[128,2048]{1,0:T(8,128)(2,1)S(1)}, u32[]{:S(2)}, u32[]{:S(2)}) %collective-permute-start.21) | collective-permute-done | bytes 524320 | tf_op jit(solution)/shard_map/ppermute | solution.py:22
  167.1 1.6 collective-permute-start.22
  168.7 1.0 collective-permute-start.23
  170.4 13.3 %collective-permute-done.27.more = bf16[1024,1152]{1,0:T(8,128)(2,1)S(1)} collective-permute-done((bf16[1024,1152]{1,0:T(8,128)(2,1)S(1)}, bf16[1024,1152]{1,0:T(8,128)(2,1)S(1)}, u32[]{:S(2)}, u32[]{:S(2)}) %collective-permute-start.27) | collective-permute-done | bytes 2359328 | tf_op jit(solution)/shard_map/ppermute | solution.py:22
  184.2 0.9 maximum_select_fusion.2
  185.1 2.7 %shard_map.104 = (f32[1024,384]{1,0:T(8,128)}, f32[1024,384]{1,0:T(8,128)}, f32[1024,384]{1,0:T(8,128)}) custom-call(f32[1024,768]{1,0:T(8,128)S(1)} %convolution_add_fusion.both, f32[1024,384]{1,0:T(8,128)S(1)} %convolution_add_fusion.2.down, bf16[1024,1152]{1,0:T(8,128)(2,1)S(1)} %collective-permute-done.28.got, ...), custom_call_target="tpu_custom_call" | custom-call | flops 20000000000 | tf_op jit(solution)/shard_map/pallas_call | solution.py:131
  (112 shorter events, 19.6 us)
Async XLA Ops:
  0.6 3.0 %copy-start.3 = (bf16[128,2048]{1,0:T(8,128)(2,1)S(1)}, bf16[128,2048]{1,0:T(8,128)(2,1)}, u32[]{:S(2)}) copy-start(bf16[128,2048]{1,0:T(8,128)(2,1)} %param.7) | copy-start | bytes 1572868
  0.6 3.2 %copy-start.4 = (bf16[128,2048]{1,0:T(8,128)(2,1)S(1)}, bf16[128,2048]{1,0:T(8,128)(2,1)}, u32[]{:S(2)}) copy-start(bf16[128,2048]{1,0:T(8,128)(2,1)} %param.8) | copy-start | bytes 1572868
  5.9 55.1 %all-to-all-start = ((bf16[2,264,2048]{2,1,0:T(8,128)(2,1)}), bf16[2,264,2048]{2,1,0:T(8,128)(2,1)S(1)}, u32[]{:S(2)}, u32[]{:S(2)}) async-start(bf16[2,264,2048]{2,1,0:T(8,128)(2,1)} %pad_maximum_fusion.3), calls=%async_computation | async-start | bytes 4325376 | tf_op jit(solution)/shard_map/all_to_all | solution.py:28
  13.2 14.8 %collective-permute-start.1 = (bf16[136,2048]{1,0:T(8,128)(2,1)}, bf16[136,2048]{1,0:T(8,128)(2,1)S(1)}, u32[]{:S(2)}, u32[]{:S(2)}) collective-permute-start(bf16[136,2048]{1,0:T(8,128)(2,1)} %concatenate.108), channel_id=1, source_target_pairs={{0,4},{2,6},{4,0},{6,2},{8,12},{10,14},{12,8},{14,10},{16,20},{18,... | collective-permute-start | bytes 1671176 | tf_op jit(solution)/shard_map/ppermute | solution.py:22
  14.8 13.3 %collective-permute-start = (bf16[128,2048]{1,0:T(8,128)(2,1)S(1)}, bf16[128,2048]{1,0:T(8,128)(2,1)S(1)}, u32[]{:S(2)}, u32[]{:S(2)}) collective-permute-start(bf16[128,2048]{1,0:T(8,128)(2,1)S(1)} %maximum_select_fusion.1), channel_id=1, source_target_pairs={{0,2},{2,0},{4,6},{6,4},{8,10},{10,8},{12,14},{14,12},{16,18},{18,... | collective-permute-start | bytes 1572872 | tf_op jit(solution)/shard_map/ppermute | solution.py:22
  16.3 36.4 %collective-permute-start.5 = (bf16[1024,384]{1,0:T(8,128)(2,1)}, bf16[1024,384]{1,0:T(8,128)(2,1)}, u32[]{:S(2)}, u32[]{:S(2)}) collective-permute-start(bf16[1024,384]{1,0:T(8,128)(2,1)} %bitcast.40), channel_id=1, source_target_pairs={{0,8},{2,10},{4,12},{6,14},{8,0},{10,2},{12,4},{14,6},{16,24},{18,... | collective-permute-start | bytes 2359304 | tf_op jit(solution)/shard_map/ppermute | solution.py:22
  28.1 0.8 copy-start.6
  28.9 1.5 copy-start.8
  28.9 13.8 %collective-permute-start.2 = (bf16[136,2048]{1,0:T(8,128)(2,1)}, bf16[136,2048]{1,0:T(8,128)(2,1)}, u32[]{:S(2)}, u32[]{:S(2)}) collective-permute-start(bf16[136,2048]{1,0:T(8,128)(2,1)} %concatenate.108), channel_id=1, source_target_pairs={{0,2},{2,0},{4,6},{6,4},{8,10},{10,8},{12,14},{14,12},{16,18},{18,... | collective-permute-start | bytes 1671176 | tf_op jit(solution)/shard_map/ppermute | solution.py:22
  30.4 12.3 %collective-permute-start.3 = (bf16[128,2048]{1,0:T(8,128)(2,1)S(1)}, bf16[128,2048]{1,0:T(8,128)(2,1)}, u32[]{:S(2)}, u32[]{:S(2)}) collective-permute-start(bf16[128,2048]{1,0:T(8,128)(2,1)S(1)} %maximum_select_fusion.1), channel_id=1, source_target_pairs={{0,4},{2,6},{4,0},{6,2},{8,12},{10,14},{12,8},{14,10},{16,20},{18,... | collective-permute-start | bytes 1572872 | tf_op jit(solution)/shard_map/ppermute | solution.py:22
  30.9 43.2 %collective-permute-start.6 = (bf16[1024,384]{1,0:T(8,128)(2,1)}, bf16[1024,384]{1,0:T(8,128)(2,1)}, u32[]{:S(2)}, u32[]{:S(2)}) collective-permute-start(bf16[1024,384]{1,0:T(8,128)(2,1)} %bitcast.37), channel_id=1, source_target_pairs={{0,8},{2,10},{4,12},{6,14},{8,0},{10,2},{12,4},{14,6},{16,24},{18,... | collective-permute-start | bytes 2359304 | tf_op jit(solution)/shard_map/ppermute | solution.py:22
  42.7 18.4 %collective-permute-start.7 = (bf16[128,2048]{1,0:T(8,128)(2,1)}, bf16[128,2048]{1,0:T(8,128)(2,1)}, u32[]{:S(2)}, u32[]{:S(2)}) collective-permute-start(bf16[128,2048]{1,0:T(8,128)(2,1)} %copy-done.6), channel_id=1, source_target_pairs={{0,4},{2,6},{4,0},{6,2},{8,12},{10,14},{12,8},{14,10},{16,20},{18,... | collective-permute-start | bytes 1572872 | tf_op jit(solution)/shard_map/ppermute | solution.py:22
  43.4 17.7 %collective-permute-start.4 = (bf16[136,2048]{1,0:T(8,128)(2,1)}, bf16[136,2048]{1,0:T(8,128)(2,1)}, u32[]{:S(2)}, u32[]{:S(2)}) collective-permute-start(bf16[136,2048]{1,0:T(8,128)(2,1)} %copy-done.8), channel_id=1, source_target_pairs={{0,2},{2,0},{4,6},{6,4},{8,10},{10,8},{12,14},{14,12},{16,18},{18,... | collective-permute-start | bytes 1671176 | tf_op jit(solution)/shard_map/ppermute | solution.py:22
  61.0 13.1 %copy-start = (bf16[1024,768]{1,0:T(8,128)(2,1)S(1)}, bf16[1024,768]{1,0:T(8,128)(2,1)}, u32[]{:S(2)}) copy-start(bf16[1024,768]{1,0:T(8,128)(2,1)} %constant_dynamic-update-slice_fusion.1) | copy-start | bytes 4718596
  61.0 14.4 %copy-start.9 = (bf16[136,2048]{1,0:T(8,128)(2,1)S(1)}, bf16[136,2048]{1,0:T(8,128)(2,1)}, u32[]{:S(2)}) copy-start(bf16[136,2048]{1,0:T(8,128)(2,1)} %copy-done.8) | copy-start | bytes 1671172
  61.1 16.1 %copy-start.7 = (bf16[128,2048]{1,0:T(8,128)(2,1)S(1)}, bf16[128,2048]{1,0:T(8,128)(2,1)}, u32[]{:S(2)}) copy-start(bf16[128,2048]{1,0:T(8,128)(2,1)} %copy-done.6) | copy-start | bytes 1572868
  61.2 24.7 %collective-permute-start.9 = (bf16[264,2048]{1,0:T(8,128)(2,1)S(1)}, bf16[264,2048]{1,0:T(8,128)(2,1)S(1)}, u32[]{:S(2)}, u32[]{:S(2)}) collective-permute-start(bf16[264,2048]{1,0:T(8,128)(2,1)S(1)} %fusion.1), channel_id=1, source_target_pairs={{0,4},{2,6},{4,0},{6,2},{8,12},{10,14},{12,8},{14,10},{16,20},{18,... | collective-permute-start | bytes 3244040 | tf_op jit(solution)/shard_map/ppermute | solution.py:22
  62.8 24.4 %collective-permute-start.8 = (bf16[264,2048]{1,0:T(8,128)(2,1)S(1)}, bf16[264,2048]{1,0:T(8,128)(2,1)S(1)}, u32[]{:S(2)}, u32[]{:S(2)}) collective-permute-start(bf16[264,2048]{1,0:T(8,128)(2,1)S(1)} %fusion.1), channel_id=1, source_target_pairs={{0,2},{2,0},{4,6},{6,4},{8,10},{10,8},{12,14},{14,12},{16,18},{18,... | collective-permute-start | bytes 3244040 | tf_op jit(solution)/shard_map/ppermute | solution.py:22
  79.8 1.1 copy-start.5
  80.9 17.7 %collective-permute-start.12 = (bf16[1024,384]{1,0:T(8,128)(2,1)S(1)}, bf16[1024,384]{1,0:T(8,128)(2,1)S(1)}, u32[]{:S(2)}, u32[]{:S(2)}) collective-permute-start(bf16[1024,384]{1,0:T(8,128)(2,1)S(1)} %bitcast.43), channel_id=1, source_target_pairs={{0,8},{2,10},{4,12},{6,14},{8,0},{10,2},{12,4},{14,6},{16,24},{18,... | collective-permute-start | bytes 2359304 | tf_op jit(solution)/shard_map/ppermute | solution.py:22
  87.4 11.6 %collective-permute-start.10 = (bf16[128,2048]{1,0:T(8,128)(2,1)S(1)}, bf16[128,2048]{1,0:T(8,128)(2,1)S(1)}, u32[]{:S(2)}, u32[]{:S(2)}) collective-permute-start(bf16[128,2048]{1,0:T(8,128)(2,1)S(1)} %get-tuple-element.115), channel_id=1, source_target_pairs={{0,4},{2,6},{4,0},{6,2},{8,12},{10,14},{12,8},{14,10},{16,20},{18,... | collective-permute-start | bytes 1572872 | tf_op jit(solution)/shard_map/ppermute | solution.py:22
  87.8 12.1 %collective-permute-start.11 = (bf16[136,2048]{1,0:T(8,128)(2,1)S(1)}, bf16[136,2048]{1,0:T(8,128)(2,1)S(1)}, u32[]{:S(2)}, u32[]{:S(2)}) collective-permute-start(bf16[136,2048]{1,0:T(8,128)(2,1)S(1)} %slice.239), channel_id=1, source_target_pairs={{0,2},{2,0},{4,6},{6,4},{8,10},{10,8},{12,14},{14,12},{16,18},{18,... | collective-permute-start | bytes 1671176 | tf_op jit(solution)/shard_map/ppermute | solution.py:22
  89.4 13.0 %collective-permute-start.14 = (bf16[1024,768]{1,0:T(8,128)(2,1)S(1)}, bf16[1024,768]{1,0:T(8,128)(2,1)S(1)}, u32[]{:S(2)}, u32[]{:S(2)}) collective-permute-start(bf16[1024,768]{1,0:T(8,128)(2,1)S(1)} %constant_dynamic-update-slice_fusion), channel_id=1, source_target_pairs={{0,1},{1,0},{2,3},{3,2},{4,5},{5,4},{6,7},{7,6},{8,9},{9,8},{10,11... | collective-permute-start | bytes 4718600 | tf_op jit(solution)/shard_map/ppermute | solution.py:20
  100.0 2.3 %collective-permute-start.13 = (bf16[1024,384]{1,0:T(8,128)(2,1)S(1)}, bf16[1024,384]{1,0:T(8,128)(2,1)S(1)}, u32[]{:S(2)}, u32[]{:S(2)}) collective-permute-start(bf16[1024,384]{1,0:T(8,128)(2,1)S(1)} %collective-permute-done.12), channel_id=1, source_target_pairs={{0,1},{1,0},{2,3},{3,2},{4,5},{5,4},{6,7},{7,6},{8,9},{9,8},{10,11... | collective-permute-start | bytes 2359304 | tf_op jit(solution)/shard_map/ppermute | solution.py:20
  112.8 1.1 copy-start.1
  112.8 1.4 copy-start.2
  113.2 4.8 %collective-permute-start.15 = (bf16[1024,1152]{1,0:T(8,128)(2,1)S(1)}, bf16[1024,1152]{1,0:T(8,128)(2,1)S(1)}, u32[]{:S(2)}, u32[]{:S(2)}) collective-permute-start(bf16[1024,1152]{1,0:T(8,128)(2,1)S(1)} %pad_maximum_fusion.1), channel_id=1, source_target_pairs={{0,1},{1,0},{2,3},{3,2},{4,5},{5,4},{6,7},{7,6},{8,9},{9,8},{10,11... | collective-permute-start | bytes 7077896 | tf_op jit(solution)/shard_map/ppermute | solution.py:20
  118.4 4.8 %collective-permute-start.16 = (bf16[1024,768]{1,0:T(8,128)(2,1)S(1)}, bf16[1024,768]{1,0:T(8,128)(2,1)S(1)}, u32[]{:S(2)}, u32[]{:S(2)}) collective-permute-start(bf16[1024,768]{1,0:T(8,128)(2,1)S(1)} %pad_maximum_fusion.8), channel_id=1, source_target_pairs={{0,1},{1,0},{2,3},{3,2},{4,5},{5,4},{6,7},{7,6},{8,9},{9,8},{10,11... | collective-permute-start | bytes 4718600 | tf_op jit(solution)/shard_map/ppermute | solution.py:20
  118.6 4.4 %collective-permute-start.17 = (bf16[1024,384]{1,0:T(8,128)(2,1)S(1)}, bf16[1024,384]{1,0:T(8,128)(2,1)S(1)}, u32[]{:S(2)}, u32[]{:S(2)}) collective-permute-start(bf16[1024,384]{1,0:T(8,128)(2,1)S(1)} %bitcast.44), channel_id=1, source_target_pairs={{0,1},{1,0},{2,3},{3,2},{4,5},{5,4},{6,7},{7,6},{8,9},{9,8},{10,11... | collective-permute-start | bytes 2359304 | tf_op jit(solution)/shard_map/ppermute | solution.py:20
  119.2 64.6 %collective-permute-start.27 = (bf16[1024,1152]{1,0:T(8,128)(2,1)S(1)}, bf16[1024,1152]{1,0:T(8,128)(2,1)S(1)}, u32[]{:S(2)}, u32[]{:S(2)}) collective-permute-start(bf16[1024,1152]{1,0:T(8,128)(2,1)S(1)} %fusion), channel_id=1, source_target_pairs={{0,8},{2,10},{4,12},{6,14},{8,0},{10,2},{12,4},{14,6},{16,24},{18,... | collective-permute-start | bytes 7077896 | tf_op jit(solution)/shard_map/ppermute | solution.py:22
  132.3 15.2 %collective-permute-start.19 = (bf16[128,2048]{1,0:T(8,128)(2,1)S(1)}, bf16[128,2048]{1,0:T(8,128)(2,1)S(1)}, u32[]{:S(2)}, u32[]{:S(2)}) collective-permute-start(bf16[128,2048]{1,0:T(8,128)(2,1)S(1)} %pad_maximum_fusion.14), channel_id=1, source_target_pairs={{0,2},{2,0},{4,6},{6,4},{8,10},{10,8},{12,14},{14,12},{16,18},{18,... | collective-permute-start | bytes 1572872 | tf_op jit(solution)/shard_map/ppermute | solution.py:22
  133.9 13.7 %collective-permute-start.18 = (bf16[128,2048]{1,0:T(8,128)(2,1)S(1)}, bf16[128,2048]{1,0:T(8,128)(2,1)S(1)}, u32[]{:S(2)}, u32[]{:S(2)}) collective-permute-start(bf16[128,2048]{1,0:T(8,128)(2,1)S(1)} %pad_maximum_fusion.15), channel_id=1, source_target_pairs={{0,4},{2,6},{4,0},{6,2},{8,12},{10,14},{12,8},{14,10},{16,20},{18,... | collective-permute-start | bytes 1572872 | tf_op jit(solution)/shard_map/ppermute | solution.py:22
  147.7 9.3 %collective-permute-start.24 = (bf16[64,2048]{1,0:T(8,128)(2,1)S(1)}, bf16[64,2048]{1,0:T(8,128)(2,1)S(1)}, u32[]{:S(2)}, u32[]{:S(2)}) collective-permute-start(bf16[64,2048]{1,0:T(8,128)(2,1)S(1)} %get-tuple-element.102), channel_id=1, source_target_pairs={{0,2},{2,0},{4,6},{6,4},{8,10},{10,8},{12,14},{14,12},{16,18},{18,... | collective-permute-start | bytes 786440 | tf_op jit(solution)/shard_map/ppermute | solution.py:22
  148.3 9.2 %collective-permute-start.25 = (bf16[64,2048]{1,0:T(8,128)(2,1)S(1)}, bf16[64,2048]{1,0:T(8,128)(2,1)S(1)}, u32[]{:S(2)}, u32[]{:S(2)}) collective-permute-start(bf16[64,2048]{1,0:T(8,128)(2,1)S(1)} %get-tuple-element.103), channel_id=1, source_target_pairs={{0,4},{2,6},{4,0},{6,2},{8,12},{10,14},{12,8},{14,10},{16,20},{18,... | collective-permute-start | bytes 786440 | tf_op jit(solution)/shard_map/ppermute | solution.py:22
  150.0 16.8 %collective-permute-start.21 = (bf16[128,2048]{1,0:T(8,128)(2,1)S(1)}, bf16[128,2048]{1,0:T(8,128)(2,1)S(1)}, u32[]{:S(2)}, u32[]{:S(2)}) collective-permute-start(bf16[128,2048]{1,0:T(8,128)(2,1)S(1)} %pad_maximum_fusion.17), channel_id=1, source_target_pairs={{0,2},{2,0},{4,6},{6,4},{8,10},{10,8},{12,14},{14,12},{16,18},{18,... | collective-permute-start | bytes 1572872 | tf_op jit(solution)/shard_map/ppermute | solution.py:22
  151.6 15.4 %collective-permute-start.20 = (bf16[128,2048]{1,0:T(8,128)(2,1)S(1)}, bf16[128,2048]{1,0:T(8,128)(2,1)S(1)}, u32[]{:S(2)}, u32[]{:S(2)}) collective-permute-start(bf16[128,2048]{1,0:T(8,128)(2,1)S(1)} %pad_maximum_fusion.16), channel_id=1, source_target_pairs={{0,4},{2,6},{4,0},{6,2},{8,12},{10,14},{12,8},{14,10},{16,20},{18,... | collective-permute-start | bytes 1572872 | tf_op jit(solution)/shard_map/ppermute | solution.py:22
  157.8 26.0 %collective-permute-start.26 = (bf16[128,2048]{1,0:T(8,128)(2,1)S(1)}, bf16[128,2048]{1,0:T(8,128)(2,1)S(1)}, u32[]{:S(2)}, u32[]{:S(2)}) collective-permute-start(bf16[128,2048]{1,0:T(8,128)(2,1)S(1)} %add_convert_fusion.5), channel_id=1, source_target_pairs={{0,16},{2,18},{4,20},{6,22},{8,24},{10,26},{12,28},{14,30},{16,0},... | collective-permute-start | bytes 1572872 | tf_op jit(solution)/shard_map/ppermute | solution.py:22
  161.8 23.3 %collective-permute-start.28 = (bf16[1024,1152]{1,0:T(8,128)(2,1)S(1)}, bf16[1024,1152]{1,0:T(8,128)(2,1)S(1)}, u32[]{:S(2)}, u32[]{:S(2)}) collective-permute-start(bf16[1024,1152]{1,0:T(8,128)(2,1)S(1)} %pad_maximum_fusion.2), channel_id=1, source_target_pairs={{0,1},{1,0},{2,3},{3,2},{4,5},{5,4},{6,7},{7,6},{8,9},{9,8},{10,11... | collective-permute-start | bytes 7077896 | tf_op jit(solution)/shard_map/ppermute | solution.py:20
  167.1 16.7 %collective-permute-start.22 = (bf16[64,2048]{1,0:T(8,128)(2,1)S(1)}, bf16[64,2048]{1,0:T(8,128)(2,1)S(1)}, u32[]{:S(2)}, u32[]{:S(2)}) collective-permute-start(bf16[64,2048]{1,0:T(8,128)(2,1)S(1)} %get-tuple-element.96), channel_id=1, source_target_pairs={{0,2},{2,0},{4,6},{6,4},{8,10},{10,8},{12,14},{14,12},{16,18},{18,... | collective-permute-start | bytes 786440 | tf_op jit(solution)/shard_map/ppermute | solution.py:22
  168.7 15.1 %collective-permute-start.23 = (bf16[64,2048]{1,0:T(8,128)(2,1)S(1)}, bf16[64,2048]{1,0:T(8,128)(2,1)S(1)}, u32[]{:S(2)}, u32[]{:S(2)}) collective-permute-start(bf16[64,2048]{1,0:T(8,128)(2,1)S(1)} %get-tuple-element.97), channel_id=1, source_target_pairs={{0,4},{2,6},{4,0},{6,2},{8,12},{10,14},{12,8},{14,10},{16,20},{18,... | collective-permute-start | bytes 786440 | tf_op jit(solution)/shard_map/ppermute | solution.py:22

commit v4 on v3

--- a/solution.py
+++ b/solution.py
@@ -99,7 +99,7 @@
 def dx_rows(act_a, act_b, w_a, w_b):
     rows, depth = act_a.shape
     width = w_a.shape[0]
-    tile = min(width, 256)
+    tile = min(width, 512)
     whole = pl.BlockSpec((rows, depth), lambda i: (0, 0))
     part = pl.BlockSpec((tile, depth), lambda i: (i, 0))
     return pl.pallas_call(
@@ -108,7 +108,7 @@
         in_specs=[whole, whole, part, part],
         out_specs=pl.BlockSpec((rows, tile), lambda i: (0, i)),
         out_shape=jax.ShapeDtypeStruct((rows, width), low),
-        compiler_params=pltpu.CompilerParams(vmem_limit_bytes=10 << 20),
+        compiler_params=pltpu.CompilerParams(vmem_limit_bytes=16 << 20),
         cost_estimate=pl.CostEstimate(
             flops=4 * rows * depth * width, bytes_accessed=4 * width * depth + 2 * rows * width, transcendentals=0
         ),
@@ -175,7 +175,7 @@
     far = after(far, g_xy, x_xy)
     far_of_x = swap(far, ACROSS_X)
     far_of_y = swap(far, ACROSS_Y)
-    x_near_parts = x_own, x_x, x_y, after(x_xy, both_pair)
+    x_near_parts = x_own, x_x, x_y, x_xy
     g_near_parts = g_own, g_x, g_y, after(g_xy, both_pair)
     x_near, g_near = join(x_near_parts), join(g_near_parts)
     x_near, g_near = lax.optimization_barrier((x_near, g_near))
@@ -188,7 +188,7 @@
     both_pair_other = swap(both_pair, 0)
     both_b = jnp.concatenate([both_pair, both_pair_other], axis=0)
     pre_b_near = dot(x_near, both_b)
-    down_pair = after(down_pair, g_far_xy, x_far_xy)
+    down_pair = after(down_pair, x_far_xy)
     down_pair_other = swap(down_pair, 0)
     down_b = jnp.concatenate([down_pair, down_pair_other], axis=0)
     x_far, x_far_x, x_far_y = [v[:tok_rows] for v in (far, far_of_x, far_of_y)]

time: 188 us -> 187 us (level)
  transfers between devices with their start and end apart: 30 -> 30, of which waited for: 18 -> 18; matrix products, arithmetic and copies ran while one was open for 18% -> 18% of each run, Pallas kernels for 6% -> 5%
where the time goes in v4:
time: 187 us
  waiting for transfers between devices  87.1 us (47%)
  starting transfers between devices  34.9 us (19%)
  matrix products  27.6 us (15%)
  local copies, waits for them, and re-layouts  13.8 us (7%)
  Pallas kernels  11.2 us (6%)
  other arithmetic  10.8 us (6%)
    ppermute x23, waiting for transfers between devices, swap(): return lax.ppermute(rows, 'expert', [(i, i ^ bit) for i in range(experts)])  77.4 us
    ppermute x23, starting transfers between devices, swap(): return lax.ppermute(rows, 'expert', [(i, i ^ bit) for i in range(experts)])  28.8 us
    dot_general x24, matrix products, dot(): return lax.dot_general(a, b, dims, preferred_element_type=wide)  27.6 us
    pallas_call x2, Pallas kernels, dx_rows(): pl.pallas_call(dx_kernel, grid=(width // tile,), in_specs=[whole, whole,...  8.59 us
    all_to_all x1, waiting for transfers between devices, swap_far(): lax.all_to_all(jnp.stack([rows, rows]), 'expert', split_axis=0, concat_ax...  6.28 us
    all_to_all x1, starting transfers between devices, swap_far(): lax.all_to_all(jnp.stack([rows, rows]), 'expert', split_axis=0, concat_ax...  5.3 us
    unnamed x23, local copies, waits for them, and re-layouts  4.72 us
  transfers between devices with their start and end apart: 30, of which 18 were waited for; matrix products, arithmetic and copies ran while one was open for 18% of the time, Pallas kernels for 5%

profile of v4, /device:TPU:0, one launch (start us, length us, event | category | flops | bytes accessed | tf_op | source)
XLA Modules:
  0.0 186.8 jit_solution(272768505743768839)
XLA Ops:
  0.7 0.8 select_reduce_fusion
  1.5 1.1 fusion.39
  2.6 1.1 fusion.38
  4.3 1.6 pad_maximum_fusion.3
  5.9 5.3 %all-to-all-start = ((bf16[2,264,2048]{2,1,0:T(8,128)(2,1)}), bf16[2,264,2048]{2,1,0:T(8,128)(2,1)S(1)}, u32[]{:S(2)}, u32[]{:S(2)}) async-start(bf16[2,264,2048]{2,1,0:T(8,128)(2,1)} %pad_maximum_fusion.3), calls=%async_computation | async-start | bytes 4325376 | tf_op jit(solution)/shard_map/all_to_all | solution.py:28
  11.2 2.1 %concatenate.108 = bf16[136,2048]{1,0:T(8,128)(2,1)} concatenate(bf16[128,2048]{1,0:T(8,128)(2,1)S(1)} %maximum_select_fusion, bf16[1,2048]{1,0:T(2,128)(2,1)S(1)} %get-tuple-element.124, bf16[1,2048]{1,0:T(2,128)(2,1)S(1)} %get-tuple-element.123, bf16[1,2048]{1,0:T(2,128)(2,1)S(1)} %get-tuple-element.122, bf16[5,2048]{1,0:T(8,128)(2,1)S(1)} %broadcast_in_dim.22), dimensions={0} | concatenate | bytes 1114112 | tf_op jit(solution)/shard_map/concatenate | solution.py:164
  13.2 1.5 collective-permute-start.1
  14.8 1.5 collective-permute-start
  16.3 1.6 collective-permute-start.5
  17.8 10.3 %collective-permute-done = bf16[128,2048]{1,0:T(8,128)(2,1)S(1)} collective-permute-done((bf16[128,2048]{1,0:T(8,128)(2,1)S(1)}, bf16[128,2048]{1,0:T(8,128)(2,1)S(1)}, u32[]{:S(2)}, u32[]{:S(2)}) %collective-permute-start) | collective-permute-done | bytes 524320 | tf_op jit(solution)/shard_map/ppermute | solution.py:22
  28.1 0.8 copy-done.6
  28.9 1.5 collective-permute-start.2
  30.9 1.6 collective-permute-start.6
  33.2 9.5 %collective-permute-done.3 = bf16[128,2048]{1,0:T(8,128)(2,1)} collective-permute-done((bf16[128,2048]{1,0:T(8,128)(2,1)S(1)}, bf16[128,2048]{1,0:T(8,128)(2,1)}, u32[]{:S(2)}, u32[]{:S(2)}) %collective-permute-start.3) | collective-permute-done | bytes 524320 | tf_op jit(solution)/shard_map/ppermute | solution.py:22
  43.4 1.2 collective-permute-start.4
  44.6 8.0 %collective-permute-done.5 = bf16[1024,384]{1,0:T(8,128)(2,1)} collective-permute-done((bf16[1024,384]{1,0:T(8,128)(2,1)}, bf16[1024,384]{1,0:T(8,128)(2,1)}, u32[]{:S(2)}, u32[]{:S(2)}) %collective-permute-start.5) | collective-permute-done | bytes 786464 | tf_op jit(solution)/shard_map/ppermute | solution.py:22
  52.7 2.1 %constant_dynamic-update-slice_fusion.1 = bf16[1024,768]{1,0:T(8,128)(2,1)} fusion(bf16[1024,384]{1,0:T(8,128)(2,1)} %collective-permute-done.5), kind=kLoop, calls=%fused_computation.89 | loop fusion | bytes 1572864
  54.7 6.3 %all-to-all-done = bf16[2,264,2048]{2,1,0:T(8,128)(2,1)S(1)} async-done(((bf16[2,264,2048]{2,1,0:T(8,128)(2,1)}), bf16[2,264,2048]{2,1,0:T(8,128)(2,1)S(1)}, u32[]{:S(2)}, u32[]{:S(2)}) %all-to-all-start) | async-done | bytes 2162720 | tf_op jit(solution)/shard_map/all_to_all | solution.py:28
  61.2 1.6 collective-permute-start.9
  62.8 1.5 collective-permute-start.8
  64.3 9.8 %collective-permute-done.6 = bf16[1024,384]{1,0:T(8,128)(2,1)} collective-permute-done((bf16[1024,384]{1,0:T(8,128)(2,1)}, bf16[1024,384]{1,0:T(8,128)(2,1)}, u32[]{:S(2)}, u32[]{:S(2)}) %collective-permute-start.6) | collective-permute-done | bytes 786464 | tf_op jit(solution)/shard_map/ppermute | solution.py:22
  74.1 1.3 constant_dynamic-update-slice_fusion
  75.5 1.1 slice.293
  77.3 1.4 pad_maximum_fusion.4
  78.7 1.1 slice.233
  80.1 0.8 copy-done.5
  81.1 4.8 %collective-permute-done.9 = bf16[264,2048]{1,0:T(8,128)(2,1)S(1)} collective-permute-done((bf16[264,2048]{1,0:T(8,128)(2,1)S(1)}, bf16[264,2048]{1,0:T(8,128)(2,1)S(1)}, u32[]{:S(2)}, u32[]{:S(2)}) %collective-permute-start.9) | collective-permute-done | bytes 1081376 | tf_op jit(solution)/shard_map/ppermute | solution.py:22
  85.9 1.4 collective-permute-done.8
  87.9 1.6 collective-permute-start.11
  89.8 8.9 %collective-permute-done.12 = bf16[1024,384]{1,0:T(8,128)(2,1)S(1)} collective-permute-done((bf16[1024,384]{1,0:T(8,128)(2,1)S(1)}, bf16[1024,384]{1,0:T(8,128)(2,1)S(1)}, u32[]{:S(2)}, u32[]{:S(2)}) %collective-permute-start.12) | collective-permute-done | bytes 786464 | tf_op jit(solution)/shard_map/ppermute | solution.py:22
  101.6 1.8 fusion.40
  103.4 1.8 fusion.41
  105.2 1.5 multiply_convert_fusion.11
  107.4 1.5 multiply_convert_fusion.9
  109.0 0.8 add_convert_fusion.3
  109.7 1.0 fusion.18
  110.8 1.1 add_convert_fusion.1
  114.1 1.0 fusion.24
  115.9 1.1 convolution_add_fusion.1
  118.9 3.1 %collective-permute-done.17 = bf16[1024,384]{1,0:T(8,128)(2,1)S(1)} collective-permute-done((bf16[1024,384]{1,0:T(8,128)(2,1)S(1)}, bf16[1024,384]{1,0:T(8,128)(2,1)S(1)}, u32[]{:S(2)}, u32[]{:S(2)}) %collective-permute-start.17) | collective-permute-done | bytes 786464 | tf_op jit(solution)/shard_map/ppermute | solution.py:20
  122.5 1.8 fusion.42
  124.2 1.5 multiply_convert_fusion.5
  125.8 4.2 %shard_map.102 = bf16[512,2048]{1,0:T(8,128)(2,1)S(1)} custom-call(bf16[512,768]{1,0:T(8,128)(2,1)S(1)} %pad_maximum_fusion.12.act_a, bf16[512,768]{1,0:T(8,128)(2,1)S(1)} %pad_maximum_fusion.11.act_b, bf16[2048,768]{1,0:T(8,128)(2,1)S(1)} %pad_maximum_fusion.w_a, bf16[2048,768]{1,0:T(8,128)(2,1)S(1)} %constant_dynamic-update-slice_fusion.4.w_b), custom_call_target="tpu_custom_call" | custom-call | flops 3221225472 | bytes 8388608 | tf_op jit(solution)/shard_map/pallas_call | solution.py:105
  130.2 1.6 collective-permute-start.19
  131.8 1.3 collective-permute-start.18
  133.0 1.8 fusion.43
  134.8 1.5 multiply_convert_fusion.3
  136.5 1.0 fusion.12
  138.2 4.4 %shard_map.103 = bf16[512,2048]{1,0:T(8,128)(2,1)S(1)} custom-call(bf16[512,768]{1,0:T(8,128)(2,1)S(1)} %pad_maximum_fusion.13.act_a, bf16[512,768]{1,0:T(8,128)(2,1)S(1)} %pad_maximum_fusion.10.act_b, bf16[2048,768]{1,0:T(8,128)(2,1)S(1)} %pad_maximum_fusion.w_a, bf16[2048,768]{1,0:T(8,128)(2,1)S(1)} %constant_dynamic-update-slice_fusion.4.w_b), custom_call_target="tpu_custom_call" | custom-call | flops 3221225472 | bytes 8388608 | tf_op jit(solution)/shard_map/pallas_call | solution.py:105
  143.4 1.0 fusion.6
  144.5 1.1 collective-permute-done.18
  146.2 1.2 collective-permute-start.25
  147.6 1.5 collective-permute-start.21
  149.2 0.9 collective-permute-start.20
  150.2 4.8 %collective-permute-done.24 = bf16[64,2048]{1,0:T(8,128)(2,1)S(1)} collective-permute-done((bf16[64,2048]{1,0:T(8,128)(2,1)S(1)}, bf16[64,2048]{1,0:T(8,128)(2,1)S(1)}, u32[]{:S(2)}, u32[]{:S(2)}) %collective-permute-start.24) | collective-permute-done | bytes 262176 | tf_op jit(solution)/shard_map/ppermute | solution.py:22
  155.7 2.9 %collective-permute-start.26 = (bf16[128,2048]{1,0:T(8,128)(2,1)S(1)}, bf16[128,2048]{1,0:T(8,128)(2,1)S(1)}, u32[]{:S(2)}, u32[]{:S(2)}) collective-permute-start(bf16[128,2048]{1,0:T(8,128)(2,1)S(1)} %add_convert_fusion.5), channel_id=1, source_target_pairs={{0,16},{2,18},{4,20},{6,22},{8,24},{10,26},{12,28},{14,30},{16,0},... | collective-permute-start | bytes 1572872 | tf_op jit(solution)/shard_map/ppermute | solution.py:22
  159.4 1.0 add_convert_fusion
  160.7 1.1 convolution_add_fusion.both
  161.8 2.3 %collective-permute-done.21 = bf16[128,2048]{1,0:T(8,128)(2,1)S(1)} collective-permute-done((bf16[128,2048]{1,0:T(8,128)(2,1)S(1)}, bf16[128,2048]{1,0:T(8,128)(2,1)S(1)}, u32[]{:S(2)}, u32[]{:S(2)}) %collective-permute-start.21) | collective-permute-done | bytes 524320 | tf_op jit(solution)/shard_map/ppermute | solution.py:22
  164.5 1.5 collective-permute-start.22
  166.1 1.2 collective-permute-start.23
  168.0 14.7 %collective-permute-done.27.more = bf16[1024,1152]{1,0:T(8,128)(2,1)S(1)} collective-permute-done((bf16[1024,1152]{1,0:T(8,128)(2,1)S(1)}, bf16[1024,1152]{1,0:T(8,128)(2,1)S(1)}, u32[]{:S(2)}, u32[]{:S(2)}) %collective-permute-start.27) | collective-permute-done | bytes 2359328 | tf_op jit(solution)/shard_map/ppermute | solution.py:22
  183.2 0.9 maximum_select_fusion.2
  184.2 2.7 %shard_map.104 = (f32[1024,384]{1,0:T(8,128)}, f32[1024,384]{1,0:T(8,128)}, f32[1024,384]{1,0:T(8,128)}) custom-call(f32[1024,768]{1,0:T(8,128)S(1)} %convolution_add_fusion.both, f32[1024,384]{1,0:T(8,128)S(1)} %convolution_add_fusion.2.down, bf16[1024,1152]{1,0:T(8,128)(2,1)S(1)} %collective-permute-done.28.got, ...), custom_call_target="tpu_custom_call" | custom-call | flops 20000000000 | tf_op jit(solution)/shard_map/pallas_call | solution.py:131
  (112 shorter events, 19.8 us)
Async XLA Ops:
  0.6 3.0 %copy-start.3 = (bf16[128,2048]{1,0:T(8,128)(2,1)S(1)}, bf16[128,2048]{1,0:T(8,128)(2,1)}, u32[]{:S(2)}) copy-start(bf16[128,2048]{1,0:T(8,128)(2,1)} %param.7) | copy-start | bytes 1572868
  0.6 3.2 %copy-start.4 = (bf16[128,2048]{1,0:T(8,128)(2,1)S(1)}, bf16[128,2048]{1,0:T(8,128)(2,1)}, u32[]{:S(2)}) copy-start(bf16[128,2048]{1,0:T(8,128)(2,1)} %param.8) | copy-start | bytes 1572868
  5.9 55.1 %all-to-all-start = ((bf16[2,264,2048]{2,1,0:T(8,128)(2,1)}), bf16[2,264,2048]{2,1,0:T(8,128)(2,1)S(1)}, u32[]{:S(2)}, u32[]{:S(2)}) async-start(bf16[2,264,2048]{2,1,0:T(8,128)(2,1)} %pad_maximum_fusion.3), calls=%async_computation | async-start | bytes 4325376 | tf_op jit(solution)/shard_map/all_to_all | solution.py:28
  13.2 14.8 %collective-permute-start.1 = (bf16[136,2048]{1,0:T(8,128)(2,1)}, bf16[136,2048]{1,0:T(8,128)(2,1)S(1)}, u32[]{:S(2)}, u32[]{:S(2)}) collective-permute-start(bf16[136,2048]{1,0:T(8,128)(2,1)} %concatenate.108), channel_id=1, source_target_pairs={{0,4},{2,6},{4,0},{6,2},{8,12},{10,14},{12,8},{14,10},{16,20},{18,... | collective-permute-start | bytes 1671176 | tf_op jit(solution)/shard_map/ppermute | solution.py:22
  14.8 13.3 %collective-permute-start = (bf16[128,2048]{1,0:T(8,128)(2,1)S(1)}, bf16[128,2048]{1,0:T(8,128)(2,1)S(1)}, u32[]{:S(2)}, u32[]{:S(2)}) collective-permute-start(bf16[128,2048]{1,0:T(8,128)(2,1)S(1)} %maximum_select_fusion.1), channel_id=1, source_target_pairs={{0,2},{2,0},{4,6},{6,4},{8,10},{10,8},{12,14},{14,12},{16,18},{18,... | collective-permute-start | bytes 1572872 | tf_op jit(solution)/shard_map/ppermute | solution.py:22
  16.3 36.4 %collective-permute-start.5 = (bf16[1024,384]{1,0:T(8,128)(2,1)}, bf16[1024,384]{1,0:T(8,128)(2,1)}, u32[]{:S(2)}, u32[]{:S(2)}) collective-permute-start(bf16[1024,384]{1,0:T(8,128)(2,1)} %bitcast.40), channel_id=1, source_target_pairs={{0,8},{2,10},{4,12},{6,14},{8,0},{10,2},{12,4},{14,6},{16,24},{18,... | collective-permute-start | bytes 2359304 | tf_op jit(solution)/shard_map/ppermute | solution.py:22
  28.1 0.8 copy-start.6
  28.9 1.5 copy-start.8
  28.9 13.8 %collective-permute-start.2 = (bf16[136,2048]{1,0:T(8,128)(2,1)}, bf16[136,2048]{1,0:T(8,128)(2,1)}, u32[]{:S(2)}, u32[]{:S(2)}) collective-permute-start(bf16[136,2048]{1,0:T(8,128)(2,1)} %concatenate.108), channel_id=1, source_target_pairs={{0,2},{2,0},{4,6},{6,4},{8,10},{10,8},{12,14},{14,12},{16,18},{18,... | collective-permute-start | bytes 1671176 | tf_op jit(solution)/shard_map/ppermute | solution.py:22
  30.4 12.3 %collective-permute-start.3 = (bf16[128,2048]{1,0:T(8,128)(2,1)S(1)}, bf16[128,2048]{1,0:T(8,128)(2,1)}, u32[]{:S(2)}, u32[]{:S(2)}) collective-permute-start(bf16[128,2048]{1,0:T(8,128)(2,1)S(1)} %maximum_select_fusion.1), channel_id=1, source_target_pairs={{0,4},{2,6},{4,0},{6,2},{8,12},{10,14},{12,8},{14,10},{16,20},{18,... | collective-permute-start | bytes 1572872 | tf_op jit(solution)/shard_map/ppermute | solution.py:22
  30.9 43.2 %collective-permute-start.6 = (bf16[1024,384]{1,0:T(8,128)(2,1)}, bf16[1024,384]{1,0:T(8,128)(2,1)}, u32[]{:S(2)}, u32[]{:S(2)}) collective-permute-start(bf16[1024,384]{1,0:T(8,128)(2,1)} %bitcast.37), channel_id=1, source_target_pairs={{0,8},{2,10},{4,12},{6,14},{8,0},{10,2},{12,4},{14,6},{16,24},{18,... | collective-permute-start | bytes 2359304 | tf_op jit(solution)/shard_map/ppermute | solution.py:22
  42.7 18.4 %collective-permute-start.7 = (bf16[128,2048]{1,0:T(8,128)(2,1)}, bf16[128,2048]{1,0:T(8,128)(2,1)}, u32[]{:S(2)}, u32[]{:S(2)}) collective-permute-start(bf16[128,2048]{1,0:T(8,128)(2,1)} %copy-done.6), channel_id=1, source_target_pairs={{0,4},{2,6},{4,0},{6,2},{8,12},{10,14},{12,8},{14,10},{16,20},{18,... | collective-permute-start | bytes 1572872 | tf_op jit(solution)/shard_map/ppermute | solution.py:22
  43.4 17.7 %collective-permute-start.4 = (bf16[136,2048]{1,0:T(8,128)(2,1)}, bf16[136,2048]{1,0:T(8,128)(2,1)}, u32[]{:S(2)}, u32[]{:S(2)}) collective-permute-start(bf16[136,2048]{1,0:T(8,128)(2,1)} %copy-done.8), channel_id=1, source_target_pairs={{0,2},{2,0},{4,6},{6,4},{8,10},{10,8},{12,14},{14,12},{16,18},{18,... | collective-permute-start | bytes 1671176 | tf_op jit(solution)/shard_map/ppermute | solution.py:22
  61.0 13.1 %copy-start = (bf16[1024,768]{1,0:T(8,128)(2,1)S(1)}, bf16[1024,768]{1,0:T(8,128)(2,1)}, u32[]{:S(2)}) copy-start(bf16[1024,768]{1,0:T(8,128)(2,1)} %constant_dynamic-update-slice_fusion.1) | copy-start | bytes 4718596
  61.0 14.4 %copy-start.9 = (bf16[136,2048]{1,0:T(8,128)(2,1)S(1)}, bf16[136,2048]{1,0:T(8,128)(2,1)}, u32[]{:S(2)}) copy-start(bf16[136,2048]{1,0:T(8,128)(2,1)} %copy-done.8) | copy-start | bytes 1671172
  61.1 16.1 %copy-start.7 = (bf16[128,2048]{1,0:T(8,128)(2,1)S(1)}, bf16[128,2048]{1,0:T(8,128)(2,1)}, u32[]{:S(2)}) copy-start(bf16[128,2048]{1,0:T(8,128)(2,1)} %copy-done.6) | copy-start | bytes 1572868
  61.2 24.7 %collective-permute-start.9 = (bf16[264,2048]{1,0:T(8,128)(2,1)S(1)}, bf16[264,2048]{1,0:T(8,128)(2,1)S(1)}, u32[]{:S(2)}, u32[]{:S(2)}) collective-permute-start(bf16[264,2048]{1,0:T(8,128)(2,1)S(1)} %fusion.1), channel_id=1, source_target_pairs={{0,4},{2,6},{4,0},{6,2},{8,12},{10,14},{12,8},{14,10},{16,20},{18,... | collective-permute-start | bytes 3244040 | tf_op jit(solution)/shard_map/ppermute | solution.py:22
  62.8 24.4 %collective-permute-start.8 = (bf16[264,2048]{1,0:T(8,128)(2,1)S(1)}, bf16[264,2048]{1,0:T(8,128)(2,1)S(1)}, u32[]{:S(2)}, u32[]{:S(2)}) collective-permute-start(bf16[264,2048]{1,0:T(8,128)(2,1)S(1)} %fusion.1), channel_id=1, source_target_pairs={{0,2},{2,0},{4,6},{6,4},{8,10},{10,8},{12,14},{14,12},{16,18},{18,... | collective-permute-start | bytes 3244040 | tf_op jit(solution)/shard_map/ppermute | solution.py:22
  79.8 1.1 copy-start.5
  80.9 17.7 %collective-permute-start.12 = (bf16[1024,384]{1,0:T(8,128)(2,1)S(1)}, bf16[1024,384]{1,0:T(8,128)(2,1)S(1)}, u32[]{:S(2)}, u32[]{:S(2)}) collective-permute-start(bf16[1024,384]{1,0:T(8,128)(2,1)S(1)} %bitcast.43), channel_id=1, source_target_pairs={{0,8},{2,10},{4,12},{6,14},{8,0},{10,2},{12,4},{14,6},{16,24},{18,... | collective-permute-start | bytes 2359304 | tf_op jit(solution)/shard_map/ppermute | solution.py:22
  87.4 11.6 %collective-permute-start.10 = (bf16[128,2048]{1,0:T(8,128)(2,1)S(1)}, bf16[128,2048]{1,0:T(8,128)(2,1)S(1)}, u32[]{:S(2)}, u32[]{:S(2)}) collective-permute-start(bf16[128,2048]{1,0:T(8,128)(2,1)S(1)} %get-tuple-element.113), channel_id=1, source_target_pairs={{0,4},{2,6},{4,0},{6,2},{8,12},{10,14},{12,8},{14,10},{16,20},{18,... | collective-permute-start | bytes 1572872 | tf_op jit(solution)/shard_map/ppermute | solution.py:22
  87.9 12.1 %collective-permute-start.11 = (bf16[136,2048]{1,0:T(8,128)(2,1)S(1)}, bf16[136,2048]{1,0:T(8,128)(2,1)S(1)}, u32[]{:S(2)}, u32[]{:S(2)}) collective-permute-start(bf16[136,2048]{1,0:T(8,128)(2,1)S(1)} %slice.239), channel_id=1, source_target_pairs={{0,2},{2,0},{4,6},{6,4},{8,10},{10,8},{12,14},{14,12},{16,18},{18,... | collective-permute-start | bytes 1671176 | tf_op jit(solution)/shard_map/ppermute | solution.py:22
  89.5 12.0 %collective-permute-start.14 = (bf16[1024,768]{1,0:T(8,128)(2,1)S(1)}, bf16[1024,768]{1,0:T(8,128)(2,1)S(1)}, u32[]{:S(2)}, u32[]{:S(2)}) collective-permute-start(bf16[1024,768]{1,0:T(8,128)(2,1)S(1)} %constant_dynamic-update-slice_fusion), channel_id=1, source_target_pairs={{0,1},{1,0},{2,3},{3,2},{4,5},{5,4},{6,7},{7,6},{8,9},{9,8},{10,11... | collective-permute-start | bytes 4718600 | tf_op jit(solution)/shard_map/ppermute | solution.py:20
  99.0 2.3 %collective-permute-start.13 = (bf16[1024,384]{1,0:T(8,128)(2,1)S(1)}, bf16[1024,384]{1,0:T(8,128)(2,1)S(1)}, u32[]{:S(2)}, u32[]{:S(2)}) collective-permute-start(bf16[1024,384]{1,0:T(8,128)(2,1)S(1)} %collective-permute-done.12), channel_id=1, source_target_pairs={{0,1},{1,0},{2,3},{3,2},{4,5},{5,4},{6,7},{7,6},{8,9},{9,8},{10,11... | collective-permute-start | bytes 2359304 | tf_op jit(solution)/shard_map/ppermute | solution.py:20
  111.8 1.1 copy-start.1
  111.8 1.4 copy-start.2
  112.2 4.7 %collective-permute-start.15 = (bf16[1024,1152]{1,0:T(8,128)(2,1)S(1)}, bf16[1024,1152]{1,0:T(8,128)(2,1)S(1)}, u32[]{:S(2)}, u32[]{:S(2)}) collective-permute-start(bf16[1024,1152]{1,0:T(8,128)(2,1)S(1)} %pad_maximum_fusion.1), channel_id=1, source_target_pairs={{0,1},{1,0},{2,3},{3,2},{4,5},{5,4},{6,7},{7,6},{8,9},{9,8},{10,11... | collective-permute-start | bytes 7077896 | tf_op jit(solution)/shard_map/ppermute | solution.py:20
  117.4 4.8 %collective-permute-start.16 = (bf16[1024,768]{1,0:T(8,128)(2,1)S(1)}, bf16[1024,768]{1,0:T(8,128)(2,1)S(1)}, u32[]{:S(2)}, u32[]{:S(2)}) collective-permute-start(bf16[1024,768]{1,0:T(8,128)(2,1)S(1)} %pad_maximum_fusion.8), channel_id=1, source_target_pairs={{0,1},{1,0},{2,3},{3,2},{4,5},{5,4},{6,7},{7,6},{8,9},{9,8},{10,11... | collective-permute-start | bytes 4718600 | tf_op jit(solution)/shard_map/ppermute | solution.py:20
  117.6 4.4 %collective-permute-start.17 = (bf16[1024,384]{1,0:T(8,128)(2,1)S(1)}, bf16[1024,384]{1,0:T(8,128)(2,1)S(1)}, u32[]{:S(2)}, u32[]{:S(2)}) collective-permute-start(bf16[1024,384]{1,0:T(8,128)(2,1)S(1)} %bitcast.44), channel_id=1, source_target_pairs={{0,1},{1,0},{2,3},{3,2},{4,5},{5,4},{6,7},{7,6},{8,9},{9,8},{10,11... | collective-permute-start | bytes 2359304 | tf_op jit(solution)/shard_map/ppermute | solution.py:20
  118.2 64.6 %collective-permute-start.27 = (bf16[1024,1152]{1,0:T(8,128)(2,1)S(1)}, bf16[1024,1152]{1,0:T(8,128)(2,1)S(1)}, u32[]{:S(2)}, u32[]{:S(2)}) collective-permute-start(bf16[1024,1152]{1,0:T(8,128)(2,1)S(1)} %fusion), channel_id=1, source_target_pairs={{0,8},{2,10},{4,12},{6,14},{8,0},{10,2},{12,4},{14,6},{16,24},{18,... | collective-permute-start | bytes 7077896 | tf_op jit(solution)/shard_map/ppermute | solution.py:22
  130.2 14.3 %collective-permute-start.19 = (bf16[128,2048]{1,0:T(8,128)(2,1)S(1)}, bf16[128,2048]{1,0:T(8,128)(2,1)S(1)}, u32[]{:S(2)}, u32[]{:S(2)}) collective-permute-start(bf16[128,2048]{1,0:T(8,128)(2,1)S(1)} %pad_maximum_fusion.14), channel_id=1, source_target_pairs={{0,2},{2,0},{4,6},{6,4},{8,10},{10,8},{12,14},{14,12},{16,18},{18,... | collective-permute-start | bytes 1572872 | tf_op jit(solution)/shard_map/ppermute | solution.py:22
  131.8 13.7 %collective-permute-start.18 = (bf16[128,2048]{1,0:T(8,128)(2,1)S(1)}, bf16[128,2048]{1,0:T(8,128)(2,1)S(1)}, u32[]{:S(2)}, u32[]{:S(2)}) collective-permute-start(bf16[128,2048]{1,0:T(8,128)(2,1)S(1)} %pad_maximum_fusion.15), channel_id=1, source_target_pairs={{0,4},{2,6},{4,0},{6,2},{8,12},{10,14},{12,8},{14,10},{16,20},{18,... | collective-permute-start | bytes 1572872 | tf_op jit(solution)/shard_map/ppermute | solution.py:22
  145.6 9.3 %collective-permute-start.24 = (bf16[64,2048]{1,0:T(8,128)(2,1)S(1)}, bf16[64,2048]{1,0:T(8,128)(2,1)S(1)}, u32[]{:S(2)}, u32[]{:S(2)}) collective-permute-start(bf16[64,2048]{1,0:T(8,128)(2,1)S(1)} %get-tuple-element.100), channel_id=1, source_target_pairs={{0,2},{2,0},{4,6},{6,4},{8,10},{10,8},{12,14},{14,12},{16,18},{18,... | collective-permute-start | bytes 786440 | tf_op jit(solution)/shard_map/ppermute | solution.py:22
  146.2 9.2 %collective-permute-start.25 = (bf16[64,2048]{1,0:T(8,128)(2,1)S(1)}, bf16[64,2048]{1,0:T(8,128)(2,1)S(1)}, u32[]{:S(2)}, u32[]{:S(2)}) collective-permute-start(bf16[64,2048]{1,0:T(8,128)(2,1)S(1)} %get-tuple-element.101), channel_id=1, source_target_pairs={{0,4},{2,6},{4,0},{6,2},{8,12},{10,14},{12,8},{14,10},{16,20},{18,... | collective-permute-start | bytes 786440 | tf_op jit(solution)/shard_map/ppermute | solution.py:22
  147.6 16.5 %collective-permute-start.21 = (bf16[128,2048]{1,0:T(8,128)(2,1)S(1)}, bf16[128,2048]{1,0:T(8,128)(2,1)S(1)}, u32[]{:S(2)}, u32[]{:S(2)}) collective-permute-start(bf16[128,2048]{1,0:T(8,128)(2,1)S(1)} %pad_maximum_fusion.17), channel_id=1, source_target_pairs={{0,2},{2,0},{4,6},{6,4},{8,10},{10,8},{12,14},{14,12},{16,18},{18,... | collective-permute-start | bytes 1572872 | tf_op jit(solution)/shard_map/ppermute | solution.py:22
  149.2 15.2 %collective-permute-start.20 = (bf16[128,2048]{1,0:T(8,128)(2,1)S(1)}, bf16[128,2048]{1,0:T(8,128)(2,1)S(1)}, u32[]{:S(2)}, u32[]{:S(2)}) collective-permute-start(bf16[128,2048]{1,0:T(8,128)(2,1)S(1)} %pad_maximum_fusion.16), channel_id=1, source_target_pairs={{0,4},{2,6},{4,0},{6,2},{8,12},{10,14},{12,8},{14,10},{16,20},{18,... | collective-permute-start | bytes 1572872 | tf_op jit(solution)/shard_map/ppermute | solution.py:22
  155.7 27.1 %collective-permute-start.26 = (bf16[128,2048]{1,0:T(8,128)(2,1)S(1)}, bf16[128,2048]{1,0:T(8,128)(2,1)S(1)}, u32[]{:S(2)}, u32[]{:S(2)}) collective-permute-start(bf16[128,2048]{1,0:T(8,128)(2,1)S(1)} %add_convert_fusion.5), channel_id=1, source_target_pairs={{0,16},{2,18},{4,20},{6,22},{8,24},{10,26},{12,28},{14,30},{16,0},... | collective-permute-start | bytes 1572872 | tf_op jit(solution)/shard_map/ppermute | solution.py:22
  160.6 23.5 %collective-permute-start.28 = (bf16[1024,1152]{1,0:T(8,128)(2,1)S(1)}, bf16[1024,1152]{1,0:T(8,128)(2,1)S(1)}, u32[]{:S(2)}, u32[]{:S(2)}) collective-permute-start(bf16[1024,1152]{1,0:T(8,128)(2,1)S(1)} %pad_maximum_fusion.2), channel_id=1, source_target_pairs={{0,1},{1,0},{2,3},{3,2},{4,5},{5,4},{6,7},{7,6},{8,9},{9,8},{10,11... | collective-permute-start | bytes 7077896 | tf_op jit(solution)/shard_map/ppermute | solution.py:20
  164.5 18.3 %collective-permute-start.22 = (bf16[64,2048]{1,0:T(8,128)(2,1)S(1)}, bf16[64,2048]{1,0:T(8,128)(2,1)S(1)}, u32[]{:S(2)}, u32[]{:S(2)}) collective-permute-start(bf16[64,2048]{1,0:T(8,128)(2,1)S(1)} %get-tuple-element.94), channel_id=1, source_target_pairs={{0,2},{2,0},{4,6},{6,4},{8,10},{10,8},{12,14},{14,12},{16,18},{18,... | collective-permute-start | bytes 786440 | tf_op jit(solution)/shard_map/ppermute | solution.py:22
  166.1 16.8 %collective-permute-start.23 = (bf16[64,2048]{1,0:T(8,128)(2,1)S(1)}, bf16[64,2048]{1,0:T(8,128)(2,1)S(1)}, u32[]{:S(2)}, u32[]{:S(2)}) collective-permute-start(bf16[64,2048]{1,0:T(8,128)(2,1)S(1)} %get-tuple-element.95), channel_id=1, source_target_pairs={{0,4},{2,6},{4,0},{6,2},{8,12},{10,14},{12,8},{14,10},{16,20},{18,... | collective-permute-start | bytes 786440 | tf_op jit(solution)/shard_map/ppermute | solution.py:22

commit v5 on v4

--- a/solution.py
+++ b/solution.py
@@ -162,11 +162,11 @@
     both_mine = jnp.concatenate([gate_mine, up_mine], axis=1)
     x_own = turn(tokens)
     g_own = jnp.concatenate([turn(out_grad), gate_rows(gates, expert_ids, experts)], axis=0)
-    far = swap_far(jnp.concatenate([x_own, g_own], axis=0), ACROSS_Z)
+    x_x = swap(x_own, ACROSS_X)
+    g_y = swap(g_own, ACROSS_Y)
     gate_pair, up_pair = swap(gate_mine, PAIR), swap(up_mine, PAIR)
     both_pair = jnp.concatenate([gate_pair, up_pair], axis=1)
-    x_x = swap(x_own, ACROSS_X)
-    g_y = swap(g_own, ACROSS_Y)
+    far = swap_far(jnp.concatenate([x_own, g_own], axis=0), ACROSS_Z)
     g_x = swap(after(g_own, x_x, g_y), ACROSS_X)
     x_y = swap(after(x_own, x_x, g_y), ACROSS_Y)
     g_y, x_x = after((g_y, x_x), g_x, x_y)

time: 187 us -> 187 us (level)
  no operation moved by 1% of the time
where the time goes in v5:
time: 187 us
  waiting for transfers between devices  87.1 us (47%)
  starting transfers between devices  34.9 us (19%)
  matrix products  27.6 us (15%)
  local copies, waits for them, and re-layouts  13.8 us (7%)
  Pallas kernels  11.2 us (6%)
  other arithmetic  10.8 us (6%)
    ppermute x23, waiting for transfers between devices, swap(): return lax.ppermute(rows, 'expert', [(i, i ^ bit) for i in range(experts)])  77.4 us
    ppermute x23, starting transfers between devices, swap(): return lax.ppermute(rows, 'expert', [(i, i ^ bit) for i in range(experts)])  28.8 us
    dot_general x24, matrix products, dot(): return lax.dot_general(a, b, dims, preferred_element_type=wide)  27.6 us
    pallas_call x2, Pallas kernels, dx_rows(): pl.pallas_call(dx_kernel, grid=(width // tile,), in_specs=[whole, whole,...  8.59 us
    all_to_all x1, waiting for transfers between devices, swap_far(): lax.all_to_all(jnp.stack([rows, rows]), 'expert', split_axis=0, concat_ax...  6.28 us
    all_to_all x1, starting transfers between devices, swap_far(): lax.all_to_all(jnp.stack([rows, rows]), 'expert', split_axis=0, concat_ax...  5.3 us
    unnamed x23, local copies, waits for them, and re-layouts  4.72 us
  transfers between devices with their start and end apart: 30, of which 18 were waited for; matrix products, arithmetic and copies ran while one was open for 18% of the time, Pallas kernels for 5%

profile of v5, /device:TPU:0, one launch (start us, length us, event | category | flops | bytes accessed | tf_op | source)
XLA Modules:
  0.0 186.8 jit_solution(272768505743768839)
XLA Ops:
  0.7 0.8 select_reduce_fusion
  1.5 1.1 fusion.39
  2.6 1.1 fusion.38
  4.3 1.6 pad_maximum_fusion.3
  5.9 5.3 %all-to-all-start = ((bf16[2,264,2048]{2,1,0:T(8,128)(2,1)}), bf16[2,264,2048]{2,1,0:T(8,128)(2,1)S(1)}, u32[]{:S(2)}, u32[]{:S(2)}) async-start(bf16[2,264,2048]{2,1,0:T(8,128)(2,1)} %pad_maximum_fusion.3), calls=%async_computation | async-start | bytes 4325376 | tf_op jit(solution)/shard_map/all_to_all | solution.py:28
  11.2 2.1 %concatenate.108 = bf16[136,2048]{1,0:T(8,128)(2,1)} concatenate(bf16[128,2048]{1,0:T(8,128)(2,1)S(1)} %maximum_select_fusion, bf16[1,2048]{1,0:T(2,128)(2,1)S(1)} %get-tuple-element.124, bf16[1,2048]{1,0:T(2,128)(2,1)S(1)} %get-tuple-element.123, bf16[1,2048]{1,0:T(2,128)(2,1)S(1)} %get-tuple-element.122, bf16[5,2048]{1,0:T(8,128)(2,1)S(1)} %broadcast_in_dim.22), dimensions={0} | concatenate | bytes 1114112 | tf_op jit(solution)/shard_map/concatenate | solution.py:164
  13.2 1.5 collective-permute-start.1
  14.8 1.5 collective-permute-start
  16.3 1.6 collective-permute-start.5
  17.8 10.3 %collective-permute-done = bf16[128,2048]{1,0:T(8,128)(2,1)S(1)} collective-permute-done((bf16[128,2048]{1,0:T(8,128)(2,1)S(1)}, bf16[128,2048]{1,0:T(8,128)(2,1)S(1)}, u32[]{:S(2)}, u32[]{:S(2)}) %collective-permute-start) | collective-permute-done | bytes 524320 | tf_op jit(solution)/shard_map/ppermute | solution.py:22
  28.1 0.8 copy-done.6
  28.9 1.5 collective-permute-start.2
  30.9 1.6 collective-permute-start.6
  33.2 9.5 %collective-permute-done.3 = bf16[128,2048]{1,0:T(8,128)(2,1)} collective-permute-done((bf16[128,2048]{1,0:T(8,128)(2,1)S(1)}, bf16[128,2048]{1,0:T(8,128)(2,1)}, u32[]{:S(2)}, u32[]{:S(2)}) %collective-permute-start.3) | collective-permute-done | bytes 524320 | tf_op jit(solution)/shard_map/ppermute | solution.py:22
  43.4 1.2 collective-permute-start.4
  44.6 8.0 %collective-permute-done.5 = bf16[1024,384]{1,0:T(8,128)(2,1)} collective-permute-done((bf16[1024,384]{1,0:T(8,128)(2,1)}, bf16[1024,384]{1,0:T(8,128)(2,1)}, u32[]{:S(2)}, u32[]{:S(2)}) %collective-permute-start.5) | collective-permute-done | bytes 786464 | tf_op jit(solution)/shard_map/ppermute | solution.py:22
  52.7 2.1 %constant_dynamic-update-slice_fusion.1 = bf16[1024,768]{1,0:T(8,128)(2,1)} fusion(bf16[1024,384]{1,0:T(8,128)(2,1)} %collective-permute-done.5), kind=kLoop, calls=%fused_computation.89 | loop fusion | bytes 1572864
  54.7 6.3 %all-to-all-done = bf16[2,264,2048]{2,1,0:T(8,128)(2,1)S(1)} async-done(((bf16[2,264,2048]{2,1,0:T(8,128)(2,1)}), bf16[2,264,2048]{2,1,0:T(8,128)(2,1)S(1)}, u32[]{:S(2)}, u32[]{:S(2)}) %all-to-all-start) | async-done | bytes 2162720 | tf_op jit(solution)/shard_map/all_to_all | solution.py:28
  61.2 1.6 collective-permute-start.9
  62.8 1.5 collective-permute-start.8
  64.3 9.8 %collective-permute-done.6 = bf16[1024,384]{1,0:T(8,128)(2,1)} collective-permute-done((bf16[1024,384]{1,0:T(8,128)(2,1)}, bf16[1024,384]{1,0:T(8,128)(2,1)}, u32[]{:S(2)}, u32[]{:S(2)}) %collective-permute-start.6) | collective-permute-done | bytes 786464 | tf_op jit(solution)/shard_map/ppermute | solution.py:22
  74.1 1.3 constant_dynamic-update-slice_fusion
  75.5 1.1 slice.293
  77.3 1.4 pad_maximum_fusion.4
  78.7 1.1 slice.233
  80.1 0.8 copy-done.5
  81.1 4.8 %collective-permute-done.9 = bf16[264,2048]{1,0:T(8,128)(2,1)S(1)} collective-permute-done((bf16[264,2048]{1,0:T(8,128)(2,1)S(1)}, bf16[264,2048]{1,0:T(8,128)(2,1)S(1)}, u32[]{:S(2)}, u32[]{:S(2)}) %collective-permute-start.9) | collective-permute-done | bytes 1081376 | tf_op jit(solution)/shard_map/ppermute | solution.py:22
  85.9 1.4 collective-permute-done.8
  87.9 1.6 collective-permute-start.11
  89.8 8.9 %collective-permute-done.12 = bf16[1024,384]{1,0:T(8,128)(2,1)S(1)} collective-permute-done((bf16[1024,384]{1,0:T(8,128)(2,1)S(1)}, bf16[1024,384]{1,0:T(8,128)(2,1)S(1)}, u32[]{:S(2)}, u32[]{:S(2)}) %collective-permute-start.12) | collective-permute-done | bytes 786464 | tf_op jit(solution)/shard_map/ppermute | solution.py:22
  101.6 1.8 fusion.40
  103.4 1.8 fusion.41
  105.2 1.5 multiply_convert_fusion.11
  107.4 1.5 multiply_convert_fusion.9
  109.0 0.8 add_convert_fusion.3
  109.7 1.0 fusion.18
  110.8 1.1 add_convert_fusion.1
  114.1 1.0 fusion.24
  115.9 1.1 convolution_add_fusion.1
  118.9 3.1 %collective-permute-done.17 = bf16[1024,384]{1,0:T(8,128)(2,1)S(1)} collective-permute-done((bf16[1024,384]{1,0:T(8,128)(2,1)S(1)}, bf16[1024,384]{1,0:T(8,128)(2,1)S(1)}, u32[]{:S(2)}, u32[]{:S(2)}) %collective-permute-start.17) | collective-permute-done | bytes 786464 | tf_op jit(solution)/shard_map/ppermute | solution.py:20
  122.5 1.8 fusion.42
  124.2 1.5 multiply_convert_fusion.5
  125.8 4.2 %shard_map.102 = bf16[512,2048]{1,0:T(8,128)(2,1)S(1)} custom-call(bf16[512,768]{1,0:T(8,128)(2,1)S(1)} %pad_maximum_fusion.12.act_a, bf16[512,768]{1,0:T(8,128)(2,1)S(1)} %pad_maximum_fusion.11.act_b, bf16[2048,768]{1,0:T(8,128)(2,1)S(1)} %pad_maximum_fusion.w_a, bf16[2048,768]{1,0:T(8,128)(2,1)S(1)} %constant_dynamic-update-slice_fusion.4.w_b), custom_call_target="tpu_custom_call" | custom-call | flops 3221225472 | bytes 8388608 | tf_op jit(solution)/shard_map/pallas_call | solution.py:105
  130.2 1.6 collective-permute-start.19
  131.8 1.3 collective-permute-start.18
  133.0 1.8 fusion.43
  134.8 1.5 multiply_convert_fusion.3
  136.5 1.0 fusion.12
  138.2 4.4 %shard_map.103 = bf16[512,2048]{1,0:T(8,128)(2,1)S(1)} custom-call(bf16[512,768]{1,0:T(8,128)(2,1)S(1)} %pad_maximum_fusion.13.act_a, bf16[512,768]{1,0:T(8,128)(2,1)S(1)} %pad_maximum_fusion.10.act_b, bf16[2048,768]{1,0:T(8,128)(2,1)S(1)} %pad_maximum_fusion.w_a, bf16[2048,768]{1,0:T(8,128)(2,1)S(1)} %constant_dynamic-update-slice_fusion.4.w_b), custom_call_target="tpu_custom_call" | custom-call | flops 3221225472 | bytes 8388608 | tf_op jit(solution)/shard_map/pallas_call | solution.py:105
  143.4 1.0 fusion.6
  144.5 1.1 collective-permute-done.18
  146.2 1.2 collective-permute-start.25
  147.6 1.5 collective-permute-start.21
  149.2 0.9 collective-permute-start.20
  150.2 4.8 %collective-permute-done.24 = bf16[64,2048]{1,0:T(8,128)(2,1)S(1)} collective-permute-done((bf16[64,2048]{1,0:T(8,128)(2,1)S(1)}, bf16[64,2048]{1,0:T(8,128)(2,1)S(1)}, u32[]{:S(2)}, u32[]{:S(2)}) %collective-permute-start.24) | collective-permute-done | bytes 262176 | tf_op jit(solution)/shard_map/ppermute | solution.py:22
  155.7 2.9 %collective-permute-start.26 = (bf16[128,2048]{1,0:T(8,128)(2,1)S(1)}, bf16[128,2048]{1,0:T(8,128)(2,1)S(1)}, u32[]{:S(2)}, u32[]{:S(2)}) collective-permute-start(bf16[128,2048]{1,0:T(8,128)(2,1)S(1)} %add_convert_fusion.5), channel_id=1, source_target_pairs={{0,16},{2,18},{4,20},{6,22},{8,24},{10,26},{12,28},{14,30},{16,0},... | collective-permute-start | bytes 1572872 | tf_op jit(solution)/shard_map/ppermute | solution.py:22
  159.4 1.0 add_convert_fusion
  160.7 1.1 convolution_add_fusion.both
  161.8 2.3 %collective-permute-done.21 = bf16[128,2048]{1,0:T(8,128)(2,1)S(1)} collective-permute-done((bf16[128,2048]{1,0:T(8,128)(2,1)S(1)}, bf16[128,2048]{1,0:T(8,128)(2,1)S(1)}, u32[]{:S(2)}, u32[]{:S(2)}) %collective-permute-start.21) | collective-permute-done | bytes 524320 | tf_op jit(solution)/shard_map/ppermute | solution.py:22
  164.5 1.5 collective-permute-start.22
  166.1 1.2 collective-permute-start.23
  168.0 14.7 %collective-permute-done.27.more = bf16[1024,1152]{1,0:T(8,128)(2,1)S(1)} collective-permute-done((bf16[1024,1152]{1,0:T(8,128)(2,1)S(1)}, bf16[1024,1152]{1,0:T(8,128)(2,1)S(1)}, u32[]{:S(2)}, u32[]{:S(2)}) %collective-permute-start.27) | collective-permute-done | bytes 2359328 | tf_op jit(solution)/shard_map/ppermute | solution.py:22
  183.2 0.9 maximum_select_fusion.2
  184.2 2.7 %shard_map.104 = (f32[1024,384]{1,0:T(8,128)}, f32[1024,384]{1,0:T(8,128)}, f32[1024,384]{1,0:T(8,128)}) custom-call(f32[1024,768]{1,0:T(8,128)S(1)} %convolution_add_fusion.both, f32[1024,384]{1,0:T(8,128)S(1)} %convolution_add_fusion.2.down, bf16[1024,1152]{1,0:T(8,128)(2,1)S(1)} %collective-permute-done.28.got, ...), custom_call_target="tpu_custom_call" | custom-call | flops 20000000000 | tf_op jit(solution)/shard_map/pallas_call | solution.py:131
  (112 shorter events, 19.8 us)
Async XLA Ops:
  0.6 3.0 %copy-start.3 = (bf16[128,2048]{1,0:T(8,128)(2,1)S(1)}, bf16[128,2048]{1,0:T(8,128)(2,1)}, u32[]{:S(2)}) copy-start(bf16[128,2048]{1,0:T(8,128)(2,1)} %param.7) | copy-start | bytes 1572868
  0.6 3.2 %copy-start.4 = (bf16[128,2048]{1,0:T(8,128)(2,1)S(1)}, bf16[128,2048]{1,0:T(8,128)(2,1)}, u32[]{:S(2)}) copy-start(bf16[128,2048]{1,0:T(8,128)(2,1)} %param.8) | copy-start | bytes 1572868
  5.9 55.1 %all-to-all-start = ((bf16[2,264,2048]{2,1,0:T(8,128)(2,1)}), bf16[2,264,2048]{2,1,0:T(8,128)(2,1)S(1)}, u32[]{:S(2)}, u32[]{:S(2)}) async-start(bf16[2,264,2048]{2,1,0:T(8,128)(2,1)} %pad_maximum_fusion.3), calls=%async_computation | async-start | bytes 4325376 | tf_op jit(solution)/shard_map/all_to_all | solution.py:28
  13.2 14.8 %collective-permute-start.1 = (bf16[136,2048]{1,0:T(8,128)(2,1)}, bf16[136,2048]{1,0:T(8,128)(2,1)S(1)}, u32[]{:S(2)}, u32[]{:S(2)}) collective-permute-start(bf16[136,2048]{1,0:T(8,128)(2,1)} %concatenate.108), channel_id=1, source_target_pairs={{0,4},{2,6},{4,0},{6,2},{8,12},{10,14},{12,8},{14,10},{16,20},{18,... | collective-permute-start | bytes 1671176 | tf_op jit(solution)/shard_map/ppermute | solution.py:22
  14.8 13.3 %collective-permute-start = (bf16[128,2048]{1,0:T(8,128)(2,1)S(1)}, bf16[128,2048]{1,0:T(8,128)(2,1)S(1)}, u32[]{:S(2)}, u32[]{:S(2)}) collective-permute-start(bf16[128,2048]{1,0:T(8,128)(2,1)S(1)} %maximum_select_fusion.1), channel_id=1, source_target_pairs={{0,2},{2,0},{4,6},{6,4},{8,10},{10,8},{12,14},{14,12},{16,18},{18,... | collective-permute-start | bytes 1572872 | tf_op jit(solution)/shard_map/ppermute | solution.py:22
  16.3 36.4 %collective-permute-start.5 = (bf16[1024,384]{1,0:T(8,128)(2,1)}, bf16[1024,384]{1,0:T(8,128)(2,1)}, u32[]{:S(2)}, u32[]{:S(2)}) collective-permute-start(bf16[1024,384]{1,0:T(8,128)(2,1)} %bitcast.40), channel_id=1, source_target_pairs={{0,8},{2,10},{4,12},{6,14},{8,0},{10,2},{12,4},{14,6},{16,24},{18,... | collective-permute-start | bytes 2359304 | tf_op jit(solution)/shard_map/ppermute | solution.py:22
  28.1 0.8 copy-start.6
  28.9 1.5 copy-start.8
  28.9 13.8 %collective-permute-start.2 = (bf16[136,2048]{1,0:T(8,128)(2,1)}, bf16[136,2048]{1,0:T(8,128)(2,1)}, u32[]{:S(2)}, u32[]{:S(2)}) collective-permute-start(bf16[136,2048]{1,0:T(8,128)(2,1)} %concatenate.108), channel_id=1, source_target_pairs={{0,2},{2,0},{4,6},{6,4},{8,10},{10,8},{12,14},{14,12},{16,18},{18,... | collective-permute-start | bytes 1671176 | tf_op jit(solution)/shard_map/ppermute | solution.py:22
  30.4 12.3 %collective-permute-start.3 = (bf16[128,2048]{1,0:T(8,128)(2,1)S(1)}, bf16[128,2048]{1,0:T(8,128)(2,1)}, u32[]{:S(2)}, u32[]{:S(2)}) collective-permute-start(bf16[128,2048]{1,0:T(8,128)(2,1)S(1)} %maximum_select_fusion.1), channel_id=1, source_target_pairs={{0,4},{2,6},{4,0},{6,2},{8,12},{10,14},{12,8},{14,10},{16,20},{18,... | collective-permute-start | bytes 1572872 | tf_op jit(solution)/shard_map/ppermute | solution.py:22
  30.9 43.2 %collective-permute-start.6 = (bf16[1024,384]{1,0:T(8,128)(2,1)}, bf16[1024,384]{1,0:T(8,128)(2,1)}, u32[]{:S(2)}, u32[]{:S(2)}) collective-permute-start(bf16[1024,384]{1,0:T(8,128)(2,1)} %bitcast.37), channel_id=1, source_target_pairs={{0,8},{2,10},{4,12},{6,14},{8,0},{10,2},{12,4},{14,6},{16,24},{18,... | collective-permute-start | bytes 2359304 | tf_op jit(solution)/shard_map/ppermute | solution.py:22
  42.7 18.4 %collective-permute-start.7 = (bf16[128,2048]{1,0:T(8,128)(2,1)}, bf16[128,2048]{1,0:T(8,128)(2,1)}, u32[]{:S(2)}, u32[]{:S(2)}) collective-permute-start(bf16[128,2048]{1,0:T(8,128)(2,1)} %copy-done.6), channel_id=1, source_target_pairs={{0,4},{2,6},{4,0},{6,2},{8,12},{10,14},{12,8},{14,10},{16,20},{18,... | collective-permute-start | bytes 1572872 | tf_op jit(solution)/shard_map/ppermute | solution.py:22
  43.4 17.7 %collective-permute-start.4 = (bf16[136,2048]{1,0:T(8,128)(2,1)}, bf16[136,2048]{1,0:T(8,128)(2,1)}, u32[]{:S(2)}, u32[]{:S(2)}) collective-permute-start(bf16[136,2048]{1,0:T(8,128)(2,1)} %copy-done.8), channel_id=1, source_target_pairs={{0,2},{2,0},{4,6},{6,4},{8,10},{10,8},{12,14},{14,12},{16,18},{18,... | collective-permute-start | bytes 1671176 | tf_op jit(solution)/shard_map/ppermute | solution.py:22
  61.0 13.1 %copy-start = (bf16[1024,768]{1,0:T(8,128)(2,1)S(1)}, bf16[1024,768]{1,0:T(8,128)(2,1)}, u32[]{:S(2)}) copy-start(bf16[1024,768]{1,0:T(8,128)(2,1)} %constant_dynamic-update-slice_fusion.1) | copy-start | bytes 4718596
  61.0 14.4 %copy-start.9 = (bf16[136,2048]{1,0:T(8,128)(2,1)S(1)}, bf16[136,2048]{1,0:T(8,128)(2,1)}, u32[]{:S(2)}) copy-start(bf16[136,2048]{1,0:T(8,128)(2,1)} %copy-done.8) | copy-start | bytes 1671172
  61.1 16.1 %copy-start.7 = (bf16[128,2048]{1,0:T(8,128)(2,1)S(1)}, bf16[128,2048]{1,0:T(8,128)(2,1)}, u32[]{:S(2)}) copy-start(bf16[128,2048]{1,0:T(8,128)(2,1)} %copy-done.6) | copy-start | bytes 1572868
  61.2 24.7 %collective-permute-start.9 = (bf16[264,2048]{1,0:T(8,128)(2,1)S(1)}, bf16[264,2048]{1,0:T(8,128)(2,1)S(1)}, u32[]{:S(2)}, u32[]{:S(2)}) collective-permute-start(bf16[264,2048]{1,0:T(8,128)(2,1)S(1)} %fusion.1), channel_id=1, source_target_pairs={{0,4},{2,6},{4,0},{6,2},{8,12},{10,14},{12,8},{14,10},{16,20},{18,... | collective-permute-start | bytes 3244040 | tf_op jit(solution)/shard_map/ppermute | solution.py:22
  62.8 24.4 %collective-permute-start.8 = (bf16[264,2048]{1,0:T(8,128)(2,1)S(1)}, bf16[264,2048]{1,0:T(8,128)(2,1)S(1)}, u32[]{:S(2)}, u32[]{:S(2)}) collective-permute-start(bf16[264,2048]{1,0:T(8,128)(2,1)S(1)} %fusion.1), channel_id=1, source_target_pairs={{0,2},{2,0},{4,6},{6,4},{8,10},{10,8},{12,14},{14,12},{16,18},{18,... | collective-permute-start | bytes 3244040 | tf_op jit(solution)/shard_map/ppermute | solution.py:22
  79.8 1.1 copy-start.5
  80.9 17.7 %collective-permute-start.12 = (bf16[1024,384]{1,0:T(8,128)(2,1)S(1)}, bf16[1024,384]{1,0:T(8,128)(2,1)S(1)}, u32[]{:S(2)}, u32[]{:S(2)}) collective-permute-start(bf16[1024,384]{1,0:T(8,128)(2,1)S(1)} %bitcast.43), channel_id=1, source_target_pairs={{0,8},{2,10},{4,12},{6,14},{8,0},{10,2},{12,4},{14,6},{16,24},{18,... | collective-permute-start | bytes 2359304 | tf_op jit(solution)/shard_map/ppermute | solution.py:22
  87.4 11.6 %collective-permute-start.10 = (bf16[128,2048]{1,0:T(8,128)(2,1)S(1)}, bf16[128,2048]{1,0:T(8,128)(2,1)S(1)}, u32[]{:S(2)}, u32[]{:S(2)}) collective-permute-start(bf16[128,2048]{1,0:T(8,128)(2,1)S(1)} %get-tuple-element.113), channel_id=1, source_target_pairs={{0,4},{2,6},{4,0},{6,2},{8,12},{10,14},{12,8},{14,10},{16,20},{18,... | collective-permute-start | bytes 1572872 | tf_op jit(solution)/shard_map/ppermute | solution.py:22
  87.9 12.1 %collective-permute-start.11 = (bf16[136,2048]{1,0:T(8,128)(2,1)S(1)}, bf16[136,2048]{1,0:T(8,128)(2,1)S(1)}, u32[]{:S(2)}, u32[]{:S(2)}) collective-permute-start(bf16[136,2048]{1,0:T(8,128)(2,1)S(1)} %slice.239), channel_id=1, source_target_pairs={{0,2},{2,0},{4,6},{6,4},{8,10},{10,8},{12,14},{14,12},{16,18},{18,... | collective-permute-start | bytes 1671176 | tf_op jit(solution)/shard_map/ppermute | solution.py:22
  89.5 12.0 %collective-permute-start.14 = (bf16[1024,768]{1,0:T(8,128)(2,1)S(1)}, bf16[1024,768]{1,0:T(8,128)(2,1)S(1)}, u32[]{:S(2)}, u32[]{:S(2)}) collective-permute-start(bf16[1024,768]{1,0:T(8,128)(2,1)S(1)} %constant_dynamic-update-slice_fusion), channel_id=1, source_target_pairs={{0,1},{1,0},{2,3},{3,2},{4,5},{5,4},{6,7},{7,6},{8,9},{9,8},{10,11... | collective-permute-start | bytes 4718600 | tf_op jit(solution)/shard_map/ppermute | solution.py:20
  99.0 2.3 %collective-permute-start.13 = (bf16[1024,384]{1,0:T(8,128)(2,1)S(1)}, bf16[1024,384]{1,0:T(8,128)(2,1)S(1)}, u32[]{:S(2)}, u32[]{:S(2)}) collective-permute-start(bf16[1024,384]{1,0:T(8,128)(2,1)S(1)} %collective-permute-done.12), channel_id=1, source_target_pairs={{0,1},{1,0},{2,3},{3,2},{4,5},{5,4},{6,7},{7,6},{8,9},{9,8},{10,11... | collective-permute-start | bytes 2359304 | tf_op jit(solution)/shard_map/ppermute | solution.py:20
  111.8 1.1 copy-start.1
  111.8 1.4 copy-start.2
  112.2 4.7 %collective-permute-start.15 = (bf16[1024,1152]{1,0:T(8,128)(2,1)S(1)}, bf16[1024,1152]{1,0:T(8,128)(2,1)S(1)}, u32[]{:S(2)}, u32[]{:S(2)}) collective-permute-start(bf16[1024,1152]{1,0:T(8,128)(2,1)S(1)} %pad_maximum_fusion.1), channel_id=1, source_target_pairs={{0,1},{1,0},{2,3},{3,2},{4,5},{5,4},{6,7},{7,6},{8,9},{9,8},{10,11... | collective-permute-start | bytes 7077896 | tf_op jit(solution)/shard_map/ppermute | solution.py:20
  117.4 4.8 %collective-permute-start.16 = (bf16[1024,768]{1,0:T(8,128)(2,1)S(1)}, bf16[1024,768]{1,0:T(8,128)(2,1)S(1)}, u32[]{:S(2)}, u32[]{:S(2)}) collective-permute-start(bf16[1024,768]{1,0:T(8,128)(2,1)S(1)} %pad_maximum_fusion.8), channel_id=1, source_target_pairs={{0,1},{1,0},{2,3},{3,2},{4,5},{5,4},{6,7},{7,6},{8,9},{9,8},{10,11... | collective-permute-start | bytes 4718600 | tf_op jit(solution)/shard_map/ppermute | solution.py:20
  117.6 4.4 %collective-permute-start.17 = (bf16[1024,384]{1,0:T(8,128)(2,1)S(1)}, bf16[1024,384]{1,0:T(8,128)(2,1)S(1)}, u32[]{:S(2)}, u32[]{:S(2)}) collective-permute-start(bf16[1024,384]{1,0:T(8,128)(2,1)S(1)} %bitcast.44), channel_id=1, source_target_pairs={{0,1},{1,0},{2,3},{3,2},{4,5},{5,4},{6,7},{7,6},{8,9},{9,8},{10,11... | collective-permute-start | bytes 2359304 | tf_op jit(solution)/shard_map/ppermute | solution.py:20
  118.2 64.6 %collective-permute-start.27 = (bf16[1024,1152]{1,0:T(8,128)(2,1)S(1)}, bf16[1024,1152]{1,0:T(8,128)(2,1)S(1)}, u32[]{:S(2)}, u32[]{:S(2)}) collective-permute-start(bf16[1024,1152]{1,0:T(8,128)(2,1)S(1)} %fusion), channel_id=1, source_target_pairs={{0,8},{2,10},{4,12},{6,14},{8,0},{10,2},{12,4},{14,6},{16,24},{18,... | collective-permute-start | bytes 7077896 | tf_op jit(solution)/shard_map/ppermute | solution.py:22
  130.2 14.3 %collective-permute-start.19 = (bf16[128,2048]{1,0:T(8,128)(2,1)S(1)}, bf16[128,2048]{1,0:T(8,128)(2,1)S(1)}, u32[]{:S(2)}, u32[]{:S(2)}) collective-permute-start(bf16[128,2048]{1,0:T(8,128)(2,1)S(1)} %pad_maximum_fusion.14), channel_id=1, source_target_pairs={{0,2},{2,0},{4,6},{6,4},{8,10},{10,8},{12,14},{14,12},{16,18},{18,... | collective-permute-start | bytes 1572872 | tf_op jit(solution)/shard_map/ppermute | solution.py:22
  131.8 13.7 %collective-permute-start.18 = (bf16[128,2048]{1,0:T(8,128)(2,1)S(1)}, bf16[128,2048]{1,0:T(8,128)(2,1)S(1)}, u32[]{:S(2)}, u32[]{:S(2)}) collective-permute-start(bf16[128,2048]{1,0:T(8,128)(2,1)S(1)} %pad_maximum_fusion.15), channel_id=1, source_target_pairs={{0,4},{2,6},{4,0},{6,2},{8,12},{10,14},{12,8},{14,10},{16,20},{18,... | collective-permute-start | bytes 1572872 | tf_op jit(solution)/shard_map/ppermute | solution.py:22
  145.6 9.3 %collective-permute-start.24 = (bf16[64,2048]{1,0:T(8,128)(2,1)S(1)}, bf16[64,2048]{1,0:T(8,128)(2,1)S(1)}, u32[]{:S(2)}, u32[]{:S(2)}) collective-permute-start(bf16[64,2048]{1,0:T(8,128)(2,1)S(1)} %get-tuple-element.100), channel_id=1, source_target_pairs={{0,2},{2,0},{4,6},{6,4},{8,10},{10,8},{12,14},{14,12},{16,18},{18,... | collective-permute-start | bytes 786440 | tf_op jit(solution)/shard_map/ppermute | solution.py:22
  146.2 9.2 %collective-permute-start.25 = (bf16[64,2048]{1,0:T(8,128)(2,1)S(1)}, bf16[64,2048]{1,0:T(8,128)(2,1)S(1)}, u32[]{:S(2)}, u32[]{:S(2)}) collective-permute-start(bf16[64,2048]{1,0:T(8,128)(2,1)S(1)} %get-tuple-element.101), channel_id=1, source_target_pairs={{0,4},{2,6},{4,0},{6,2},{8,12},{10,14},{12,8},{14,10},{16,20},{18,... | collective-permute-start | bytes 786440 | tf_op jit(solution)/shard_map/ppermute | solution.py:22
  147.6 16.5 %collective-permute-start.21 = (bf16[128,2048]{1,0:T(8,128)(2,1)S(1)}, bf16[128,2048]{1,0:T(8,128)(2,1)S(1)}, u32[]{:S(2)}, u32[]{:S(2)}) collective-permute-start(bf16[128,2048]{1,0:T(8,128)(2,1)S(1)} %pad_maximum_fusion.17), channel_id=1, source_target_pairs={{0,2},{2,0},{4,6},{6,4},{8,10},{10,8},{12,14},{14,12},{16,18},{18,... | collective-permute-start | bytes 1572872 | tf_op jit(solution)/shard_map/ppermute | solution.py:22
  149.2 15.2 %collective-permute-start.20 = (bf16[128,2048]{1,0:T(8,128)(2,1)S(1)}, bf16[128,2048]{1,0:T(8,128)(2,1)S(1)}, u32[]{:S(2)}, u32[]{:S(2)}) collective-permute-start(bf16[128,2048]{1,0:T(8,128)(2,1)S(1)} %pad_maximum_fusion.16), channel_id=1, source_target_pairs={{0,4},{2,6},{4,0},{6,2},{8,12},{10,14},{12,8},{14,10},{16,20},{18,... | collective-permute-start | bytes 1572872 | tf_op jit(solution)/shard_map/ppermute | solution.py:22
  155.7 27.1 %collective-permute-start.26 = (bf16[128,2048]{1,0:T(8,128)(2,1)S(1)}, bf16[128,2048]{1,0:T(8,128)(2,1)S(1)}, u32[]{:S(2)}, u32[]{:S(2)}) collective-permute-start(bf16[128,2048]{1,0:T(8,128)(2,1)S(1)} %add_convert_fusion.5), channel_id=1, source_target_pairs={{0,16},{2,18},{4,20},{6,22},{8,24},{10,26},{12,28},{14,30},{16,0},... | collective-permute-start | bytes 1572872 | tf_op jit(solution)/shard_map/ppermute | solution.py:22
  160.6 23.5 %collective-permute-start.28 = (bf16[1024,1152]{1,0:T(8,128)(2,1)S(1)}, bf16[1024,1152]{1,0:T(8,128)(2,1)S(1)}, u32[]{:S(2)}, u32[]{:S(2)}) collective-permute-start(bf16[1024,1152]{1,0:T(8,128)(2,1)S(1)} %pad_maximum_fusion.2), channel_id=1, source_target_pairs={{0,1},{1,0},{2,3},{3,2},{4,5},{5,4},{6,7},{7,6},{8,9},{9,8},{10,11... | collective-permute-start | bytes 7077896 | tf_op jit(solution)/shard_map/ppermute | solution.py:20
  164.5 18.3 %collective-permute-start.22 = (bf16[64,2048]{1,0:T(8,128)(2,1)S(1)}, bf16[64,2048]{1,0:T(8,128)(2,1)S(1)}, u32[]{:S(2)}, u32[]{:S(2)}) collective-permute-start(bf16[64,2048]{1,0:T(8,128)(2,1)S(1)} %get-tuple-element.94), channel_id=1, source_target_pairs={{0,2},{2,0},{4,6},{6,4},{8,10},{10,8},{12,14},{14,12},{16,18},{18,... | collective-permute-start | bytes 786440 | tf_op jit(solution)/shard_map/ppermute | solution.py:22
  166.1 16.8 %collective-permute-start.23 = (bf16[64,2048]{1,0:T(8,128)(2,1)S(1)}, bf16[64,2048]{1,0:T(8,128)(2,1)S(1)}, u32[]{:S(2)}, u32[]{:S(2)}) collective-permute-start(bf16[64,2048]{1,0:T(8,128)(2,1)S(1)} %get-tuple-element.95), channel_id=1, source_target_pairs={{0,4},{2,6},{4,0},{6,2},{8,12},{10,14},{12,8},{14,10},{16,20},{18,... | collective-permute-start | bytes 786440 | tf_op jit(solution)/shard_map/ppermute | solution.py:22
